TPU v7x, 32 devices: a whole 2x2x4 slice. The times are simulated.
32 devices in a mesh: seq: 16 (over z, x, core), ch: 2 (over y).
Axes of the slice: x: 2, y: 2, z: 4, core: 2. Of those that a mesh axis runs over, the one named last changes fastest.
Arguments:
- hidden: bfloat16 [2048, 2048], P('seq', 'ch'), may hold values from -400 to 400, as said below
- tokens: int32 [2048], replicated, may hold values from 0 to 3
- edit_bounds: int32 [8, 2], replicated, may hold values from 0 to 2047
- norm_gain: float32 [2048], replicated, may hold values from 0.1 to 1.9
- base_embed: float32 [4, 2048], replicated, may hold values from -6 to 6
- w_in: bfloat16 [2, 2048, 4096], P(None, None, 'ch'), may hold values from -0.125 to 0.125
- conv_w: float32 [4, 4096], P(None, 'ch'), may hold values from -3 to 3
- conv_b: float32 [4096], P('ch'), may hold values from -3 to 3
- proj_bc: bfloat16 [32, 4096], P(None, 'ch'), may hold values from -0.1875 to 0.1875
- decay_rate: float32 [16, 4096], P(None, 'ch'), may hold values from 1.953125e-05 to 0.11, as said below
- skip_gain: float32 [4096], P('ch'), may hold values from -4 to 4
- w_out: bfloat16 [4096, 2048], P('ch'), may hold values from -0.09375 to 0.09375
Outputs:
- mixed: bfloat16 [2048, 2048], P('seq', 'ch')
Inputs may be any that keep to these rules, and one draw needn't show every extreme that they name: The hidden states have row and column scales that differ. `decay_rate`: each entry is a positive decay rate per position. `edit_bounds`: positions in the window; a span's start and end come in no fixed order and may coincide with others.
All inputs are finite; a program needn't handle non-finite values.
Results may differ from a plain program's by a relative error of at most 0.014.
Values may be sent and summed in bfloat16 or wider, within the bound.
No kernel may reach another device: no remote copies, remote signals or barrier semaphores. Data moves between devices by JAX's collectives and lax.ppermute only.
A program may use at most 128 MiB of HBM per device.

v0:
```python
import jax
import jax.numpy as jnp
from jax import lax
from jax.sharding import PartitionSpec as P

CONV = 4


epsilon = 1e-05


def from_partner(block, axis, apart):
    count = lax.axis_size(axis)
    route = []
    for low in range(count):
        high = low | 1 << apart
        if high != low and high < count:
            route += [(low, high), (high, low)]
    return lax.ppermute(block, axis, route)


def passed_along(block, axis, distance):
    devices = range(lax.axis_size(axis))
    route = [(i - distance, i) for i in devices if i - distance in devices]
    return lax.ppermute(block, axis, route)


def carried_in(part, axis, combine, identity):
    place = lax.axis_index(axis)
    gathered = jax.tree.map(lambda a: lax.all_gather(a, axis), part)
    state = jax.tree.map(lambda a, e: jnp.zeros_like(a) + jnp.asarray(e, a.dtype), part, identity)

    def one(step, state):
        return combine(
            state, jax.tree.map(lambda a: lax.dynamic_index_in_dim(a, step, 0, False), gathered)
        )

    return lax.fori_loop(0, place, one, state)


def link(before, follow):
    return (before[0] * follow[0], before[1] * follow[0] + follow[1])


def link_pair(before, follow):
    return link(before[0:2], follow[0:2]) + link(before[2:4], follow[2:4])


def keep_rows(places, edit_bounds):
    hit_count = jnp.sum(
        (places[:, None] == edit_bounds.reshape(-1)[None, :]).astype(jnp.float32), axis=1
    )
    return 1.0 / (1.0 + hit_count)


def norm_rows(rows, bases, norm_gain, base_embed):
    row_values = rows.astype(jnp.float32)
    inv_rms = lax.rsqrt(jnp.mean(row_values * row_values, axis=1, keepdims=True) + epsilon)
    one_hot = (bases[:, None] == jnp.arange(4, dtype=jnp.int32)[None, :]).astype(jnp.float32)
    embedded = one_hot[:, 0:1] * base_embed[0][None, :]
    for base_index in range(1, 4):
        embedded = (
            embedded + one_hot[:, base_index : base_index + 1] * base_embed[base_index][None, :]
        )
    return (row_values * inv_rms * norm_gain[None, :] + embedded).astype(jnp.bfloat16)


def run_chain(
    start_state, keep_both, inputs_b, inputs_r, mixed_both, decay_mult, drive_gain, want_rows
):
    row_count = mixed_both.shape[1]
    inner_width = mixed_both.shape[2]
    state_size = inputs_b.shape[1]
    turns = 8
    per_turn = row_count // turns
    keep_blocks = keep_both.T.reshape(turns, per_turn, 2)
    b_blocks = inputs_b.transpose(2, 0, 1).reshape(turns, per_turn, 2, state_size)
    r_blocks = inputs_r.transpose(2, 0, 1).reshape(turns, per_turn, 2, state_size)
    x_blocks = mixed_both.transpose(1, 0, 2).reshape(turns, per_turn, 2, inner_width)

    def turn_step(state, block):
        keep_block, b_block, r_block, x_block = block
        outputs = []
        for row_index in range(per_turn):
            x_float = x_block[row_index].astype(jnp.float32)
            state = (
                keep_block[row_index][:, None, None] * decay_mult[None] * state
                + drive_gain[None] * b_block[row_index][:, :, None] * x_float[:, None, :]
            )
            if want_rows:
                outputs.append(jnp.sum(r_block[row_index][:, :, None] * state, axis=1))
        if want_rows:
            return (state, jnp.stack(outputs))
        return (state, jnp.zeros((), jnp.float32))

    final_state, produced = lax.scan(
        turn_step, start_state, (keep_blocks, b_blocks, r_blocks, x_blocks)
    )
    if want_rows:
        return (final_state, produced.reshape(row_count, 2, inner_width).transpose(1, 0, 2))
    return (final_state, None)


def body(
    hidden,
    tokens,
    edit_bounds,
    norm_gain,
    base_embed,
    w_in,
    conv_w,
    conv_b,
    proj_bc,
    decay_rate,
    skip_gain,
    w_out,
):
    row_count = hidden.shape[0]
    seq_count = lax.axis_size("seq")
    where_am = lax.axis_index("seq")
    levels = seq_count.bit_length() - 1
    own_bases = lax.dynamic_slice_in_dim(tokens, where_am * row_count, row_count)
    partner_shard = hidden
    for bit_index in range(levels):
        partner_shard = from_partner(partner_shard, "seq", bit_index)
    owner_dev = seq_count - 1 - where_am
    to_gather = jnp.stack([hidden, partner_shard])
    gathered = lax.all_gather(to_gather, "ch", axis=2, tiled=True)
    normed = norm_rows(gathered[0], own_bases, norm_gain, base_embed)
    far_bases = lax.dynamic_slice_in_dim(tokens, owner_dev * row_count, row_count)
    partner = norm_rows(gathered[1], far_bases, norm_gain, base_embed)
    offsets = jnp.arange(row_count, dtype=jnp.int32)
    keep_ahead = keep_rows(where_am * row_count + offsets, edit_bounds)
    back_rows = partner[::-1, ::-1]
    keep_back = keep_rows(owner_dev * row_count + row_count - 1 - offsets, edit_bounds)
    stacked = jnp.concatenate([normed, back_rows], axis=0)
    both_proj = lax.dot_general(
        stacked, w_in, (((1,), (1,)), ((), ())), preferred_element_type=jnp.float32
    ).astype(jnp.bfloat16)
    x_part = both_proj[:, 0, :].reshape(2, row_count, -1)
    z_part = both_proj[:, 1, :].reshape(2, row_count, -1)
    rims = x_part[:, row_count - CONV + 1 :, :]
    rims_in = passed_along(rims, "seq", 1)
    padded = jnp.concatenate([rims_in, x_part], axis=1)
    conv_sum = conv_b[None, None, :] + jnp.zeros(x_part.shape, jnp.float32)
    for tap_index in range(CONV):
        conv_sum = (
            conv_sum
            + padded[:, tap_index : tap_index + row_count, :].astype(jnp.float32)
            * conv_w[tap_index][None, None, :]
        )
    mixed_in = jax.nn.silu(conv_sum).astype(jnp.bfloat16)
    partial_bc = jnp.einsum("kc,slc->skl", proj_bc, mixed_in, preferred_element_type=jnp.float32)
    inputs_bc = lax.psum(partial_bc, "ch")
    state_size = decay_rate.shape[0]
    inputs_b = inputs_bc[:, :state_size]
    inputs_r = inputs_bc[:, state_size:]
    decay_mult = jnp.exp(-decay_rate)
    drive_gain = jnp.sqrt(-jnp.expm1(-2.0 * decay_rate))
    keep_both = jnp.stack([keep_ahead, keep_back])
    zero_state = jnp.zeros((2,) + decay_rate.shape, jnp.float32)
    local_end, unused = run_chain(
        zero_state, keep_both, inputs_b, inputs_r, mixed_in, decay_mult, drive_gain, False
    )
    block_decay = jnp.exp(-float(row_count) * decay_rate)
    pass_ahead = jnp.prod(keep_ahead) * block_decay
    pass_back = jnp.prod(keep_back) * block_decay
    identity_pair = (jnp.ones_like(decay_mult), jnp.zeros_like(decay_mult))
    carried = carried_in(
        (pass_ahead, local_end[0], pass_back, local_end[1]),
        "seq",
        link_pair,
        identity_pair + identity_pair,
    )
    carry_fore = carried[1]
    carry_aft = carried[3]
    entering = jnp.stack([carry_fore, carry_aft])
    final_unused, read_rows = run_chain(
        entering, keep_both, inputs_b, inputs_r, mixed_in, decay_mult, drive_gain, True
    )
    y_out = read_rows + skip_gain[None, None, :] * mixed_in.astype(jnp.float32)
    gated = (y_out * jax.nn.silu(z_part.astype(jnp.float32))).astype(jnp.bfloat16)
    gated_ahead = gated[0]
    gated_back = gated[1]
    for bit_index in range(levels):
        gated_back = from_partner(gated_back, "seq", bit_index)
    aligned = gated_back[::-1]
    summed = (
        jnp.dot(gated_ahead, w_out, preferred_element_type=jnp.float32)
        + jnp.dot(aligned, w_out, preferred_element_type=jnp.float32)[:, ::-1]
    )
    return lax.psum_scatter(summed.astype(jnp.bfloat16), "ch", scatter_dimension=1, tiled=True)


def solution(mesh):
    placed = (
        P("seq", "ch"),
        P(),
        P(),
        P(),
        P(),
        P(None, None, "ch"),
        P(None, "ch"),
        P("ch"),
        P(None, "ch"),
        P(None, "ch"),
        P("ch"),
        P("ch", None),
    )
    return jax.shard_map(
        body, mesh=mesh, in_specs=placed, out_specs=P("seq", "ch"), check_vma=False
    )
```

profile of v0, /device:TPU:0, one launch (start us, length us, event | category | flops | bytes accessed | tf_op | source)
XLA Modules:
  0.0 372.6 jit_solution(4190376621125632962)
XLA Ops:
  8.5 2.9 collective-permute-start.1
  11.3 6.6 %collective-permute-done.1 = bf16[128,1024]{1,0:T(8,128)(2,1)S(1)} collective-permute-done((bf16[128,1024]{1,0:T(8,128)(2,1)S(1)}, bf16[128,1024]{1,0:T(8,128)(2,1)S(1)}, u32[]{:S(2)}, u32[]{:S(2)}) %collective-permute-start.1) | collective-permute-done | bytes 262176 | tf_op jit(solution)/shard_map/ppermute | solution.py:19
  17.9 1.8 collective-permute-start.2
  19.8 6.0 %collective-permute-done.2 = bf16[128,1024]{1,0:T(8,128)(2,1)S(1)} collective-permute-done((bf16[128,1024]{1,0:T(8,128)(2,1)S(1)}, bf16[128,1024]{1,0:T(8,128)(2,1)S(1)}, u32[]{:S(2)}, u32[]{:S(2)}) %collective-permute-start.2) | collective-permute-done | bytes 262176 | tf_op jit(solution)/shard_map/ppermute | solution.py:19
  25.8 2.5 collective-permute-start.3
  28.3 10.9 %collective-permute-done.3 = bf16[128,1024]{1,0:T(8,128)(2,1)S(1)} collective-permute-done((bf16[128,1024]{1,0:T(8,128)(2,1)S(1)}, bf16[128,1024]{1,0:T(8,128)(2,1)S(1)}, u32[]{:S(2)}, u32[]{:S(2)}) %collective-permute-start.3) | collective-permute-done | bytes 262176 | tf_op jit(solution)/shard_map/ppermute | solution.py:19
  39.2 1.8 pad_maximum_fusion.1
  42.8 3.0 fusion.187
  47.5 15.8 %all-gather.8.cloned.1.call-done = bf16[2,128,2048]{2,1,0:T(8,128)(2,1)} async-done(((bf16[2,128,1024]{2,1,0:T(8,128)(2,1)}), bf16[2,128,2048]{2,1,0:T(8,128)(2,1)}) %all-gather.8.cloned.1.call-update) | async-done | bytes 1048592 | tf_op jit(solution)/shard_map/all_gather | solution.py:128
  64.8 2.2 fusion.176
  67.0 1.8 rev.9
  68.8 8.6 %convolution_convert_fusion = bf16[256,2,2048]{2,0,1:T(8,128)(2,1)S(1)} fusion(bf16[2,2048,2048]{2,1,0:T(8,128)(2,1)} %param.23, bf16[128,2048]{1,0:T(8,128)(2,1)S(1)} %rev.9, bf16[128,2048]{1,0:T(8,128)(2,1)S(1)} %get-tuple-element.481), kind=kOutput, calls=%fused_computation.335 | convolution fusion | flops 4298113024 | bytes 19922944 | tf_op jit(solution)/shard_map/dot_general | solution.py:137
  78.6 1.7 collective-permute-start.4
  81.1 1.5 multiply_convert_fusion
  84.2 7.2 %psum.7 = f32[2,32,128]{2,1,0:T(8,128)S(1)} all-reduce(f32[2,32,128]{2,1,0:T(8,128)S(1)} %convolution_bitcast_fusion), channel_id=1, replica_groups=mesh['seq'=16,'ch'=2] {'ch'}, use_global_device_ids=true, to_apply=%region_5.6 | all-reduce | flops 8192 | bytes 65536 | tf_op jit(solution)/shard_map/psum | solution.py:154
  91.6 11.1 %while.41 = (s32[]{:T(128)}, f32[2,16,2048]{2,1,0:T(8,128)S(1)}, f32[8,16,2]{2,1,0:T(8,128)S(1)}, f32[16,2048]{1,0:T(8,128)S(1)}, f32[16,2048]{1,0:T(8,128)S(1)}...) while((s32[]{:T(128)}, f32[2,16,2048]{2,1,0:T(8,128)S(1)}, ...), condition=%wide.region_7.8_spmd.clone, body=%wide.region_6.7_spmd.clone.sunk | while | flops 5373970 | bytes 1448915 | solution.py:96
  104.2 2.7 all-gather.16.cloned.1.call-done
  106.9 42.4 %all-gather.14.cloned.1.call-done = f32[256,2048]{1,0:T(8,128)} async-done(((f32[16,2048]{1,0:T(8,128)}), f32[256,2048]{1,0:T(8,128)}) %all-gather.14.cloned.1.call-update) | async-done | bytes 2097168 | tf_op jit(solution)/shard_map/all_gather | solution.py:30
  149.3 42.2 %all-gather.10.cloned.1.call-done = f32[16,16,2048]{2,1,0:T(8,128)} async-done(((f32[1,16,2048]{2,1,0:T(8,128)}), f32[16,16,2048]{2,1,0:T(8,128)}) %all-gather.10.cloned.1.call-update) | async-done | bytes 2097168 | tf_op jit(solution)/shard_map/all_gather | solution.py:30
  191.5 42.2 %all-gather.12.cloned.1.call-done = f32[16,16,2048]{2,1,0:T(8,128)} async-done(((f32[1,16,2048]{2,1,0:T(8,128)}), f32[16,16,2048]{2,1,0:T(8,128)}) %all-gather.12.cloned.1.call-update) | async-done | bytes 2097168 | tf_op jit(solution)/shard_map/all_gather | solution.py:30
  234.0 34.4 %while.40 = (s32[]{:T(128)}, f32[2,16,2048]{2,1,0:T(8,128)S(1)}, f32[8,16,2,2048]{3,2,1,0:T(2,128)}, f32[8,16,2]{2,1,0:T(8,128)S(1)}, f32[16,2048]{1,0:T(8,128)S...) while((s32[]{:T(128)}, f32[2,16,2048]{2,1,0:T(8,128)S(1)}, ...), condition=%wide.region_28.29_spmd, body=%wide.region_11.28_spmd.sunk | while | flops 11272209 | bytes 5848121 | solution.py:96
  268.4 3.4 fusion.172
  271.9 1.6 collective-permute-start.5
  275.0 3.1 collective-permute-start.6
  278.0 12.4 %collective-permute-done.6 = bf16[128,2048]{1,0:T(8,128)(2,1)S(1)} collective-permute-done((bf16[128,2048]{1,0:T(8,128)(2,1)S(1)}, bf16[128,2048]{1,0:T(8,128)(2,1)S(1)}, u32[]{:S(2)}, u32[]{:S(2)}) %collective-permute-start.6) | collective-permute-done | bytes 524320 | tf_op jit(solution)/shard_map/ppermute | solution.py:19
  290.5 5.5 %collective-permute-start.7 = (bf16[128,2048]{1,0:T(8,128)(2,1)S(1)}, bf16[128,2048]{1,0:T(8,128)(2,1)S(1)}, u32[]{:S(2)}, u32[]{:S(2)}) collective-permute-start(bf16[128,2048]{1,0:T(8,128)(2,1)S(1)} %collective-permute-done.6), channel_id=1, source_target_pairs={{0,8},{8,0},{2,10},{10,2},{4,12},{12,4},{6,14},{14,6},{16,24},{24,... | collective-permute-start | bytes 1572872 | tf_op jit(solution)/shard_map/ppermute | solution.py:19
  296.0 11.9 %collective-permute-done.7 = bf16[128,2048]{1,0:T(8,128)(2,1)S(1)} collective-permute-done((bf16[128,2048]{1,0:T(8,128)(2,1)S(1)}, bf16[128,2048]{1,0:T(8,128)(2,1)S(1)}, u32[]{:S(2)}, u32[]{:S(2)}) %collective-permute-start.7) | collective-permute-done | bytes 524320 | tf_op jit(solution)/shard_map/ppermute | solution.py:19
  307.9 12.1 %collective-permute-start.8 = (bf16[128,2048]{1,0:T(8,128)(2,1)S(1)}, bf16[128,2048]{1,0:T(8,128)(2,1)S(1)}, u32[]{:S(2)}, u32[]{:S(2)}) collective-permute-start(bf16[128,2048]{1,0:T(8,128)(2,1)S(1)} %collective-permute-done.7), channel_id=1, source_target_pairs={{0,16},{16,0},{2,18},{18,2},{4,20},{20,4},{6,22},{22,6},{8,24},{24... | collective-permute-start | bytes 1572872 | tf_op jit(solution)/shard_map/ppermute | solution.py:19
  319.9 4.7 %fusion.185 = f32[128,2048]{1,0:T(8,128)S(1)} fusion(bf16[2048,2048]{1,0:T(8,128)(2,1)} %param.29, bf16[2,128,2048]{2,1,0:T(8,128)(2,1)S(1)} %fusion.172), kind=kOutput, calls=%fused_computation.369 | convolution fusion | flops 1073741824 | bytes 9961472 | tf_op jit(solution)/shard_map/dot_general | solution.py:189
  324.6 17.9 %collective-permute-done.8 = bf16[128,2048]{1,0:T(8,128)(2,1)S(1)} collective-permute-done((bf16[128,2048]{1,0:T(8,128)(2,1)S(1)}, bf16[128,2048]{1,0:T(8,128)(2,1)S(1)}, u32[]{:S(2)}, u32[]{:S(2)}) %collective-permute-start.8) | collective-permute-done | bytes 524320 | tf_op jit(solution)/shard_map/ppermute | solution.py:19
  343.1 4.6 %fusion.199 = f32[128,2048]{1,0:T(8,128)S(1)} fusion(bf16[128,2048]{1,0:T(8,128)(2,1)S(1)} %rev.10, bf16[2048,2048]{1,0:T(8,128)(2,1)} %param.29), kind=kOutput, calls=%fused_computation.411 | convolution fusion | flops 1073741824 | bytes 9961472 | tf_op jit(solution)/shard_map/dot_general | solution.py:190
  350.2 15.6 %reduce-scatter.2.cloned.1.call-done = bf16[128,1024]{1,0:T(8,128)(2,1)} async-done(((bf16[128,2048]{1,0:T(8,128)(2,1)}), bf16[128,1024]{1,0:T(8,128)(2,1)}) %reduce-scatter.2.cloned.1.call-update) | async-done | bytes 262160 | tf_op jit(solution)/shard_map/reduce_scatter | solution.py:192
  (294 shorter events, 61.0 us)
Async XLA Ops:
  6.5 77.2 %copy-start = (bf16[32,2048]{1,0:T(8,128)(2,1)S(1)}, bf16[32,2048]{1,0:T(8,128)(2,1)}, u32[]{:S(2)}) copy-start(bf16[32,2048]{1,0:T(8,128)(2,1)} %param.26) | copy-start | bytes 393220
  6.5 40.9 %copy-start.1 = (f32[4,2048]{1,0:T(4,128)S(1)}, f32[4,2048]{1,0:T(4,128)}, u32[]{:S(2)}) copy-start(f32[4,2048]{1,0:T(4,128)} %param.22) | copy-start | bytes 98308
  6.5 40.9 %copy-start.2 = (f32[4,2048]{1,0:T(4,128)S(1)}, f32[4,2048]{1,0:T(4,128)}, u32[]{:S(2)}) copy-start(f32[4,2048]{1,0:T(4,128)} %param.24) | copy-start | bytes 98308
  6.5 58.3 %copy-start.3 = (f32[2048]{0:T(1024)S(1)}, f32[2048]{0:T(1024)}, u32[]{:S(2)}) copy-start(f32[2048]{0:T(1024)} %param.21) | copy-start | bytes 24580
  6.5 56.8 %all-gather.8.cloned.1.call-start = ((), (), s32[]{:S(2)}) async-start(), calls=%async_computation.1 | async-start | bytes 1572864 | tf_op jit(solution)/shard_map/all_gather | solution.py:128
  6.6 1.9 collective-permute-start
  8.5 9.5 %collective-permute-start.1 = (bf16[128,1024]{1,0:T(8,128)(2,1)S(1)}, bf16[128,1024]{1,0:T(8,128)(2,1)S(1)}, u32[]{:S(2)}, u32[]{:S(2)}) collective-permute-start(bf16[128,1024]{1,0:T(8,128)(2,1)S(1)} %collective-permute-done), channel_id=1, source_target_pairs={{0,4},{4,0},{2,6},{6,2},{8,12},{12,8},{10,14},{14,10},{16,20},{20,... | collective-permute-start | bytes 786440 | tf_op jit(solution)/shard_map/ppermute | solution.py:19
  17.9 7.8 %collective-permute-start.2 = (bf16[128,1024]{1,0:T(8,128)(2,1)S(1)}, bf16[128,1024]{1,0:T(8,128)(2,1)S(1)}, u32[]{:S(2)}, u32[]{:S(2)}) collective-permute-start(bf16[128,1024]{1,0:T(8,128)(2,1)S(1)} %collective-permute-done.1), channel_id=1, source_target_pairs={{0,8},{8,0},{2,10},{10,2},{4,12},{12,4},{6,14},{14,6},{16,24},{24,... | collective-permute-start | bytes 786440 | tf_op jit(solution)/shard_map/ppermute | solution.py:19
  25.8 13.5 %collective-permute-start.3 = (bf16[128,1024]{1,0:T(8,128)(2,1)S(1)}, bf16[128,1024]{1,0:T(8,128)(2,1)S(1)}, u32[]{:S(2)}, u32[]{:S(2)}) collective-permute-start(bf16[128,1024]{1,0:T(8,128)(2,1)S(1)} %collective-permute-done.2), channel_id=1, source_target_pairs={{0,16},{16,0},{2,18},{18,2},{4,20},{20,4},{6,22},{22,6},{8,24},{24... | collective-permute-start | bytes 786440 | tf_op jit(solution)/shard_map/ppermute | solution.py:19
  41.1 65.9 %all-gather.16.cloned.1.call-start = ((), (), s32[]{:S(2)}) async-start(), calls=%async_computation.6 | async-start | bytes 2228224 | tf_op jit(solution)/shard_map/all_gather | solution.py:30
  45.8 103.5 %all-gather.14.cloned.1.call-start = ((), (), s32[]{:S(2)}) async-start(), calls=%async_computation.5 | async-start | bytes 2228224 | tf_op jit(solution)/shard_map/all_gather | solution.py:30
  46.6 145.0 %all-gather.10.cloned.1.call-start = ((), (), s32[]{:S(2)}) async-start(), calls=%async_computation.2 | async-start | bytes 2228224 | tf_op jit(solution)/shard_map/all_gather | solution.py:30
  77.4 3.8 %copy-start.4 = (f32[2048]{0:T(1024)S(1)}, f32[2048]{0:T(1024)}, u32[]{:S(2)}) copy-start(f32[2048]{0:T(1024)} %param.25) | copy-start | bytes 24580
  78.6 2.5 collective-permute-start.4
  103.5 130.3 %all-gather.12.cloned.1.call-start = ((), (), s32[]{:S(2)}) async-start(), calls=%async_computation.3 | async-start | bytes 2228224 | tf_op jit(solution)/shard_map/all_gather | solution.py:30
  104.1 261.7 %reduce-scatter.2.cloned.1.call-start = ((), (), s32[]{:S(2)}) async-start(), calls=%async_computation.4 | async-start | bytes 786432 | tf_op jit(solution)/shard_map/reduce_scatter | solution.py:192
  234.0 34.4 %copy-start.5 = (f32[2048]{0:T(1024)S(1)}, f32[2048]{0:T(1024)}, u32[]{:S(2)}) copy-start(f32[2048]{0:T(1024)} %param.28) | copy-start | bytes 24580
  271.9 3.1 collective-permute-start.5
  275.0 15.5 %collective-permute-start.6 = (bf16[128,2048]{1,0:T(8,128)(2,1)S(1)}, bf16[128,2048]{1,0:T(8,128)(2,1)S(1)}, u32[]{:S(2)}, u32[]{:S(2)}) collective-permute-start(bf16[128,2048]{1,0:T(8,128)(2,1)S(1)} %collective-permute-done.5), channel_id=1, source_target_pairs={{0,4},{4,0},{2,6},{6,2},{8,12},{12,8},{10,14},{14,10},{16,20},{20,... | collective-permute-start | bytes 1572872 | tf_op jit(solution)/shard_map/ppermute | solution.py:19
  290.5 17.4 %collective-permute-start.7 = (bf16[128,2048]{1,0:T(8,128)(2,1)S(1)}, bf16[128,2048]{1,0:T(8,128)(2,1)S(1)}, u32[]{:S(2)}, u32[]{:S(2)}) collective-permute-start(bf16[128,2048]{1,0:T(8,128)(2,1)S(1)} %collective-permute-done.6), channel_id=1, source_target_pairs={{0,8},{8,0},{2,10},{10,2},{4,12},{12,4},{6,14},{14,6},{16,24},{24,... | collective-permute-start | bytes 1572872 | tf_op jit(solution)/shard_map/ppermute | solution.py:19
  307.9 34.6 %collective-permute-start.8 = (bf16[128,2048]{1,0:T(8,128)(2,1)S(1)}, bf16[128,2048]{1,0:T(8,128)(2,1)S(1)}, u32[]{:S(2)}, u32[]{:S(2)}) collective-permute-start(bf16[128,2048]{1,0:T(8,128)(2,1)S(1)} %collective-permute-done.7), channel_id=1, source_target_pairs={{0,16},{16,0},{2,18},{18,2},{4,20},{20,4},{6,22},{22,6},{8,24},{24... | collective-permute-start | bytes 1572872 | tf_op jit(solution)/shard_map/ppermute | solution.py:19
Sparse Core Ops, SparseCore 0:
  41.2 22.0 all-gather.7
  65.5 41.4 all-gather.15
  109.1 40.1 all-gather.13
  151.3 40.1 all-gather.9
  193.5 40.1 all-gather.11
  350.3 15.3 reduce-scatter.1
where the time goes:
time: 373 us
  waiting for transfers between devices  232 us (62%)
  other arithmetic  50 us (13%)
  starting transfers between devices  31.8 us (9%)
  local copies, waits for them, and re-layouts  18.5 us (5%)
  matrix products  18.3 us (5%)
  between operations  13.7 us (4%)
  blocking collectives  7.25 us (2%)
    all_gather x4, waiting for transfers between devices, carried_in(): gathered = jax.tree.map(lambda a: lax.all_gather(a, axis), part)  130 us
    ppermute x8, waiting for transfers between devices, from_partner(): return lax.ppermute(block, axis, route)  68.7 us
    ppermute x8, starting transfers between devices, from_partner(): return lax.ppermute(block, axis, route)  29.9 us
    reduce_sum x40, other arithmetic, turn_step(): outputs.append(jnp.sum(r_block[row_index][:, :, None] * state, axis=1))  24.1 us
    all_gather x1, waiting for transfers between devices, body(): gathered = lax.all_gather(to_gather, 'ch', axis=2, tiled=True)  15.8 us
    reduce_scatter x1, waiting for transfers between devices, body(): lax.psum_scatter(summed.astype(jnp.bfloat16), 'ch', scatter_dimension=1,...  15.6 us
    dot_general x1, matrix products, body(): lax.dot_general(stacked, w_in, (((1,), (1,)), ((), ())), preferred_elemen...  8.57 us
    add x8, other arithmetic, turn_step(): keep_block[row_index][:, None, None] * decay_mult[None] * state  8 us
  transfers between devices with their start and end apart: 15, of which 15 were waited for; matrix products, arithmetic and copies ran while one was open for 11% of the time, Pallas kernels for 0%

commit v1 on v0

v1 whole, which is shorter than its diff:
```python
import functools

import jax
import jax.numpy as jnp
from jax import lax
from jax.experimental import pallas as pl
from jax.experimental.pallas import tpu as pltpu
from jax.sharding import PartitionSpec as P

CONV = 4
STATE = 16
EDGE = 16
LANES = 128
SUBS = 8
STREAMS = 2
VMEM_BYTES = 52 << 20
epsilon = 1e-05
f32 = jnp.float32
bf16 = jnp.bfloat16

WHOLE = pl.BlockSpec(memory_space=pltpu.VMEM)
SCALARS = pl.BlockSpec(memory_space=pltpu.SMEM)


def params():
    return pltpu.CompilerParams(vmem_limit_bytes=VMEM_BYTES)


def shaped(shape, dtype=f32):
    return jax.ShapeDtypeStruct(shape, dtype)


def swap(block, axis, apart):
    count = lax.axis_size(axis)
    return lax.ppermute(block, axis, [(i, i ^ apart) for i in range(count)])


def both_halves(block):
    if lax.axis_size("ch") == 2:
        return block, swap(block, "ch", 1), lax.axis_index("ch")
    full = lax.all_gather(block, "ch", axis=1, tiled=True)
    half = full.shape[1] // 2
    return full[:, :half], full[:, half:], jnp.int32(0)


def norm_kernel(flags, low, high, low_edge, high_edge, hot, gain, embed, out):
    rows = low.shape[0]
    half = low.shape[1]

    def one(first, second, first_row, count, scale):
        a = first[...].astype(f32)
        b = second[...].astype(f32)
        total = jnp.sum(a * a, axis=1, keepdims=True) + jnp.sum(b * b, axis=1, keepdims=True)
        inv_rms = lax.rsqrt(total / (2 * half) + epsilon)
        for part, values in enumerate((a, b)):
            cols = slice(part * half, (part + 1) * half)
            marks = hot[first_row : first_row + count, :]
            embedded = marks[:, 0:1] * embed[0:1, cols]
            for base in range(1, 4):
                embedded = embedded + marks[:, base : base + 1] * embed[base : base + 1, cols]
            normed = values * inv_rms * gain[0:1, cols] + embedded
            if scale is not None:
                normed = normed * scale
            out[first_row : first_row + count, cols] = normed.astype(bf16)

    valid = flags[1].astype(f32)

    @pl.when(flags[0] == 0)
    def _():
        one(low, high, 0, rows, None)
        one(low_edge, high_edge, rows, EDGE, valid)

    @pl.when(flags[0] != 0)
    def _():
        one(high, low, 0, rows, None)
        one(high_edge, low_edge, rows, EDGE, valid)


def signal_kernel(
    flags, own, other, w, conv_w, conv_b, proj, rows_out, c_out, bc_out, x_tiles, proj_rows, acc
):
    step = pl.program_id(0)
    rows = own.shape[0] - EDGE
    length = 2 * rows
    width = own.shape[1]
    padded = length + EDGE
    block = w.shape[2]
    tiles = block // LANES

    @pl.when(step == 0)
    def _():
        def place(first, second):
            rows_out[0:EDGE, :] = first[rows:, :]
            rows_out[EDGE : EDGE + rows, :] = first[:rows, :]
            rows_out[EDGE + rows : padded, :] = second[:rows, :]
            r = lax.broadcasted_iota(jnp.int32, (LANES, LANES), 0)
            q = lax.broadcasted_iota(jnp.int32, (LANES, LANES), 1)
            turn = jnp.where(r + q == LANES - 1, 1.0, 0.0).astype(bf16)
            for t in range(width // LANES):
                to = slice(t * LANES, (t + 1) * LANES)
                at = slice(width - (t + 1) * LANES, width - t * LANES)
                for base, piece in (
                    (0, first[:rows, at]),
                    (rows, second[:, at]),
                ):
                    turned = jnp.dot(piece, turn, preferred_element_type=f32)
                    rows_out[padded + base : padded + base + piece.shape[0], to] = turned.astype(
                        bf16
                    )

        @pl.when(flags[0] == 0)
        def _():
            place(own, other)

        @pl.when(flags[0] != 0)
        def _():
            place(other, own)

        proj_rows[...] = jnp.zeros(proj_rows.shape, bf16)
        acc[...] = jnp.zeros(acc.shape, f32)
        c_out[...] = jnp.zeros(c_out.shape, f32)

    x = jnp.dot(rows_out[...], w[0], preferred_element_type=f32).astype(bf16).astype(f32)
    for t in range(tiles):
        x_tiles[t] = x[:, t * LANES : (t + 1) * LANES]
    inner = 2 * STATE
    for s in range(STREAMS):
        mixed = []
        for t in range(tiles):
            cols = slice(t * LANES, (t + 1) * LANES)
            total = conv_b[0:1, cols]
            for k in range(CONV):
                at = EDGE - CONV + 1 + k if s == 0 else padded + CONV - 1 - k
                total = total + x_tiles[t, at : at + length, :] * conv_w[k : k + 1, cols]
            c = jax.nn.silu(total).astype(bf16)
            c_out[s, pl.ds(step * tiles + t, length, stride=SUBS), :] = c.astype(f32)
            mixed.append(c)
        mixed = mixed[0] if tiles == 1 else jnp.concatenate(mixed, axis=1)
        for half in range(2):
            i = 2 * half + s
            proj_rows[i, inner * i : inner * (i + 1), :] = proj[...]
            acc[...] += lax.dot_general(
                mixed[half * rows : (half + 1) * rows],
                proj_rows[i],
                (((1,), (1,)), ((), ())),
                preferred_element_type=f32,
            )

    @pl.when(step == pl.num_programs(0) - 1)
    def _():
        bc_out[...] = acc[...]


def gate_kernel(flags, rows_in, w, z_out):
    padded = rows_in.shape[0] // 2
    length = padded - EDGE
    z_out[0] = jnp.dot(rows_in[EDGE:padded, :], w[0], preferred_element_type=f32).astype(bf16)
    z_out[1] = jnp.dot(
        rows_in[padded : padded + length, :], w[0], preferred_element_type=f32
    ).astype(bf16)


def spread(bc, wide, slot, stream, first, rows):
    for n in range(STATE):
        for half in range(2):
            lane = 2 * STATE * (2 * half + stream) + first + n
            wide[slot + n, half * rows : (half + 1) * rows, :] = jnp.broadcast_to(
                bc[:, lane : lane + 1], (rows, LANES)
            )


def tile_at(ref, n):
    return ref[n * SUBS : (n + 1) * SUBS, :]


def end_kernel(bc_own, bc_far, weigh, c, decay, end_gain, bc_out, end_out, wide):
    rows = bc_own.shape[0]
    length = 2 * rows
    bc_out[...] = (bc_own[...] + bc_far[...]) * weigh[...]
    bc = bc_out[...]
    for s in range(STREAMS):
        spread(bc, wide, s * STATE, s, 0, rows)
    a = [tile_at(decay, n) for n in range(STATE)]

    def one(j, state):
        after = []
        for s in range(STREAMS):
            t = j if s == 0 else length - 1 - j
            x = c[s, pl.ds(pl.multiple_of(t * SUBS, SUBS), SUBS), :]
            for n in range(STATE):
                b = wide[s * STATE + n, pl.ds(t, 1), :]
                after.append(a[n] * state[s * STATE + n] + b * x)
        return tuple(after)

    zero = jnp.zeros((SUBS, LANES), f32)
    state = lax.fori_loop(0, length, one, (zero,) * (STREAMS * STATE), unroll=8)
    for s in range(STREAMS):
        for n in range(STATE):
            end_out[s, n * SUBS : (n + 1) * SUBS, :] = state[s * STATE + n] * tile_at(end_gain, n)


def local_kernel(stream, bc_in, c, decay, gain, skip, y_out, wide):
    rows = bc_in.shape[0]
    length = 2 * rows
    bc = bc_in[...]
    spread(bc, wide, 0, stream, 0, rows)
    spread(bc, wide, STATE, stream, STATE, rows)
    a = [tile_at(decay, n) for n in range(STATE)]
    g = [tile_at(gain, n) for n in range(STATE)]
    direct = skip[...]

    def one(j, state):
        t = j if stream == 0 else length - 1 - j
        at = pl.ds(pl.multiple_of(t * SUBS, SUBS), SUBS)
        x = c[0, at, :]
        after = []
        sums = [direct * x, None]
        for n in range(STATE):
            h = a[n] * state[n] + wide[n, pl.ds(t, 1), :] * (g[n] * x)
            after.append(h)
            term = wide[STATE + n, pl.ds(t, 1), :] * h
            sums[n % 2] = term if sums[n % 2] is None else sums[n % 2] + term
        y_out[at, :] = sums[0] + sums[1]
        return tuple(after)

    zero = jnp.zeros((SUBS, LANES), f32)
    lax.fori_loop(0, length, one, (zero,) * STATE, unroll=8)


def finish_kernel(
    flags, bc_in, entering, decay, y_f, y_b, z, w_hbm, send, keep, w, sem, wide, y, gated
):
    rows = bc_in.shape[0]
    length = 2 * rows
    inner = z.shape[2]
    width = w.shape[1]
    fetch = pltpu.make_async_copy(
        w_hbm.at[pl.ds(pl.multiple_of(flags[0] * inner, inner), inner), :], w, sem
    )
    fetch.start()
    bc = bc_in[...]
    for s in range(STREAMS):
        spread(bc, wide, s * STATE, s, STATE, rows)
    a = [tile_at(decay, n) for n in range(STATE)]
    before = (y_f, y_b)

    def one(j, state):
        after = []
        for s in range(STREAMS):
            t = j if s == 0 else length - 1 - j
            at = pl.ds(pl.multiple_of(t * SUBS, SUBS), SUBS)
            sums = [before[s][at, :], None]
            for n in range(STATE):
                h = a[n] * state[s * STATE + n]
                after.append(h)
                term = wide[s * STATE + n, pl.ds(t, 1), :] * h
                sums[n % 2] = term if sums[n % 2] is None else sums[n % 2] + term
            y[s, at, :] = sums[0] + sums[1]
        return tuple(after)

    start = tuple(
        entering[s, n * SUBS : (n + 1) * SUBS, :] for s in range(STREAMS) for n in range(STATE)
    )
    lax.fori_loop(0, length, one, start, unroll=4)
    for s in range(STREAMS):
        for t in range(inner // LANES):
            cols = slice(t * LANES, (t + 1) * LANES)
            values = y[s, pl.ds(t, length, stride=SUBS), :]
            gated[s, :, cols] = (values * jax.nn.silu(z[s, :, cols].astype(f32))).astype(bf16)
    fetch.wait()
    back = LANES - 1 - lax.broadcasted_iota(jnp.int32, (rows, LANES), 1)
    strip = min(2 * LANES, width)

    def put(near, half):
        where = slice(half * rows, (half + 1) * rows)
        for first in range(0, width, strip):
            ahead = jnp.dot(
                gated[0, where, :], w[:, first : first + strip], preferred_element_type=f32
            )
            behind = jnp.dot(
                gated[1, where, :],
                w[:, width - first - strip : width - first],
                preferred_element_type=f32,
            )
            for t in range(strip // LANES):
                mirrored = behind[:, strip - (t + 1) * LANES : strip - t * LANES]
                total = ahead[:, t * LANES : (t + 1) * LANES] + jnp.take_along_axis(
                    mirrored, back, axis=1
                )
                near[:, first + t * LANES : first + (t + 1) * LANES] = total.astype(near.dtype)

    @pl.when(flags[0] == 0)
    def _():
        put(send, 1)
        put(keep, 0)

    @pl.when(flags[0] != 0)
    def _():
        put(send, 0)
        put(keep, 1)


def as_tiles(values, tiles):
    spaced = values.reshape(values.shape[0], tiles, LANES)
    if tiles < SUBS:
        spaced = jnp.pad(spaced, ((0, 0), (0, SUBS - tiles), (0, 0)))
    return spaced.reshape(values.shape[0] * SUBS, LANES)


def body(
    hidden,
    tokens,
    edit_bounds,
    norm_gain,
    base_embed,
    w_in,
    conv_w,
    conv_b,
    proj_bc,
    decay_rate,
    skip_gain,
    w_out,
):
    rows = hidden.shape[0]
    width = w_in.shape[1]
    local = w_in.shape[2]
    inner = local // 2
    tiles = inner // LANES
    length = 2 * rows
    padded = length + EDGE
    seq_count = lax.axis_size("seq")
    ch_count = lax.axis_size("ch")
    chips = seq_count // 2
    place = lax.axis_index("seq")
    core = place % 2
    chip = place // 2

    first, second, exchanged = both_halves(hidden)
    rim = lax.dynamic_slice_in_dim(hidden, core * (rows - EDGE), EDGE)
    pairs = [(i, i + 1) for i in range(1, seq_count - 1, 2)]
    rim = lax.ppermute(rim, "seq", pairs + [(j, i) for i, j in pairs])
    rim_first, rim_second, _ = both_halves(rim)
    own_bases = lax.dynamic_slice_in_dim(tokens, place * rows, rows)
    rim_at = jnp.where(core == 0, place * rows - EDGE, (place + 1) * rows)
    rim_bases = lax.dynamic_slice_in_dim(
        tokens, jnp.clip(rim_at, 0, seq_count * rows - EDGE), EDGE
    )
    bases = jnp.concatenate([own_bases, rim_bases])
    hot = (bases[:, None] == jnp.arange(4, dtype=jnp.int32)[None, :]).astype(f32)
    valid = jnp.where(core == 0, place > 0, place < seq_count - 1)
    normed = pl.pallas_call(
        norm_kernel,
        out_shape=shaped((rows + EDGE, width), bf16),
        in_specs=[SCALARS] + [WHOLE] * 7,
        out_specs=WHOLE,
        compiler_params=params(),
        name="norm",
    )(
        jnp.stack([exchanged, valid.astype(jnp.int32)]),
        first,
        second,
        rim_first,
        rim_second,
        hot,
        norm_gain[None, :],
        base_embed,
    )
    partner = swap(normed, "seq", 1)

    marks = edit_bounds.reshape(-1)
    places = jnp.arange(seq_count * rows, dtype=jnp.int32)
    weight = 1.0 + jnp.sum((places[:, None] == marks[None, :]).astype(f32), axis=1)
    chip_weight = jnp.prod(weight.reshape(chips, length), axis=1)
    own_weight = lax.dynamic_slice_in_dim(weight, chip * length, length)
    before = places[:length, None] >= places[None, :length]
    run_f = jnp.prod(jnp.where(before, own_weight[None, :], 1.0), axis=1)
    run_b = jnp.prod(jnp.where(before.T, own_weight[None, :], 1.0), axis=1)
    runs = jnp.stack([run_f, run_b]).reshape(2, 2, rows)
    pairs_bc = jnp.stack([runs, 1.0 / runs], axis=2)
    weigh = jnp.broadcast_to(
        pairs_bc.transpose(3, 1, 0, 2)[..., None], (rows, 2, STREAMS, 2, STATE)
    ).reshape(rows, 4 * 2 * STATE)

    rate = as_tiles(lax.dynamic_slice_in_dim(decay_rate, core * inner, inner, 1), tiles)
    decay = jnp.exp(-rate)
    gain = jnp.sqrt(-jnp.expm1(-2.0 * rate))
    skip = as_tiles(lax.dynamic_slice_in_dim(skip_gain, core * inner, inner)[None, :], tiles)
    own_keep = 1.0 / jnp.prod(own_weight)

    block = min(2 * LANES, inner)
    steps = inner // block
    whole = lambda shape: pl.BlockSpec(shape, lambda i, f: (0,) * len(shape))
    flags = core[None]
    stacked, c, bc = pl.pallas_call(
        signal_kernel,
        grid_spec=pltpu.PrefetchScalarGridSpec(
            num_scalar_prefetch=1,
            grid=(steps,),
            in_specs=[
                whole((rows + EDGE, width)),
                whole((rows + EDGE, width)),
                pl.BlockSpec((1, width, block), lambda i, f: (0, 0, f[0] * steps + i)),
                pl.BlockSpec((CONV, block), lambda i, f: (0, f[0] * steps + i)),
                pl.BlockSpec((1, block), lambda i, f: (0, f[0] * steps + i)),
                pl.BlockSpec((2 * STATE, block), lambda i, f: (0, f[0] * steps + i)),
            ],
            out_specs=[
                whole((2 * padded, width)),
                whole((STREAMS, length * SUBS, LANES)),
                whole((rows, LANES)),
            ],
            scratch_shapes=[
                pltpu.VMEM((block // LANES, 2 * padded, LANES), f32),
                pltpu.VMEM((4, LANES, block), bf16),
                pltpu.VMEM((rows, LANES), f32),
            ],
        ),
        out_shape=[
            shaped((2 * padded, width), bf16),
            shaped((STREAMS, length * SUBS, LANES)),
            shaped((rows, LANES)),
        ],
        compiler_params=params(),
        name="signal",
    )(flags, normed, partner, w_in, conv_w, conv_b[None, :], proj_bc)

    bc = bc + swap(bc, "seq", 1)
    if ch_count == 2:
        bc_far = swap(bc, "ch", 1)
    else:
        bc, bc_far = lax.psum(bc, "ch"), jnp.zeros_like(bc)

    z = pl.pallas_call(
        gate_kernel,
        grid_spec=pltpu.PrefetchScalarGridSpec(
            num_scalar_prefetch=1,
            grid=(steps,),
            in_specs=[
                whole((2 * padded, width)),
                pl.BlockSpec((1, width, block), lambda i, f: (1, 0, f[0] * steps + i)),
            ],
            out_specs=pl.BlockSpec((STREAMS, length, block), lambda i, f: (0, 0, i)),
        ),
        out_shape=shaped((STREAMS, length, inner), bf16),
        compiler_params=params(),
        name="gate",
    )(flags, stacked, w_in)

    scaled, ends = pl.pallas_call(
        end_kernel,
        out_shape=[shaped((rows, LANES)), shaped((STREAMS, STATE * SUBS, LANES))],
        in_specs=[WHOLE] * 6,
        out_specs=[WHOLE] * 2,
        scratch_shapes=[pltpu.VMEM((STREAMS * STATE, length, LANES), f32)],
        compiler_params=params(),
        name="ends",
    )(bc, bc_far, weigh, c, decay, gain * own_keep)

    local_y = []
    for s in range(STREAMS):
        local_y.append(
            pl.pallas_call(
                functools.partial(local_kernel, s),
                grid=(1,),
                out_shape=shaped((length * SUBS, LANES)),
                in_specs=[
                    pl.BlockSpec((rows, LANES), lambda i: (0, 0)),
                    pl.BlockSpec((1, length * SUBS, LANES), lambda i, s=s: (s, 0, 0)),
                    pl.BlockSpec((STATE * SUBS, LANES), lambda i: (0, 0)),
                    pl.BlockSpec((STATE * SUBS, LANES), lambda i: (0, 0)),
                    pl.BlockSpec((SUBS, LANES), lambda i: (0, 0)),
                ],
                out_specs=pl.BlockSpec((length * SUBS, LANES), lambda i: (0, 0)),
                scratch_shapes=[pltpu.VMEM((2 * STATE, length, LANES), f32)],
                compiler_params=params(),
                name="local",
            )(scaled, c, decay, gain, skip)
        )

    spots = jnp.arange(chips, dtype=jnp.int32)
    keep_of = lambda mask: 1.0 / jnp.prod(jnp.where(mask, chip_weight, 1.0))
    group = ends
    entering = jnp.zeros_like(ends)
    levels = chips.bit_length() - 1
    for level in range(levels):
        size = 1 << level
        upper = (chip >> level) & 1 == 1
        mine = spots >> level == chip >> level
        theirs = spots >> level == (chip >> level) ^ 1
        inside = chip & (size - 1)
        span = jnp.exp(rate * (-float(length * size)))
        ahead = jnp.exp(rate * (-float(length) * inside.astype(f32)))
        behind = jnp.exp(rate * (-float(length) * (size - 1 - inside).astype(f32)))
        ahead = ahead * keep_of(mine & (spots < chip))
        behind = behind * keep_of(mine & (spots > chip))
        if level == levels - 1:
            got = swap(jnp.where(upper, group[1], group[0]).astype(bf16), "seq", 2 * size)
            got = jnp.stack([got, got]).astype(f32)
        else:
            got = swap(group.astype(bf16), "seq", 2 * size).astype(f32)
        follows = jnp.stack([upper, ~upper])[:, None, None]
        lead = jnp.stack([ahead, behind])
        entering = entering + jnp.where(follows, lead * got, 0.0)
        if level < levels - 1:
            group = jnp.where(
                follows,
                got * (span * keep_of(mine))[None] + group,
                group * (span * keep_of(theirs))[None] + got,
            )

    send, keep = pl.pallas_call(
        finish_kernel,
        out_shape=[shaped((rows, width), bf16), shaped((rows, width))],
        in_specs=[SCALARS] + [WHOLE] * 6 + [pl.BlockSpec(memory_space=pl.ANY)],
        out_specs=[WHOLE] * 2,
        scratch_shapes=[
            pltpu.VMEM((inner, width), bf16),
            pltpu.SemaphoreType.DMA,
            pltpu.VMEM((STREAMS * STATE, length, LANES), f32),
            pltpu.VMEM((STREAMS, length * SUBS, LANES), f32),
            pltpu.VMEM((STREAMS, length, inner), bf16),
        ],
        compiler_params=params(),
        name="finish",
    )(flags, scaled, entering, decay, local_y[0], local_y[1], z, w_out)
    total = keep + swap(send, "seq", 1).astype(f32)
    if ch_count != 2:
        return lax.psum_scatter(total.astype(bf16), "ch", scatter_dimension=1, tiled=True)
    half = width // 2
    where = lax.axis_index("ch")
    theirs = lax.dynamic_slice_in_dim(total, (1 - where) * half, half, 1).astype(bf16)
    mine = lax.dynamic_slice_in_dim(total, where * half, half, 1)
    return (mine + swap(theirs, "ch", 1).astype(f32)).astype(bf16)


def solution(mesh):
    placed = (
        P("seq", "ch"),
        P(),
        P(),
        P(),
        P(),
        P(None, None, "ch"),
        P(None, "ch"),
        P("ch"),
        P(None, "ch"),
        P(None, "ch"),
        P("ch"),
        P("ch", None),
    )
    return jax.shard_map(
        body, mesh=mesh, in_specs=placed, out_specs=P("seq", "ch"), check_vma=False
    )
```

time: 373 us -> 110 us (0.29)
  waiting for transfers between devices: 232 us -> 22.9 us
  Pallas kernels: 0 us -> 48.7 us
  other arithmetic: 50 us -> 4.65 us
  matrix products: 18.3 us -> 0 us
  starting transfers between devices: 31.8 us -> 14 us
  blocking collectives: 7.25 us -> 0 us
  local copies, waits for them, and re-layouts: 18.5 us -> 11.3 us
  between operations: 13.7 us -> 7.75 us
    all_gather x5 -> x0, waiting for transfers between devices: 145 us -> none  [the longest x4 130 us: carried_in(): gathered = jax.tree.map(lambda a: lax.all_gather(a, axis), part)]
    pallas_call x0 -> x7, Pallas kernels: none -> 48.7 us  [the longest x2 14.9 us: body(): pl.pallas_call(functools.partial(local_kernel, s), grid=(1,), out_shape=s...]
    ppermute x9 -> x11, waiting for transfers between devices: 69.4 us -> 22.9 us  [the longest x10 22.9 us: swap(): return lax.ppermute(block, axis, [(i, i ^ apart) for i in range(count)])]
    reduce_sum x42 -> x1, other arithmetic: 25.7 us -> 0.1 us  [body(): jnp.sum((places[:, None] == marks[None, :]).astype(f32), axis=1)]
    dot_general x4 -> x0, matrix products: 18.3 us -> none  [the longest x1 8.57 us: body(): lax.dot_general(stacked, w_in, (((1,), (1,)), ((), ())), preferred_elemen...]
    ppermute x9 -> x11, starting transfers between devices: 31.6 us -> 14 us  [the longest x10 13.3 us: swap(): return lax.ppermute(block, axis, [(i, i ^ apart) for i in range(count)])]
    reduce_scatter x1 -> x0, waiting for transfers between devices: 15.6 us -> none  [body(): lax.psum_scatter(summed.astype(jnp.bfloat16), 'ch', scatter_dimension=1,...]
    convert_element_type x21 -> x5, other arithmetic: 10.8 us -> 0.95 us  [the longest x1 0.76 us: body(): return (mine + swap(theirs, 'ch', 1).astype(f32)).astype(bf16)]
  transfers between devices with their start and end apart: 15 -> 11, of which waited for: 15 -> 7; matrix products, arithmetic and copies ran while one was open for 11% -> 6% of each run, Pallas kernels for 0% -> 19%
where the time goes in v1:
time: 110 us; the launch traced here: 109 us
  Pallas kernels  48.7 us (44%)
  waiting for transfers between devices  22.9 us (21%)
  starting transfers between devices  14 us (13%)
  local copies, waits for them, and re-layouts  11.3 us (10%)
  between operations  7.75 us (7%)
  other arithmetic  4.65 us (4%)
    ppermute x10, waiting for transfers between devices, swap(): return lax.ppermute(block, axis, [(i, i ^ apart) for i in range(count)])  22.9 us
    pallas_call x2, Pallas kernels, body(): pl.pallas_call(functools.partial(local_kernel, s), grid=(1,), out_shape=s...  14.9 us
    ppermute x10, starting transfers between devices, swap(): return lax.ppermute(block, axis, [(i, i ^ apart) for i in range(count)])  13.3 us
    pallas_call x1, Pallas kernels, body(): pl.pallas_call(finish_kernel, out_shape=[shaped((rows, width), bf16), sha...  11.6 us
    pallas_call x1, Pallas kernels, body(): pl.pallas_call(signal_kernel, grid_spec=pltpu.PrefetchScalarGridSpec(num_...  8.6 us
    unnamed x21, local copies, waits for them, and re-layouts  8.5 us
    pallas_call x1, Pallas kernels, body(): pl.pallas_call(end_kernel, out_shape=[shaped((rows, LANES)), shaped((STRE...  6.76 us
    pallas_call x1, Pallas kernels, body(): pl.pallas_call(gate_kernel, grid_spec=pltpu.PrefetchScalarGridSpec(num_sc...  5.52 us
  transfers between devices with their start and end apart: 11, of which 7 were waited for; matrix products, arithmetic and copies ran while one was open for 6% of the time, Pallas kernels for 19%

profile of v1, /device:TPU:0, one launch (start us, length us, event | category | flops | bytes accessed | tf_op | source)
XLA Modules:
  0.0 109.3 jit_solution(552392151429218921)
XLA Ops:
  0.0 3.0 %collective-permute-start = (bf16[128,1024]{1,0:T(8,128)(2,1)}, bf16[128,1024]{1,0:T(8,128)(2,1)S(1)}, u32[]{:S(2)}, u32[]{:S(2)}) collective-permute-start(bf16[128,1024]{1,0:T(8,128)(2,1)} %low.1), channel_id=1, source_target_pairs={{0,1},{1,0},{2,3},{3,2},{4,5},{5,4},{6,7},{7,6},{8,9},{9,8},{10,11... | collective-permute-start | bytes 786440 | tf_op jit(solution)/shard_map/ppermute | solution.py:35
  3.0 0.8 constant_dynamic-slice_fusion
  4.5 0.8 dynamic_slice.26
  5.2 0.8 dynamic_slice.25
  7.2 0.8 select_reduce_fusion.2
  14.6 1.0 fusion.16
  15.8 3.8 %collective-permute-done.2.high_edge = bf16[16,1024]{1,0:T(8,128)(2,1)S(1)} collective-permute-done((bf16[16,1024]{1,0:T(8,128)(2,1)S(1)}, bf16[16,1024]{1,0:T(8,128)(2,1)S(1)}, u32[]{:S(2)}, u32[]{:S(2)}) %collective-permute-start.2) | collective-permute-done | bytes 32800 | tf_op jit(solution)/shard_map/ppermute | solution.py:35
  19.6 0.9 copy-done.4
  20.6 0.8 copy-done.7
  22.0 1.2 %norm.1.own = bf16[144,2048]{1,0:T(8,128)(2,1)S(1)} custom-call(s32[2]{0:T(128)S(1)} %pad_add_fusion.4.flags, bf16[128,1024]{1,0:T(8,128)(2,1)S(1)} %copy-done.4, bf16[128,1024]{1,0:T(8,128)(2,1)S(1)} %collective-permute-done.high, bf16[16,1024]{1,0:T(8,128)(2,1)S(1)} %collective-permute-done.1.low_edge, ...), custom_call_target="tpu_custom_call" | custom-call | tf_op jit(solution)/shard_map/norm/pallas_call | solution.py:351
  23.3 1.8 %collective-permute-start.3 = (bf16[144,2048]{1,0:T(8,128)(2,1)S(1)}, bf16[144,2048]{1,0:T(8,128)(2,1)S(1)}, u32[]{:S(2)}, u32[]{:S(2)}) collective-permute-start(bf16[144,2048]{1,0:T(8,128)(2,1)S(1)} %norm.1.own), channel_id=1, source_target_pairs={{0,2},{2,0},{4,6},{6,4},{8,10},{10,8},{12,14},{14,12},{16,18},{18,... | collective-permute-start | bytes 1769480 | tf_op jit(solution)/shard_map/ppermute | solution.py:35
  25.1 0.8 fusion.29
  26.9 0.9 copy-done.5
  29.2 8.6 %signal.1 = (bf16[544,2048]{1,0:T(8,128)(2,1)}, f32[2,2048,128]{2,1,0:T(8,128)}, f32[128,128]{1,0:T(8,128)S(1)}) custom-call(s32[1]{0:T(128)} %bitcast.flags, bf16[144,2048]{1,0:T(8,128)(2,1)S(1)} %norm.1.own, bf16[144,2048]{1,0:T(8,128)(2,1)S(1)} %collective-permute-done.3.other, bf16[2,2048,2048]{2,1,0:T(8,128)(2,1)} %w.3, f32[4,2048]{1,0:T(4,128)S(1)} %copy-done.6, ...), custom_call_target="tpu_custom_call" | custom-call | tf_op jit(solution)/shard_map/signal/pallas_call | solution.py:394
  38.3 0.8 collective-permute-done.4
  39.7 3.8 %collective-permute-done.5.bc_far = f32[128,128]{1,0:T(8,128)S(1)} collective-permute-done((f32[128,128]{1,0:T(8,128)S(1)}, f32[128,128]{1,0:T(8,128)S(1)}, u32[]{:S(2)}, u32[]{:S(2)}) %collective-permute-start.5) | collective-permute-done | bytes 65568 | tf_op jit(solution)/shard_map/ppermute | solution.py:35
  43.4 6.8 %ends.1 = (f32[128,128]{1,0:T(8,128)S(1)}, f32[2,128,128]{2,1,0:T(8,128)S(1)}) custom-call(f32[128,128]{1,0:T(8,128)S(1)} %add.70.bc_own, f32[128,128]{1,0:T(8,128)S(1)} %collective-permute-done.5.bc_far, f32[128,128]{1,0:T(8,128)S(1)} %copy.19.weigh, f32[2,2048,128]{2,1,0:T(8,128)} %get-tuple-element.13.c, f32[128,128]{1,0:T(8,128)S(1)} %exp.88.decay, ...), custom_call_target="tpu_custom_call" | custom-call | tf_op jit(solution)/shard_map/ends/pallas_call | solution.py:449
  50.2 1.6 %collective-permute-start.6 = (bf16[2,128,128]{2,1,0:T(8,128)(2,1)S(1)}, bf16[2,128,128]{2,1,0:T(8,128)(2,1)S(1)}, u32[]{:S(2)}, u32[]{:S(2)}) collective-permute-start(bf16[2,128,128]{2,1,0:T(8,128)(2,1)S(1)} %convert_element_type.54), channel_id=1, source_target_pairs={{0,4},{2,6},{4,0},{6,2},{8,12},{10,14},{12,8},{14,10},{16,20},{18,... | collective-permute-start | bytes 196616 | tf_op jit(solution)/shard_map/ppermute | solution.py:35
  51.9 2.6 %collective-permute-done.6 = bf16[2,128,128]{2,1,0:T(8,128)(2,1)S(1)} collective-permute-done((bf16[2,128,128]{2,1,0:T(8,128)(2,1)S(1)}, bf16[2,128,128]{2,1,0:T(8,128)(2,1)S(1)}, u32[]{:S(2)}, u32[]{:S(2)}) %collective-permute-start.6) | collective-permute-done | bytes 65568 | tf_op jit(solution)/shard_map/ppermute | solution.py:35
  54.6 2.2 %collective-permute-start.7 = (bf16[2,128,128]{2,1,0:T(8,128)(2,1)S(1)}, bf16[2,128,128]{2,1,0:T(8,128)(2,1)S(1)}, u32[]{:S(2)}, u32[]{:S(2)}) collective-permute-start(bf16[2,128,128]{2,1,0:T(8,128)(2,1)S(1)} %fusion.28), channel_id=1, source_target_pairs={{0,8},{2,10},{4,12},{6,14},{8,0},{10,2},{12,4},{14,6},{16,24},{18,... | collective-permute-start | bytes 196616 | tf_op jit(solution)/shard_map/ppermute | solution.py:35
  56.9 2.2 %collective-permute-done.7 = bf16[2,128,128]{2,1,0:T(8,128)(2,1)S(1)} collective-permute-done((bf16[2,128,128]{2,1,0:T(8,128)(2,1)S(1)}, bf16[2,128,128]{2,1,0:T(8,128)(2,1)S(1)}, u32[]{:S(2)}, u32[]{:S(2)}) %collective-permute-start.7) | collective-permute-done | bytes 65568 | tf_op jit(solution)/shard_map/ppermute | solution.py:35
  59.2 3.3 %collective-permute-start.8 = (bf16[128,128]{1,0:T(8,128)(2,1)S(1)}, bf16[128,128]{1,0:T(8,128)(2,1)S(1)}, u32[]{:S(2)}, u32[]{:S(2)}) collective-permute-start(bf16[128,128]{1,0:T(8,128)(2,1)S(1)} %fusion.17), channel_id=1, source_target_pairs={{0,16},{2,18},{4,20},{6,22},{8,24},{10,26},{12,28},{14,30},{16,0},... | collective-permute-start | bytes 98312 | tf_op jit(solution)/shard_map/ppermute | solution.py:35
  62.7 5.5 %gate.1.z = bf16[2,256,1024]{2,1,0:T(8,128)(2,1)S(1)} custom-call(s32[1]{0:T(128)} %bitcast.flags, bf16[544,2048]{1,0:T(8,128)(2,1)} %get-tuple-element.16.rows_in, bf16[2,2048,2048]{2,1,0:T(8,128)(2,1)} %w.3), custom_call_target="tpu_custom_call" | custom-call | tf_op jit(solution)/shard_map/gate/pallas_call | solution.py:433
  68.2 1.0 copy-done.1
  69.3 8.0 %local.3.y_b = f32[2048,128]{1,0:T(8,128)S(1)} custom-call(f32[128,128]{1,0:T(8,128)S(1)} %get-tuple-element.14.bc_in, f32[2,2048,128]{2,1,0:T(8,128)} %get-tuple-element.13.c, f32[128,128]{1,0:T(8,128)S(1)} %exp.88.decay, f32[128,128]{1,0:T(8,128)S(1)} %sqrt.6.gain, f32[8,128]{1,0:T(8,128)S(1)} %dynamic-slice_bitcast_fusion.skip), custom_call_target="tpu_custom_call" | custom-call | tf_op jit(solution)/shard_map/local/pallas_call | solution.py:462
  77.3 1.0 copy-done.2
  78.3 6.9 %local.2.y_f = f32[2048,128]{1,0:T(8,128)S(1)} custom-call(f32[128,128]{1,0:T(8,128)S(1)} %get-tuple-element.14.bc_in, f32[2,2048,128]{2,1,0:T(8,128)} %get-tuple-element.13.c, f32[128,128]{1,0:T(8,128)S(1)} %exp.88.decay, f32[128,128]{1,0:T(8,128)S(1)} %sqrt.6.gain, f32[8,128]{1,0:T(8,128)S(1)} %dynamic-slice_bitcast_fusion.skip), custom_call_target="tpu_custom_call" | custom-call | tf_op jit(solution)/shard_map/local/pallas_call | solution.py:462
  85.2 1.0 copy-done.3
  86.3 11.6 %finish.1 = (bf16[128,2048]{1,0:T(8,128)(2,1)S(1)}, f32[128,2048]{1,0:T(8,128)S(1)}) custom-call(s32[1]{0:T(128)} %bitcast.flags, f32[128,128]{1,0:T(8,128)S(1)} %get-tuple-element.14.bc_in, f32[2,128,128]{2,1,0:T(8,128)S(1)} %fusion.2.entering, f32[128,128]{1,0:T(8,128)S(1)} %exp.88.decay, f32[2048,128]{1,0:T(8,128)} %copy-done.3, f32[2048,128]{1,0:T(8,128)} %copy-done.2, ...), custom_call_target="tpu_custom_call" | custom-call | tf_op jit(solution)/shard_map/finish/pallas_call | solution.py:511
  98.0 1.9 %collective-permute-done.9 = bf16[128,2048]{1,0:T(8,128)(2,1)S(1)} collective-permute-done((bf16[128,2048]{1,0:T(8,128)(2,1)S(1)}, bf16[128,2048]{1,0:T(8,128)(2,1)S(1)}, u32[]{:S(2)}, u32[]{:S(2)}) %collective-permute-start.9) | collective-permute-done | bytes 524320 | tf_op jit(solution)/shard_map/ppermute | solution.py:35
  100.7 7.8 %collective-permute-done.10 = bf16[128,1024]{1,0:T(8,128)(2,1)S(1)} collective-permute-done((bf16[128,1024]{1,0:T(8,128)(2,1)S(1)}, bf16[128,1024]{1,0:T(8,128)(2,1)S(1)}, u32[]{:S(2)}, u32[]{:S(2)}) %collective-permute-start.10) | collective-permute-done | bytes 262176 | tf_op jit(solution)/shard_map/ppermute | solution.py:35
  108.5 0.8 add_convert_fusion
  (65 shorter events, 6.8 us)
Async XLA Ops:
  0.0 39.7 %copy-start = (f32[2048]{0:T(1024)S(1)}, f32[2048]{0:T(1024)}, u32[]{:S(2)}) copy-start(f32[2048]{0:T(1024)} %param.22) | copy-start | bytes 24580
  0.0 19.6 %collective-permute-start = (bf16[128,1024]{1,0:T(8,128)(2,1)}, bf16[128,1024]{1,0:T(8,128)(2,1)S(1)}, u32[]{:S(2)}, u32[]{:S(2)}) collective-permute-start(bf16[128,1024]{1,0:T(8,128)(2,1)} %low.1), channel_id=1, source_target_pairs={{0,1},{1,0},{2,3},{3,2},{4,5},{5,4},{6,7},{7,6},{8,9},{9,8},{10,11... | collective-permute-start | bytes 786440 | tf_op jit(solution)/shard_map/ppermute | solution.py:35
  3.8 11.9 %collective-permute-start.1 = (bf16[16,1024]{1,0:T(8,128)(2,1)S(1)}, bf16[16,1024]{1,0:T(8,128)(2,1)S(1)}, u32[]{:S(2)}, u32[]{:S(2)}) collective-permute-start(bf16[16,1024]{1,0:T(8,128)(2,1)S(1)} %constant_dynamic-slice_fusion), channel_id=1, source_target_pairs={{2,4},{6,8},{10,12},{14,16},{18,20},{22,24},{26,28},{4,2},{8,6},{1... | collective-permute-start | bytes 98312 | tf_op jit(solution)/shard_map/ppermute | solution.py:341
  15.7 4.0 %collective-permute-start.2 = (bf16[16,1024]{1,0:T(8,128)(2,1)S(1)}, bf16[16,1024]{1,0:T(8,128)(2,1)S(1)}, u32[]{:S(2)}, u32[]{:S(2)}) collective-permute-start(bf16[16,1024]{1,0:T(8,128)(2,1)S(1)} %collective-permute-done.1.low_edge), channel_id=1, source_target_pairs={{0,1},{1,0},{2,3},{3,2},{4,5},{5,4},{6,7},{7,6},{8,9},{9,8},{10,11... | collective-permute-start | bytes 98312 | tf_op jit(solution)/shard_map/ppermute | solution.py:35
  19.6 1.0 copy-start.4
  20.6 0.8 copy-start.7
  21.4 0.7 copy-start.9
  23.3 3.6 %collective-permute-start.3 = (bf16[144,2048]{1,0:T(8,128)(2,1)S(1)}, bf16[144,2048]{1,0:T(8,128)(2,1)S(1)}, u32[]{:S(2)}, u32[]{:S(2)}) collective-permute-start(bf16[144,2048]{1,0:T(8,128)(2,1)S(1)} %norm.1.own), channel_id=1, source_target_pairs={{0,2},{2,0},{4,6},{6,4},{8,10},{10,8},{12,14},{14,12},{16,18},{18,... | collective-permute-start | bytes 1769480 | tf_op jit(solution)/shard_map/ppermute | solution.py:35
  26.9 0.9 copy-start.5
  27.8 0.8 copy-start.6
  28.5 0.7 copy-start.8
  37.8 1.3 %collective-permute-start.4 = (f32[128,128]{1,0:T(8,128)S(1)}, f32[128,128]{1,0:T(8,128)S(1)}, u32[]{:S(2)}, u32[]{:S(2)}) collective-permute-start(f32[128,128]{1,0:T(8,128)S(1)} %get-tuple-element.12), channel_id=1, source_target_pairs={{0,2},{2,0},{4,6},{6,4},{8,10},{10,8},{12,14},{14,12},{16,18},{18,... | collective-permute-start | bytes 196616 | tf_op jit(solution)/shard_map/ppermute | solution.py:35
  39.1 4.3 %collective-permute-start.5 = (f32[128,128]{1,0:T(8,128)S(1)}, f32[128,128]{1,0:T(8,128)S(1)}, u32[]{:S(2)}, u32[]{:S(2)}) collective-permute-start(f32[128,128]{1,0:T(8,128)S(1)} %add.70.bc_own), channel_id=1, source_target_pairs={{0,1},{1,0},{2,3},{3,2},{4,5},{5,4},{6,7},{7,6},{8,9},{9,8},{10,11... | collective-permute-start | bytes 196616 | tf_op jit(solution)/shard_map/ppermute | solution.py:35
  50.2 4.3 %collective-permute-start.6 = (bf16[2,128,128]{2,1,0:T(8,128)(2,1)S(1)}, bf16[2,128,128]{2,1,0:T(8,128)(2,1)S(1)}, u32[]{:S(2)}, u32[]{:S(2)}) collective-permute-start(bf16[2,128,128]{2,1,0:T(8,128)(2,1)S(1)} %convert_element_type.54), channel_id=1, source_target_pairs={{0,4},{2,6},{4,0},{6,2},{8,12},{10,14},{12,8},{14,10},{16,20},{18,... | collective-permute-start | bytes 196616 | tf_op jit(solution)/shard_map/ppermute | solution.py:35
  54.6 4.5 %collective-permute-start.7 = (bf16[2,128,128]{2,1,0:T(8,128)(2,1)S(1)}, bf16[2,128,128]{2,1,0:T(8,128)(2,1)S(1)}, u32[]{:S(2)}, u32[]{:S(2)}) collective-permute-start(bf16[2,128,128]{2,1,0:T(8,128)(2,1)S(1)} %fusion.28), channel_id=1, source_target_pairs={{0,8},{2,10},{4,12},{6,14},{8,0},{10,2},{12,4},{14,6},{16,24},{18,... | collective-permute-start | bytes 196616 | tf_op jit(solution)/shard_map/ppermute | solution.py:35
  59.2 27.0 %collective-permute-start.8 = (bf16[128,128]{1,0:T(8,128)(2,1)S(1)}, bf16[128,128]{1,0:T(8,128)(2,1)S(1)}, u32[]{:S(2)}, u32[]{:S(2)}) collective-permute-start(bf16[128,128]{1,0:T(8,128)(2,1)S(1)} %fusion.17), channel_id=1, source_target_pairs={{0,16},{2,18},{4,20},{6,22},{8,24},{10,26},{12,28},{14,30},{16,0},... | collective-permute-start | bytes 98312 | tf_op jit(solution)/shard_map/ppermute | solution.py:35
  68.2 1.0 copy-start.1
  77.3 1.0 copy-start.2
  85.2 1.0 copy-start.3
  97.9 2.0 %collective-permute-start.9 = (bf16[128,2048]{1,0:T(8,128)(2,1)S(1)}, bf16[128,2048]{1,0:T(8,128)(2,1)S(1)}, u32[]{:S(2)}, u32[]{:S(2)}) collective-permute-start(bf16[128,2048]{1,0:T(8,128)(2,1)S(1)} %get-tuple-element.18), channel_id=1, source_target_pairs={{0,2},{2,0},{4,6},{6,4},{8,10},{10,8},{12,14},{14,12},{16,18},{18,... | collective-permute-start | bytes 1572872 | tf_op jit(solution)/shard_map/ppermute | solution.py:35
  100.1 8.4 %collective-permute-start.10 = (bf16[128,1024]{1,0:T(8,128)(2,1)S(1)}, bf16[128,1024]{1,0:T(8,128)(2,1)S(1)}, u32[]{:S(2)}, u32[]{:S(2)}) collective-permute-start(bf16[128,1024]{1,0:T(8,128)(2,1)S(1)} %dynamic-slice_convert_fusion), channel_id=1, source_target_pairs={{0,1},{1,0},{2,3},{3,2},{4,5},{5,4},{6,7},{7,6},{8,9},{9,8},{10,11... | collective-permute-start | bytes 786440 | tf_op jit(solution)/shard_map/ppermute | solution.py:35

commit v2 on v0

v2 whole, which is shorter than its diff:
```python
import functools

import jax
import jax.numpy as jnp
from jax import lax
from jax.experimental import pallas as pl
from jax.experimental.pallas import tpu as pltpu
from jax.sharding import PartitionSpec as P

CONV = 4
STATE = 16
EDGE = 16
LANES = 128
SUBS = 8
STREAMS = 2
CHUNK = 16
BLOCK = 256
HALVES = 2
epsilon = 1e-05
f32 = jnp.float32
bf16 = jnp.bfloat16

WHOLE = pl.BlockSpec(memory_space=pltpu.VMEM)
SCALARS = pl.BlockSpec(memory_space=pltpu.SMEM)
ANYWHERE = pl.BlockSpec(memory_space=pltpu.HBM)


def shaped(shape, dtype=f32):
    return jax.ShapeDtypeStruct(shape, dtype)


def call(kernel, name, outs, ins, scratch=(), megabytes=4):
    return pl.pallas_call(
        kernel,
        out_shape=outs,
        in_specs=ins,
        out_specs=jax.tree.map(lambda _: WHOLE, outs),
        scratch_shapes=list(scratch),
        compiler_params=pltpu.CompilerParams(vmem_limit_bytes=megabytes << 20),
        name=name,
    )


def tile(t):
    return slice(t * LANES, (t + 1) * LANES)


def spot():
    place = lax.axis_index("seq")
    return place, place & 1, place >> 1


def swap(block, axis, apart):
    count = lax.axis_size(axis)
    return lax.ppermute(block, axis, [(i, i ^ apart) for i in range(count)])


def in_hbm(array):
    return pltpu.with_memory_space_constraint(array, pltpu.HBM)


def both_halves(block):
    if lax.axis_size("ch") == 2:
        return block, swap(block, "ch", 1)
    full = lax.all_gather(block, "ch", axis=1, tiled=True)
    half = full.shape[1] // 2
    return full[:, :half], full[:, half:]


def rims(rim):
    seq_count, ch_count = lax.axis_size("seq"), lax.axis_size("ch")
    pairs = [(i, i + 1) for i in range(1, seq_count - 1, 2)]
    pairs = pairs + [(j, i) for i, j in pairs]
    if ch_count != 2:
        return both_halves(lax.ppermute(rim, "seq", pairs))
    return tuple(
        lax.ppermute(
            rim,
            ("seq", "ch"),
            [(i * ch_count + (k ^ apart), j * ch_count + k) for i, j in pairs for k in range(2)],
        )
        for apart in range(2)
    )


def between(chip, m):
    pair = chip >> 1
    other = pair ^ m
    below = other < pair
    return jnp.where(below, 2 * other + 2, chip + 1), jnp.where(below, chip, 2 * other), below


def init_kernel(
    bounds, tokens_all, w_in, conv_w, conv_b, proj, rate_all, skip, gain_all, embed_all, hidden,
    signal_w, taps, offset, proj_half, rate, skip_half, norm_gain, embed, rim,
    bases, weigh, decay, keeps, tokens, sems,
):
    place, core, chip = spot()
    count, rows = tokens.shape
    length = 2 * rows
    inner = signal_w.shape[1]
    chips = count // 2
    mine = pl.ds(pl.multiple_of(core * inner, inner), inner)
    copies = [
        pltpu.make_async_copy(source, target, sems.at[i])
        for i, (source, target) in enumerate(
            (
                (rate_all.at[:, mine], rate),
                (tokens_all, tokens),
                (gain_all, norm_gain),
                (embed_all, embed),
                (conv_w.at[:, mine], taps),
                (conv_b.at[:, mine], offset),
                (proj.at[:, mine], proj_half),
                (skip.at[:, mine], skip_half),
                (
                    hidden.at[pl.ds(pl.multiple_of(core * (rows - EDGE), EDGE), EDGE), :],
                    rim,
                ),
                (w_in.at[0, :, mine], signal_w),
            )
        )
    ]
    for copy in copies:
        copy.start()

    marks = [bounds[k, i] for i in range(bounds.shape[1]) for k in range(2)]
    factors = []
    for i, mark in enumerate(marks):
        total = jnp.int32(1)
        earlier = jnp.int32(0)
        for k, other in enumerate(marks):
            same = jnp.where(other == mark, 1, 0)
            total = total + same
            if k < i:
                earlier = earlier + same
        factors.append(jnp.where(earlier > 0, 1, total).astype(f32))

    start = chip * length
    at = lax.broadcasted_iota(jnp.int32, (SUBS, rows), 1) + start
    for half in range(HALVES):
        runs = [jnp.ones((SUBS, rows), f32) for _ in range(STREAMS)]
        for mark, factor in zip(marks, factors):
            here = at + half * rows
            runs[0] = runs[0] * jnp.where((here >= mark) & (mark >= start), factor, 1.0)
            runs[1] = runs[1] * jnp.where((here <= mark) & (mark < start + length), factor, 1.0)
        for s in range(STREAMS):
            first = 2 * STATE * (2 * half + s)
            for k in range(STATE // SUBS):
                weigh[first + k * SUBS : first + (k + 1) * SUBS, :] = runs[s]
                low = first + STATE + k * SUBS
                weigh[low : low + SUBS, :] = 1.0 / runs[s]

    def kept(low, high):
        total = jnp.ones((SUBS, LANES), f32)
        for mark, factor in zip(marks, factors):
            total = total * jnp.where(
                (mark >= low * length) & (mark < high * length), factor, 1.0
            )
        return 1.0 / total

    keeps[0] = kept(chip, chip + 1)
    keeps[1] = kept(chip ^ 1, (chip ^ 1) + 1)
    for m in range(1, chips // 2):
        low, high, _ = between(chip, m)
        keeps[1 + m] = kept(low, high)
    copies[0].wait()
    for t in range(inner // LANES):
        decay[:, tile(t)] = jnp.exp(-rate[:, tile(t)])

    copies[1].wait()

    def column(row):
        line = tokens[pl.ds(row, 1), :].astype(f32)
        return jnp.broadcast_to(line, (rows, rows)).T

    bases[:rows, :] = column(place)
    beyond = column(jnp.clip(jnp.where(core == 0, place - 1, place + 1), 0, count - 1))
    beyond = jnp.where(core == 0, beyond[rows - EDGE :], beyond[:EDGE])
    inside = jnp.where(core == 0, place > 0, place < count - 1)
    bases[rows:, :] = jnp.where(inside, beyond, -1.0)
    for copy in copies[2:]:
        copy.wait()


def norm_kernel(own, far, own_rim, far_rim, bases, gain, embed, out):
    rows = own.shape[0]
    half = own.shape[1]
    index = lax.axis_index("ch") if lax.axis_size("ch") == 2 else jnp.int32(0)

    def one(first, second, low, count):
        marks = bases[low : low + count, :]
        total = jnp.zeros((count, LANES), f32)
        for part in (first, second):
            for t in range(half // LANES):
                v = part[:, tile(t)].astype(f32)
                total = total + v * v
        inv_rms = lax.rsqrt(jnp.sum(total, axis=1, keepdims=True) / (2 * half) + epsilon)
        inv_rms = jnp.broadcast_to(inv_rms, (count, LANES))
        for k, part in enumerate((first, second)):
            for t in range(half // LANES):
                cols = slice(k * half + t * LANES, k * half + (t + 1) * LANES)
                e = [embed[b : b + 1, cols] for b in range(4)]
                added = jnp.where(
                    marks < 0.5, e[0], jnp.where(marks < 1.5, e[1], jnp.where(marks < 2.5, e[2], e[3]))
                )
                v = part[:, tile(t)].astype(f32) * inv_rms * gain[0:1, cols] + added
                out[low : low + count, cols] = jnp.where(marks < -0.5, 0.0, v).astype(bf16)

    @pl.when(index == 0)
    def _():
        one(own, far, 0, rows)
        one(own_rim, far_rim, rows, EDGE)

    @pl.when(index != 0)
    def _():
        one(far, own, 0, rows)
        one(far_rim, own_rim, rows, EDGE)


def signal_kernel(
    own, other, w, taps, offset, proj, w_in, lined, c_out, bc_out, gate_w, x_tiles, sem
):
    _, core, _ = spot()
    rows = own.shape[0] - EDGE
    length = 2 * rows
    width = own.shape[1]
    padded = length + EDGE
    inner = w.shape[1]
    block = min(BLOCK, inner)
    tiles = block // LANES
    fetch = pltpu.make_async_copy(
        w_in.at[1, :, pl.ds(pl.multiple_of(core * inner, inner), inner)], gate_w, sem
    )
    fetch.start()

    def line_up(first, second):
        lined[0:EDGE, :] = first[rows:, :]
        lined[EDGE : EDGE + rows, :] = first[:rows, :]
        lined[EDGE + rows : padded, :] = second[:rows, :]
        r = lax.broadcasted_iota(jnp.int32, (LANES, LANES), 0)
        q = lax.broadcasted_iota(jnp.int32, (LANES, LANES), 1)
        turn = jnp.where(r + q == LANES - 1, 1.0, 0.0).astype(bf16)
        for t in range(width // LANES):
            at = tile(width // LANES - 1 - t)
            for base, piece in ((0, first[:rows, at]), (rows, second[:, at])):
                turned = jnp.dot(piece, turn, preferred_element_type=f32).astype(bf16)
                lined[padded + base : padded + base + piece.shape[0], tile(t)] = turned

    @pl.when(core == 0)
    def _():
        line_up(own, other)

    @pl.when(core != 0)
    def _():
        line_up(other, own)

    inner_bc = 2 * STATE
    sums = [jnp.zeros((inner_bc, rows), f32) for _ in range(STREAMS * HALVES)]

    def project(b, s):
        x = jnp.dot(
            lined[s * padded : (s + 1) * padded, :],
            w[:, b * block : (b + 1) * block],
            preferred_element_type=f32,
        )
        x = x.astype(bf16).astype(f32)
        for t in range(tiles):
            x_tiles[(b % 2 * STREAMS + s) * tiles + t] = x[:, tile(t)]

    def convolve(b, s):
        mixed = []
        for t in range(tiles):
            slot = (b % 2 * STREAMS + s) * tiles + t
            cols = tile(b * tiles + t)
            total = offset[0:1, cols]
            for k in range(CONV):
                at = EDGE - CONV + 1 + k if s == 0 else CONV - 1 - k
                total = total + x_tiles[slot, at : at + length, :] * taps[k : k + 1, cols]
            c = jax.nn.silu(total).astype(bf16)
            c_out[s, b * tiles + t] = c.astype(f32)
            mixed.append(c)
        mixed = mixed[0] if tiles == 1 else jnp.concatenate(mixed, axis=1)
        for half in range(HALVES):
            sums[2 * half + s] = sums[2 * half + s] + lax.dot_general(
                proj[:, b * block : (b + 1) * block],
                mixed[half * rows : (half + 1) * rows],
                (((1,), (1,)), ((), ())),
                preferred_element_type=f32,
            )

    turns = [(b, s) for b in range(inner // block) for s in range(STREAMS)]
    project(*turns[0])
    for before, after in zip(turns, turns[1:] + [None]):
        if after is not None:
            project(*after)
        convolve(*before)
    for i, total in enumerate(sums):
        bc_out[i * inner_bc : (i + 1) * inner_bc, :] = total
    fetch.wait()


def gate_kernel(lined, w, z_out):
    padded = lined.shape[0] // 2
    length = padded - EDGE
    inner = w.shape[1]
    block = min(BLOCK, inner)
    for b in range(inner // block):
        cols = slice(b * block, (b + 1) * block)
        for s, first in ((0, EDGE), (1, padded)):
            z = jnp.dot(lined[first : first + length, :], w[:, cols], preferred_element_type=f32)
            z_out[s, :, cols] = z.astype(bf16)


def lane_of(values, lane):
    return jnp.take_along_axis(values, jnp.full(values.shape, lane, jnp.int32), axis=1)


def tiles_of(ref, count):
    return [ref[h * SUBS : (h + 1) * SUBS, tile(t)] for t in range(count) for h in range(2)]


def spread(bc, wide, stream):
    rows = bc.shape[1]
    ones = jnp.ones((2 * rows, LANES), bf16)
    lanes = lax.broadcasted_iota(jnp.int32, (STATE, 2 * rows), 1) & (rows - 1)
    group = 8
    for half in range(HALVES):
        first = 2 * STATE * (2 * half + stream)
        exact = bc[first : first + STATE, :]
        high = exact.astype(bf16)
        low = (exact - high.astype(f32)).astype(bf16)
        entries = jnp.concatenate([high, low], axis=1).astype(f32)
        for j in range(0, rows, group):
            alone = jnp.concatenate(
                [jnp.where(lanes == j + i, entries, 0.0).astype(bf16) for i in range(group)], axis=0
            )
            at = (half * rows + j) * STATE
            wide[stream, at : at + group * STATE, :] = jnp.dot(
                alone, ones, preferred_element_type=f32
            )


def end_kernel(bc_own, bc_far, weigh, c, decay, end_gain, after_z, bc_out, end_out, wide):
    rows = bc_own.shape[1]
    length = 2 * rows
    count = c.shape[1]
    bc_out[...] = (bc_own[...] + bc_far[...]) * weigh[...]
    for s in range(STREAMS):
        spread(bc_out, wide, s)
    a = tiles_of(decay, count)

    def one(j, state):
        after = []
        for s in range(STREAMS):
            t0 = j if s == 0 else length - 1 - j
            low = pl.multiple_of(t0 * STATE, STATE)
            b = [wide[s, pl.ds(low + h * SUBS, SUBS), :] for h in range(2)]
            for t in range(count):
                x = c[s, t, pl.ds(t0, 1), :]
                for h in range(2):
                    i = 2 * t + h
                    after.append(a[i] * state[s * 2 * count + i] + b[h] * x)
        return tuple(after)

    zero = jnp.zeros((SUBS, LANES), f32)
    state = lax.fori_loop(0, length, one, (zero,) * (STREAMS * 2 * count), unroll=8)
    for s in range(STREAMS):
        for t in range(count):
            for h in range(2):
                sub = slice(h * SUBS, (h + 1) * SUBS)
                end_out[s, sub, tile(t)] = state[s * 2 * count + 2 * t + h] * end_gain[sub, tile(t)]


def local_kernel(stream, bc, wide, c, decay, drive, skip, after_got, *rest):
    if stream == 1:
        w_out, y_out, readout, out_w, driven, sem = rest
        inner = decay.shape[1]
        mine = pl.ds(pl.multiple_of(spot()[1] * inner, inner), inner)
        fetch = pltpu.make_async_copy(w_out.at[mine, :], out_w, sem)
        fetch.start()
    else:
        y_out, readout, driven = rest
    rows = bc.shape[1]
    length = 2 * rows
    count = c.shape[1]
    span = CHUNK * STATE
    turned = bc[...].T.astype(bf16)
    for half in range(HALVES):
        r = lax.broadcasted_iota(jnp.int32, (rows, span), 0)
        q = lax.broadcasted_iota(jnp.int32, (rows, span), 1)
        first = 2 * STATE * (2 * half + stream) + STATE
        pick = jnp.where(r == first + (q & (STATE - 1)), 1.0, 0.0).astype(bf16)
        picked = jnp.dot(turned, pick, preferred_element_type=f32)
        step = r & (CHUNK - 1) if stream == 0 else CHUNK - 1 - (r & (CHUNK - 1))
        readout[half * rows : (half + 1) * rows, :] = jnp.where(
            q // STATE == step, picked, 0.0
        ).astype(bf16)
    a = tiles_of(decay, count)

    def chunks(n, state):
        state = list(state)
        base = n * CHUNK if stream == 0 else length - (n + 1) * CHUNK
        base = pl.multiple_of(base, CHUNK)
        low = pl.multiple_of(base * STATE, span)
        to = pl.multiple_of(n * span, span)
        for j in range(CHUNK):
            i = j if stream == 0 else CHUNK - 1 - j
            b = [wide[stream, pl.ds(low + i * STATE + h * SUBS, SUBS), :] for h in range(2)]
            for t in range(count):
                x = c[stream, t, pl.ds(base + i, 1), :]
                for h in range(2):
                    m = 2 * t + h
                    state[m] = a[m] * state[m] + b[h] * x
                both = jnp.concatenate([state[2 * t], state[2 * t + 1]], axis=0)
                driven[pl.ds(to + j * STATE, STATE), tile(t)] = (
                    both.astype(bf16) * drive[:, tile(t)]
                )
        return tuple(state)

    zero = jnp.zeros((SUBS, LANES), f32)
    lax.fori_loop(0, length // CHUNK, chunks, (zero,) * (2 * count))
    for n in range(length // CHUNK):
        base = n * CHUNK if stream == 0 else length - (n + 1) * CHUNK
        at = slice(base, base + CHUNK)
        y = jnp.dot(
            readout[at, :], driven[n * span : (n + 1) * span, :], preferred_element_type=f32
        )
        for t in range(count):
            y_out[at, tile(t)] = y[:, tile(t)] + skip[0:1, tile(t)] * c[stream, t, at, :]
    if stream == 1:
        fetch.wait()


def factor_kernel(rate, keeps, after_ends, strides, powers, first_step, leads):
    _, _, chip = spot()
    inner = rate.shape[1]
    upper = chip & 1
    for t in range(inner // LANES):
        d = rate[:, tile(t)]
        a = jnp.exp(-d)
        strides[0, :, tile(t)] = jnp.exp(-float(CHUNK) * d)
        strides[1, :, tile(t)] = jnp.exp(-float(LANES) * d)
        power = a
        for j in range(CHUNK):
            powers[j * STATE : (j + 1) * STATE, tile(t)] = power.astype(bf16)
            power = power * a
        d = d * float(-2 * LANES)
        span = jnp.exp(d)
        own = span * keeps[0, 0:1, :]
        beside = span * keeps[1, 0:1, :]
        first_step[0, 0, :, tile(t)] = jnp.where(upper == 1, own, 1.0)
        first_step[0, 1, :, tile(t)] = jnp.where(upper == 1, 1.0, own)
        first_step[1, 0, :, tile(t)] = jnp.where(upper == 1, 1.0, beside)
        first_step[1, 1, :, tile(t)] = jnp.where(upper == 1, beside, 1.0)
        for m in range(1, keeps.shape[0] - 1):
            low, high, below = between(chip, m)
            lead = jnp.exp(d * (high - low).astype(f32)) * keeps[1 + m, 0:1, :]
            leads[m - 1, 0, :, tile(t)] = jnp.where(below, lead, 0.0)
            leads[m - 1, 1, :, tile(t)] = jnp.where(below, 0.0, lead)


def pair_kernel(ends, got, first_step, after_local, *sends):
    _, _, chip = spot()
    group = [
        (got[s].astype(f32) * first_step[0, s] + ends[s] * first_step[1, s]).astype(bf16)
        for s in range(STREAMS)
    ]
    for m, send in enumerate(sends):
        _, _, below = between(chip, m + 1)
        send[...] = jnp.where(below, group[1], group[0])


def columns(gated, w, out, part):
    inner, width = w.shape
    rows, half = out.shape
    base = pl.multiple_of(part * half, half)
    back = LANES - 1 - lax.broadcasted_iota(jnp.int32, (rows, LANES), 1)
    strip = min(BLOCK, half)
    for low in range(0, half, strip):
        here = pl.ds(pl.multiple_of(base + low, strip), strip)
        there = pl.ds(pl.multiple_of(width - base - low - strip, strip), strip)
        ahead = jnp.dot(gated[0], w[:, here], preferred_element_type=f32)
        behind = jnp.dot(gated[1], w[:, there], preferred_element_type=f32)
        for t in range(strip // LANES):
            turned = jnp.take_along_axis(behind[:, tile(strip // LANES - 1 - t)], back, axis=1)
            total = ahead[:, tile(t)] + turned
            out[:, low + t * LANES : low + (t + 1) * LANES] = total.astype(out.dtype)


def part_of(own):
    if lax.axis_size("ch") != 2:
        return jnp.int32(1 if own else 0)
    return lax.axis_index("ch") if own else 1 - lax.axis_index("ch")


def finish_kernel(
    same, powers, strides, got, leads, y_f, y_b, readout_f, readout_b, z, w, *rest
):
    *arrived, out, gated = rest
    _, core, chip = spot()
    rows = out.shape[0]
    inner = w.shape[0]
    half = core if same else 1 - core
    base = pl.multiple_of(half * rows, rows)
    span = CHUNK * STATE
    local = (y_f, y_b)
    readouts = (readout_f, readout_b)
    for s in range(STREAMS):
        state = got[s].astype(f32) * jnp.where(chip & 1 == 1 - s, 1.0, 0.0)
        for m, part in enumerate(arrived):
            state = state + part[...].astype(f32) * leads[m, s]
        state = state * jnp.where(half == 1 - s, strides[1], 1.0)
        for q in range(rows // CHUNK):
            row = q * CHUNK if s == 0 else rows - (q + 1) * CHUNK
            at = pl.ds(pl.multiple_of(base + row, CHUNK), CHUNK)
            carried = powers[...].reshape(CHUNK, STATE, inner) * state.astype(bf16)[None]
            state = state * strides[0]
            y = jnp.dot(
                readouts[s][at, :], carried.reshape(span, inner), preferred_element_type=f32
            )
            y = y + local[s][at, :]
            gated[s, row : row + CHUNK, :] = (
                y * jax.nn.silu(z[s, at, :].astype(f32))
            ).astype(bf16)
    columns(gated, w, out, part_of(False))


def rest_kernel(gated, w, after_first, out):
    columns(gated, w, out, part_of(True))


def body(
    hidden,
    tokens,
    edit_bounds,
    norm_gain,
    base_embed,
    w_in,
    conv_w,
    conv_b,
    proj_bc,
    decay_rate,
    skip_gain,
    w_out,
):
    rows = hidden.shape[0]
    width = w_in.shape[1]
    inner = w_in.shape[2] // 2
    tiles = inner // LANES
    length = 2 * rows
    padded = length + EDGE
    block = min(BLOCK, inner)
    seq_count = lax.axis_size("seq")
    ch_count = lax.axis_size("ch")
    chips = seq_count // 2
    chip = spot()[2]

    first, second = both_halves(hidden)
    channels = (STATE, inner)
    pairs = chips // 2
    (
        signal_w, taps, offset, proj_half, rate, skip, gain, embed, rim,
        bases, weigh, decay, keeps,
    ) = call(
        init_kernel,
        "init",
        [
            shaped((width, inner), bf16),
            shaped((CONV, inner)),
            shaped((1, inner)),
            shaped((2 * STATE, inner), bf16),
            shaped(channels),
            shaped((1, inner)),
            shaped((1, width)),
            shaped((4, width)),
            shaped((EDGE, hidden.shape[1]), bf16),
            shaped((rows + EDGE, LANES)),
            shaped((4 * 2 * STATE, rows)),
            shaped(channels),
            shaped((max(pairs, 1) + 1, SUBS, LANES)),
        ],
        [SCALARS] + [ANYWHERE] * 10,
        [pltpu.VMEM((seq_count, rows), jnp.int32), pltpu.SemaphoreType.DMA((10,))],
    )(
        edit_bounds.T,
        *(
            in_hbm(array)
            for array in (
                tokens.reshape(seq_count, rows),
                w_in,
                conv_w,
                conv_b[None, :],
                proj_bc,
                decay_rate,
                skip_gain[None, :],
                norm_gain[None, :],
                base_embed,
                hidden,
            )
        ),
    )
    rim_first, rim_second = rims(rim)
    drive = jnp.sqrt(-jnp.expm1(-2.0 * rate))
    normed = call(norm_kernel, "norm", shaped((rows + EDGE, width), bf16), [WHOLE] * 7)(
        first, second, rim_first, rim_second, bases, gain, embed
    )
    partner = swap(normed, "seq", 1)

    lined, c, bc, gate_w = call(
        signal_kernel,
        "signal",
        [
            shaped((2 * padded, width), bf16),
            shaped((STREAMS, tiles, length, LANES)),
            shaped((4 * 2 * STATE, rows)),
            shaped((width, inner), bf16),
        ],
        [WHOLE] * 6 + [ANYWHERE],
        [
            pltpu.VMEM((2 * STREAMS * block // LANES, padded, LANES), f32),
            pltpu.SemaphoreType.DMA,
        ],
        megabytes=6,
    )(normed, partner, signal_w, taps, offset, proj_half, in_hbm(w_in))
    bc = bc + swap(bc, "seq", 1)
    if ch_count == 2:
        bc_far = swap(bc, "ch", 1)
    else:
        bc, bc_far = lax.psum(bc, "ch"), jnp.zeros_like(bc)

    z = call(gate_kernel, "gate", shaped((STREAMS, length, inner), bf16), [WHOLE] * 2)(
        lined, gate_w
    )
    later = pl.BlockSpec(memory_space=pl.ANY)
    scaled, ends, wide = call(
        end_kernel,
        "ends",
        [
            shaped((4 * 2 * STATE, rows)),
            shaped((STREAMS,) + channels),
            shaped((STREAMS, length * STATE, LANES)),
        ],
        [WHOLE] * 6 + [later],
    )(bc, bc_far, weigh, c, decay, drive * keeps[0, 0:1, 0:1], z)

    def local(s, after):
        fetched = s == 1
        return call(
            functools.partial(local_kernel, s),
            "local",
            [shaped((length, inner)), shaped((length, CHUNK * STATE), bf16)]
            + [shaped((inner, width), bf16)] * fetched,
            [WHOLE] * 6 + [later] + [ANYWHERE] * fetched,
            [pltpu.VMEM((length * STATE, inner), bf16)] + [pltpu.SemaphoreType.DMA] * fetched,
            megabytes=12,
        )(scaled, wide, c, decay, drive.astype(bf16), skip, after, *[in_hbm(w_out)] * fetched)

    got = swap(ends.astype(bf16), "seq", 2)
    strides, powers, first_step, leads = call(
        factor_kernel,
        "factors",
        [
            shaped((2,) + channels),
            shaped((CHUNK * STATE, inner), bf16),
            shaped((2, STREAMS) + channels),
            shaped((max(pairs - 1, 1), STREAMS) + channels),
        ],
        [WHOLE] * 2 + [later],
    )(rate, keeps, scaled)
    y_f, readout_f = local(0, scaled)
    arrived = []
    if pairs > 1:
        sends = call(
            pair_kernel,
            "pairs",
            [shaped(channels, bf16)] * (pairs - 1),
            [WHOLE] * 3 + [later],
        )(ends, got, first_step, y_f)
        arrived = [swap(send, "seq", 4 * m) for m, send in enumerate(sends, 1)]
    y_b, readout_b, out_w = local(1, sends[0] if pairs > 1 else got)

    def finish(same, dtype):
        return call(
            functools.partial(finish_kernel, same),
            "finish",
            [shaped((rows, width // 2), dtype), shaped((STREAMS, rows, inner), bf16)],
            [WHOLE] * (10 + len(arrived)),
        )(powers, strides, got, leads, y_f, y_b, readout_f, readout_b, z, out_w, *arrived)

    def rest(gated, dtype, after):
        return call(
            rest_kernel, "rest", shaped((rows, width // 2), dtype), [WHOLE] * 2 + [later]
        )(gated, out_w, after)

    send, gated_far = finish(False, bf16)
    came = swap(send, "seq", 1)
    keep, gated_own = finish(True, f32)
    first = keep + came.astype(f32)
    sent = first.astype(bf16)
    if ch_count == 2:
        came = swap(sent, "ch", 1)
    second = swap(rest(gated_far, bf16, sent), "seq", 1)
    second = rest(gated_own, f32, sent) + second.astype(f32)
    if ch_count == 2:
        return (second + came.astype(f32)).astype(bf16)
    total = jnp.concatenate([first, second], axis=1)
    return lax.psum_scatter(total.astype(bf16), "ch", scatter_dimension=1, tiled=True)


def solution(mesh):
    placed = (
        P("seq", "ch"),
        P(),
        P(),
        P(),
        P(),
        P(None, None, "ch"),
        P(None, "ch"),
        P("ch"),
        P(None, "ch"),
        P(None, "ch"),
        P("ch"),
        P("ch", None),
    )
    return jax.shard_map(
        body, mesh=mesh, in_specs=placed, out_specs=P("seq", "ch"), check_vma=False
    )
```

time: 373 us -> 65.5 us (0.18)
  waiting for transfers between devices: 232 us -> 9.56 us
  other arithmetic: 50 us -> 1.59 us
  Pallas kernels: 0 us -> 32.1 us
  matrix products: 18.3 us -> 0 us
  local copies, waits for them, and re-layouts: 18.5 us -> 1.19 us
  between operations: 13.7 us -> 0.21 us
  starting transfers between devices: 31.8 us -> 20.7 us
  blocking collectives: 7.25 us -> 0 us
    all_gather x5 -> x0, waiting for transfers between devices: 145 us -> none  [the longest x4 130 us: carried_in(): gathered = jax.tree.map(lambda a: lax.all_gather(a, axis), part)]
    ppermute x9 -> x13, waiting for transfers between devices: 69.4 us -> 9.56 us  [the longest x11 9.55 us: swap(): return lax.ppermute(block, axis, [(i, i ^ apart) for i in range(count)])]
    pallas_call x0 -> x13, Pallas kernels: none -> 32.1 us  [the longest x2 10.4 us: local(): call(functools.partial(local_kernel, s), 'local', [shaped((length, inner)...]
    reduce_sum x42 -> x0, other arithmetic: 25.7 us -> none  [the longest x40 24.1 us: turn_step(): outputs.append(jnp.sum(r_block[row_index][:, :, None] * state, axis=1))]
    dot_general x4 -> x0, matrix products: 18.3 us -> none  [the longest x1 8.57 us: body(): lax.dot_general(stacked, w_in, (((1,), (1,)), ((), ())), preferred_elemen...]
    reduce_scatter x1 -> x0, waiting for transfers between devices: 15.6 us -> none  [body(): lax.psum_scatter(summed.astype(jnp.bfloat16), 'ch', scatter_dimension=1,...]
    ppermute x9 -> x13, starting transfers between devices: 31.6 us -> 20.7 us  [the longest x11 19.4 us: swap(): return lax.ppermute(block, axis, [(i, i ^ apart) for i in range(count)])]
    convert_element_type x21 -> x4, other arithmetic: 10.8 us -> 1.58 us  [the longest x1 0.81 us: body(): return (second + came.astype(f32)).astype(bf16)]
  transfers between devices with their start and end apart: 15 -> 13, of which waited for: 15 -> 4; matrix products, arithmetic and copies ran while one was open for 11% -> 2% of each run, Pallas kernels for 0% -> 29%
where the time goes in v2:
time: 65.5 us; the launch traced here: 65.4 us
  Pallas kernels  32.1 us (49%)
  starting transfers between devices  20.7 us (32%)
  waiting for transfers between devices  9.56 us (15%)
  other arithmetic  1.59 us (2%)
  local copies, waits for them, and re-layouts  1.19 us (2%)
    ppermute x11, starting transfers between devices, swap(): return lax.ppermute(block, axis, [(i, i ^ apart) for i in range(count)])  19.4 us
    pallas_call x2, Pallas kernels, local(): call(functools.partial(local_kernel, s), 'local', [shaped((length, inner)...  10.4 us
    ppermute x11, waiting for transfers between devices, swap(): return lax.ppermute(block, axis, [(i, i ^ apart) for i in range(count)])  9.55 us
    pallas_call x1, Pallas kernels, body(): call(end_kernel, 'ends', [shaped((4 * 2 * STATE, rows)), shaped((STREAMS,...  5.06 us
    pallas_call x1, Pallas kernels, body(): call(signal_kernel, 'signal', [shaped((2 * padded, width), bf16), shaped(...  4.42 us
    pallas_call x2, Pallas kernels, finish(): call(functools.partial(finish_kernel, same), 'finish', [shaped((rows, wid...  4.17 us
    pallas_call x1, Pallas kernels, body(): call(init_kernel, 'init', [shaped((width, inner), bf16), shaped((CONV, in...  3.03 us
    pallas_call x1, Pallas kernels, body(): call(gate_kernel, 'gate', shaped((STREAMS, length, inner), bf16), [WHOLE]...  2.33 us
  transfers between devices with their start and end apart: 13, of which 4 were waited for; matrix products, arithmetic and copies ran while one was open for 2% of the time, Pallas kernels for 29%

profile of v2, /device:TPU:0, one launch (start us, length us, event | category | flops | bytes accessed | tf_op | source)
XLA Modules:
  0.0 65.4 jit_solution(17978418049467885820)
XLA Ops:
  0.0 3.0 %collective-permute-start = (bf16[128,1024]{1,0:T(8,128)(2,1)}, bf16[128,1024]{1,0:T(8,128)(2,1)S(1)}, u32[]{:S(2)}, u32[]{:S(2)}) collective-permute-start(bf16[128,1024]{1,0:T(8,128)(2,1)} %own.1), channel_id=1, source_target_pairs={{0,1},{1,0},{2,3},{3,2},{4,5},{5,4},{6,7},{7,6},{8,9},{9,8},{10,11... | collective-permute-start | bytes 786440 | tf_op jit(solution)/shard_map/ppermute | solution.py:55
  3.0 0.7 %copy-done.1 = s32[8,2]{0,1:T(2,128)S(1)} copy-done((s32[8,2]{0,1:T(2,128)S(1)}, s32[8,2]{0,1:T(2,128)}, u32[]{:S(2)}) %copy-start.1) | copy-done | bytes 88
  3.6 3.0 %init.1 = (bf16[2048,1024]{1,0:T(8,128)(2,1)S(1)}, f32[4,1024]{1,0:T(4,128)S(1)}, f32[1,1024]{1,0:T(1,128)S(1)}, bf16[32,1024]{1,0:T(8,128)(2,1)S(1)}, f32[16,10...) custom-call(s32[2,8]{1,0:T(2,128)S(1)} %bitcast.6, ...), custom_call_target="tpu_custom_call" | custom-call | tf_op jit(solution)/shard_map/init/pallas_call | solution.py:565
  6.7 0.7 %collective-permute-start.2 = (bf16[16,1024]{1,0:T(8,128)(2,1)S(1)}, bf16[16,1024]{1,0:T(8,128)(2,1)S(1)}, u32[]{:S(2)}, u32[]{:S(2)}) collective-permute-start(bf16[16,1024]{1,0:T(8,128)(2,1)S(1)} %get-tuple-element.43), channel_id=1, source_target_pairs={{3,4},{2,5},{7,8},{6,9},{11,12},{10,13},{15,16},{14,17},{19,20},{1... | collective-permute-start | bytes 98312 | tf_op jit(solution)/shard_map/ppermute | solution.py:77
  7.4 0.7 %collective-permute-start.1 = (bf16[16,1024]{1,0:T(8,128)(2,1)S(1)}, bf16[16,1024]{1,0:T(8,128)(2,1)S(1)}, u32[]{:S(2)}, u32[]{:S(2)}) collective-permute-start(bf16[16,1024]{1,0:T(8,128)(2,1)S(1)} %get-tuple-element.43), channel_id=1, source_target_pairs={{2,4},{3,5},{6,8},{7,9},{10,12},{11,13},{14,16},{15,17},{18,20},{1... | collective-permute-start | bytes 98312 | tf_op jit(solution)/shard_map/ppermute | solution.py:77
  8.1 1.4 %collective-permute-done.far = bf16[128,1024]{1,0:T(8,128)(2,1)S(1)} collective-permute-done((bf16[128,1024]{1,0:T(8,128)(2,1)}, bf16[128,1024]{1,0:T(8,128)(2,1)S(1)}, u32[]{:S(2)}, u32[]{:S(2)}) %collective-permute-start) | collective-permute-done | bytes 262176 | tf_op jit(solution)/shard_map/ppermute | solution.py:55
  9.5 0.6 norm.1.own
  10.1 6.0 %collective-permute-start.3 = (bf16[144,2048]{1,0:T(8,128)(2,1)S(1)}, bf16[144,2048]{1,0:T(8,128)(2,1)S(1)}, u32[]{:S(2)}, u32[]{:S(2)}) collective-permute-start(bf16[144,2048]{1,0:T(8,128)(2,1)S(1)} %norm.1.own), channel_id=1, source_target_pairs={{0,2},{2,0},{4,6},{6,4},{8,10},{10,8},{12,14},{14,12},{16,18},{18,... | collective-permute-start | bytes 1769480 | tf_op jit(solution)/shard_map/ppermute | solution.py:55
  16.1 1.6 %collective-permute-done.3.other = bf16[144,2048]{1,0:T(8,128)(2,1)S(1)} collective-permute-done((bf16[144,2048]{1,0:T(8,128)(2,1)S(1)}, bf16[144,2048]{1,0:T(8,128)(2,1)S(1)}, u32[]{:S(2)}, u32[]{:S(2)}) %collective-permute-start.3) | collective-permute-done | bytes 589856 | tf_op jit(solution)/shard_map/ppermute | solution.py:55
  17.7 4.4 %signal.1 = (bf16[544,2048]{1,0:T(8,128)(2,1)S(1)}, f32[2,8,256,128]{3,2,1,0:T(8,128)S(1)}, f32[128,128]{1,0:T(8,128)S(1)}, bf16[2048,1024]{1,0:T(8,128)(2,1)S(1)}) custom-call(bf16[144,2048]{1,0:T(8,128)(2,1)S(1)} %norm.1.own, bf16[144,2048]{1,0:T(8,128)(2,1)S(1)} %collective-permute-done.3.other, bf16[2048,1024]{1,0:T(8,128)(2,1)S(1)} %get-tuple-element.47.w, ...), custom_call_target="tpu_custom_call" | custom-call | tf_op jit(solution)/shard_map/signal/pallas_call | solution.py:610
  22.1 0.4 collective-permute-start.4
  22.6 0.5 slice.3
  23.1 0.4 collective-permute-done.4
  23.5 1.6 %collective-permute-start.5 = (f32[128,128]{1,0:T(8,128)S(1)}, f32[128,128]{1,0:T(8,128)S(1)}, u32[]{:S(2)}, u32[]{:S(2)}) collective-permute-start(f32[128,128]{1,0:T(8,128)S(1)} %add.12.bc_own), channel_id=1, source_target_pairs={{0,1},{1,0},{2,3},{3,2},{4,5},{5,4},{6,7},{7,6},{8,9},{9,8},{10,11... | collective-permute-start | bytes 196616 | tf_op jit(solution)/shard_map/ppermute | solution.py:55
  25.1 0.7 %fusion = (bf16[16,1024]{1,0:T(8,128)(2,1)S(1)}, f32[16,1024]{1,0:T(8,128)S(1)}) fusion(f32[16,1024]{1,0:T(8,128)S(1)} %get-tuple-element.41.rate, f32[]{:T(128)} %bitcast.5), kind=kLoop, calls=%fused_computation.3 | loop fusion | flops 65536 | bytes 163844 | tf_op jit(solution)/shard_map/convert_element_type | solution.py:657
  25.8 2.3 %gate.1.after_z.z = bf16[2,256,1024]{2,1,0:T(8,128)(2,1)S(1)} custom-call(bf16[544,2048]{1,0:T(8,128)(2,1)S(1)} %get-tuple-element.55.lined, bf16[2048,1024]{1,0:T(8,128)(2,1)S(1)} %get-tuple-element.56.w), custom_call_target="tpu_custom_call" | custom-call | tf_op jit(solution)/shard_map/gate/pallas_call | solution.py:632
  28.1 5.1 %ends.1 = (f32[128,128]{1,0:T(8,128)S(1)}, f32[2,16,1024]{2,1,0:T(8,128)S(1)}, f32[2,4096,128]{2,1,0:T(8,128)S(1)}) custom-call(f32[128,128]{1,0:T(8,128)S(1)} %add.12.bc_own, f32[128,128]{1,0:T(8,128)S(1)} %collective-permute-done.5.bc_far, f32[128,128]{1,0:T(8,128)S(1)} %get-tuple-element.52.weigh, f32[2,8,256,128]{3,2,1,0:T(8,128)S(1)} %get-tuple-element.53.c, ...), custom_call_target="tpu_custom_call" | custom-call | tf_op jit(solution)/shard_map/ends/pallas_call | solution.py:636
  33.2 2.5 %collective-permute-start.6 = (bf16[2,16,1024]{2,1,0:T(8,128)(2,1)S(1)}, bf16[2,16,1024]{2,1,0:T(8,128)(2,1)S(1)}, u32[]{:S(2)}, u32[]{:S(2)}) collective-permute-start(bf16[2,16,1024]{2,1,0:T(8,128)(2,1)S(1)} %convert_element_type.22), channel_id=1, source_target_pairs={{0,4},{2,6},{4,0},{6,2},{8,12},{10,14},{12,8},{14,10},{16,20},{18,... | collective-permute-start | bytes 196616 | tf_op jit(solution)/shard_map/ppermute | solution.py:55
  35.7 0.2 factors.1
  35.9 5.2 %local.2 = (f32[256,1024]{1,0:T(8,128)S(1)}, bf16[256,256]{1,0:T(8,128)(2,1)S(1)}) custom-call(f32[128,128]{1,0:T(8,128)S(1)} %get-tuple-element.57.after_ends.bc.after_got, f32[2,4096,128]{2,1,0:T(8,128)S(1)} %get-tuple-element.62.wide, f32[2,8,256,128]{3,2,1,0:T(8,128)S(1)} %get-tuple-element.53.c, f32[16,1024]{1,0:T(8,128)S(1)} %get-tuple-element.54.decay, ...), custom_call_target="tpu_custom_call" | custom-call | tf_op jit(solution)/shard_map/local/pallas_call | solution.py:649
  41.2 2.6 %collective-permute-start.8 = (bf16[16,1024]{1,0:T(8,128)(2,1)S(1)}, bf16[16,1024]{1,0:T(8,128)(2,1)S(1)}, u32[]{:S(2)}, u32[]{:S(2)}) collective-permute-start(bf16[16,1024]{1,0:T(8,128)(2,1)S(1)} %get-tuple-element.71), channel_id=1, source_target_pairs={{0,16},{2,18},{4,20},{6,22},{8,24},{10,26},{12,28},{14,30},{16,0},... | collective-permute-start | bytes 98312 | tf_op jit(solution)/shard_map/ppermute | solution.py:55
  43.8 1.4 %collective-permute-start.9 = (bf16[16,1024]{1,0:T(8,128)(2,1)S(1)}, bf16[16,1024]{1,0:T(8,128)(2,1)S(1)}, u32[]{:S(2)}, u32[]{:S(2)}) collective-permute-start(bf16[16,1024]{1,0:T(8,128)(2,1)S(1)} %get-tuple-element.72), channel_id=1, source_target_pairs={{0,24},{2,26},{4,28},{6,30},{8,16},{10,18},{12,20},{14,22},{16,8},... | collective-permute-start | bytes 98312 | tf_op jit(solution)/shard_map/ppermute | solution.py:55
  45.2 5.2 %local.3 = (f32[256,1024]{1,0:T(8,128)S(1)}, bf16[256,256]{1,0:T(8,128)(2,1)S(1)}, bf16[1024,2048]{1,0:T(8,128)(2,1)S(1)}) custom-call(f32[128,128]{1,0:T(8,128)S(1)} %get-tuple-element.57.after_ends.bc.after_got, f32[2,4096,128]{2,1,0:T(8,128)S(1)} %get-tuple-element.62.wide, f32[2,8,256,128]{3,2,1,0:T(8,128)S(1)} %get-tuple-element.53.c, ...), custom_call_target="tpu_custom_call" | custom-call | tf_op jit(solution)/shard_map/local/pallas_call | solution.py:649
  50.4 2.1 %finish.3 = (bf16[128,1024]{1,0:T(8,128)(2,1)S(1)}, bf16[2,128,1024]{2,1,0:T(8,128)(2,1)S(1)}) custom-call(bf16[256,1024]{1,0:T(8,128)(2,1)S(1)} %get-tuple-element.58.powers, f32[2,16,1024]{2,1,0:T(8,128)S(1)} %get-tuple-element.59.strides, bf16[2,16,1024]{2,1,0:T(8,128)(2,1)S(1)} %collective-permute-done.6.got, ...), custom_call_target="tpu_custom_call" | custom-call | tf_op jit(solution)/shard_map/finish/pallas_call | solution.py:684
  52.5 0.1 collective-permute-start.10
  52.6 2.1 %finish.2 = (f32[128,1024]{1,0:T(8,128)S(1)}, bf16[2,128,1024]{2,1,0:T(8,128)(2,1)S(1)}) custom-call(bf16[256,1024]{1,0:T(8,128)(2,1)S(1)} %get-tuple-element.58.powers, f32[2,16,1024]{2,1,0:T(8,128)S(1)} %get-tuple-element.59.strides, bf16[2,16,1024]{2,1,0:T(8,128)(2,1)S(1)} %collective-permute-done.6.got, f32[3,2,16,1024]{3,2,1,0:T(8,128)S(1)} %get-tuple-element.61.leads, ...), custom_call_target="tpu_custom_call" | custom-call | tf_op jit(solution)/shard_map/finish/pallas_call | solution.py:684
  54.8 0.9 %rest.3 = bf16[128,1024]{1,0:T(8,128)(2,1)S(1)} custom-call(bf16[2,128,1024]{2,1,0:T(8,128)(2,1)S(1)} %get-tuple-element.76.gated, bf16[1024,2048]{1,0:T(8,128)(2,1)S(1)} %get-tuple-element.70.w, bf16[128,1024]{1,0:T(8,128)(2,1)S(1)} %add_convert_fusion.1.after_first), custom_call_target="tpu_custom_call" | custom-call | tf_op jit(solution)/shard_map/rest/pallas_call | solution.py:692
  55.7 0.6 collective-permute-start.11
  56.3 1.3 %collective-permute-start.12 = (bf16[128,1024]{1,0:T(8,128)(2,1)S(1)}, bf16[128,1024]{1,0:T(8,128)(2,1)S(1)}, u32[]{:S(2)}, u32[]{:S(2)}) collective-permute-start(bf16[128,1024]{1,0:T(8,128)(2,1)S(1)} %add_convert_fusion.1.after_first), channel_id=1, source_target_pairs={{0,1},{1,0},{2,3},{3,2},{4,5},{5,4},{6,7},{7,6},{8,9},{9,8},{10,11... | collective-permute-start | bytes 786440 | tf_op jit(solution)/shard_map/ppermute | solution.py:55
  57.6 0.9 %rest.2 = f32[128,1024]{1,0:T(8,128)S(1)} custom-call(bf16[2,128,1024]{2,1,0:T(8,128)(2,1)S(1)} %get-tuple-element.73.gated, bf16[1024,2048]{1,0:T(8,128)(2,1)S(1)} %get-tuple-element.70.w, bf16[128,1024]{1,0:T(8,128)(2,1)S(1)} %add_convert_fusion.1.after_first), custom_call_target="tpu_custom_call" | custom-call | tf_op jit(solution)/shard_map/rest/pallas_call | solution.py:692
  58.5 6.1 %collective-permute-done.12 = bf16[128,1024]{1,0:T(8,128)(2,1)S(1)} collective-permute-done((bf16[128,1024]{1,0:T(8,128)(2,1)S(1)}, bf16[128,1024]{1,0:T(8,128)(2,1)S(1)}, u32[]{:S(2)}, u32[]{:S(2)}) %collective-permute-start.12) | collective-permute-done | bytes 262176 | tf_op jit(solution)/shard_map/ppermute | solution.py:55
  64.5 0.8 %add_convert_fusion = bf16[128,1024]{1,0:T(8,128)(2,1)} fusion(bf16[128,1024]{1,0:T(8,128)(2,1)S(1)} %collective-permute-done.12, f32[128,1024]{1,0:T(8,128)S(1)} %rest.2, bf16[128,1024]{1,0:T(8,128)(2,1)S(1)} %collective-permute-done.11), kind=kLoop, calls=%fused_computation | loop fusion | flops 655360 | bytes 1310720 | tf_op jit(solution)/shard_map/convert_element_type | solution.py:706
  (17 shorter events, 0.2 us)
Async XLA Ops:
  0.0 9.5 %collective-permute-start = (bf16[128,1024]{1,0:T(8,128)(2,1)}, bf16[128,1024]{1,0:T(8,128)(2,1)S(1)}, u32[]{:S(2)}, u32[]{:S(2)}) collective-permute-start(bf16[128,1024]{1,0:T(8,128)(2,1)} %own.1), channel_id=1, source_target_pairs={{0,1},{1,0},{2,3},{3,2},{4,5},{5,4},{6,7},{7,6},{8,9},{9,8},{10,11... | collective-permute-start | bytes 786440 | tf_op jit(solution)/shard_map/ppermute | solution.py:55
  3.0 0.7 %copy-start.1 = (s32[8,2]{0,1:T(2,128)S(1)}, s32[8,2]{0,1:T(2,128)}, u32[]{:S(2)}) copy-start(s32[8,2]{0,1:T(2,128)} %param.14) | copy-start | bytes 196
  3.6 5.8 %copy-start = (bf16[128,1024]{1,0:T(8,128)(2,1)S(1)}, bf16[128,1024]{1,0:T(8,128)(2,1)}, u32[]{:S(2)}) copy-start(bf16[128,1024]{1,0:T(8,128)(2,1)} %own.1) | copy-start | bytes 786436
  6.7 1.3 %collective-permute-start.2 = (bf16[16,1024]{1,0:T(8,128)(2,1)S(1)}, bf16[16,1024]{1,0:T(8,128)(2,1)S(1)}, u32[]{:S(2)}, u32[]{:S(2)}) collective-permute-start(bf16[16,1024]{1,0:T(8,128)(2,1)S(1)} %get-tuple-element.43), channel_id=1, source_target_pairs={{3,4},{2,5},{7,8},{6,9},{11,12},{10,13},{15,16},{14,17},{19,20},{1... | collective-permute-start | bytes 98312 | tf_op jit(solution)/shard_map/ppermute | solution.py:77
  7.4 0.7 %collective-permute-start.1 = (bf16[16,1024]{1,0:T(8,128)(2,1)S(1)}, bf16[16,1024]{1,0:T(8,128)(2,1)S(1)}, u32[]{:S(2)}, u32[]{:S(2)}) collective-permute-start(bf16[16,1024]{1,0:T(8,128)(2,1)S(1)} %get-tuple-element.43), channel_id=1, source_target_pairs={{2,4},{3,5},{6,8},{7,9},{10,12},{11,13},{14,16},{15,17},{18,20},{1... | collective-permute-start | bytes 98312 | tf_op jit(solution)/shard_map/ppermute | solution.py:77
  10.1 7.6 %collective-permute-start.3 = (bf16[144,2048]{1,0:T(8,128)(2,1)S(1)}, bf16[144,2048]{1,0:T(8,128)(2,1)S(1)}, u32[]{:S(2)}, u32[]{:S(2)}) collective-permute-start(bf16[144,2048]{1,0:T(8,128)(2,1)S(1)} %norm.1.own), channel_id=1, source_target_pairs={{0,2},{2,0},{4,6},{6,4},{8,10},{10,8},{12,14},{14,12},{16,18},{18,... | collective-permute-start | bytes 1769480 | tf_op jit(solution)/shard_map/ppermute | solution.py:55
  22.1 1.3 %collective-permute-start.4 = (f32[128,128]{1,0:T(8,128)S(1)}, f32[128,128]{1,0:T(8,128)S(1)}, u32[]{:S(2)}, u32[]{:S(2)}) collective-permute-start(f32[128,128]{1,0:T(8,128)S(1)} %get-tuple-element.51), channel_id=1, source_target_pairs={{0,2},{2,0},{4,6},{6,4},{8,10},{10,8},{12,14},{14,12},{16,18},{18,... | collective-permute-start | bytes 196616 | tf_op jit(solution)/shard_map/ppermute | solution.py:55
  23.5 4.6 %collective-permute-start.5 = (f32[128,128]{1,0:T(8,128)S(1)}, f32[128,128]{1,0:T(8,128)S(1)}, u32[]{:S(2)}, u32[]{:S(2)}) collective-permute-start(f32[128,128]{1,0:T(8,128)S(1)} %add.12.bc_own), channel_id=1, source_target_pairs={{0,1},{1,0},{2,3},{3,2},{4,5},{5,4},{6,7},{7,6},{8,9},{9,8},{10,11... | collective-permute-start | bytes 196616 | tf_op jit(solution)/shard_map/ppermute | solution.py:55
  33.2 7.9 %collective-permute-start.6 = (bf16[2,16,1024]{2,1,0:T(8,128)(2,1)S(1)}, bf16[2,16,1024]{2,1,0:T(8,128)(2,1)S(1)}, u32[]{:S(2)}, u32[]{:S(2)}) collective-permute-start(bf16[2,16,1024]{2,1,0:T(8,128)(2,1)S(1)} %convert_element_type.22), channel_id=1, source_target_pairs={{0,4},{2,6},{4,0},{6,2},{8,12},{10,14},{12,8},{14,10},{16,20},{18,... | collective-permute-start | bytes 196616 | tf_op jit(solution)/shard_map/ppermute | solution.py:55
  41.2 9.2 %collective-permute-start.8 = (bf16[16,1024]{1,0:T(8,128)(2,1)S(1)}, bf16[16,1024]{1,0:T(8,128)(2,1)S(1)}, u32[]{:S(2)}, u32[]{:S(2)}) collective-permute-start(bf16[16,1024]{1,0:T(8,128)(2,1)S(1)} %get-tuple-element.71), channel_id=1, source_target_pairs={{0,16},{2,18},{4,20},{6,22},{8,24},{10,26},{12,28},{14,30},{16,0},... | collective-permute-start | bytes 98312 | tf_op jit(solution)/shard_map/ppermute | solution.py:55
  43.8 6.6 %collective-permute-start.9 = (bf16[16,1024]{1,0:T(8,128)(2,1)S(1)}, bf16[16,1024]{1,0:T(8,128)(2,1)S(1)}, u32[]{:S(2)}, u32[]{:S(2)}) collective-permute-start(bf16[16,1024]{1,0:T(8,128)(2,1)S(1)} %get-tuple-element.72), channel_id=1, source_target_pairs={{0,24},{2,26},{4,28},{6,30},{8,16},{10,18},{12,20},{14,22},{16,8},... | collective-permute-start | bytes 98312 | tf_op jit(solution)/shard_map/ppermute | solution.py:55
  45.2 5.2 %collective-permute-start.7 = (bf16[16,1024]{1,0:T(8,128)(2,1)S(1)}, bf16[16,1024]{1,0:T(8,128)(2,1)S(1)}, u32[]{:S(2)}, u32[]{:S(2)}) collective-permute-start(bf16[16,1024]{1,0:T(8,128)(2,1)S(1)} %get-tuple-element.66.after_got), channel_id=1, source_target_pairs={{0,8},{2,10},{4,12},{6,14},{8,0},{10,2},{12,4},{14,6},{16,24},{18,... | collective-permute-start | bytes 98312 | tf_op jit(solution)/shard_map/ppermute | solution.py:55
  52.5 2.2 %collective-permute-start.10 = (bf16[128,1024]{1,0:T(8,128)(2,1)S(1)}, bf16[128,1024]{1,0:T(8,128)(2,1)S(1)}, u32[]{:S(2)}, u32[]{:S(2)}) collective-permute-start(bf16[128,1024]{1,0:T(8,128)(2,1)S(1)} %get-tuple-element.75), channel_id=1, source_target_pairs={{0,2},{2,0},{4,6},{6,4},{8,10},{10,8},{12,14},{14,12},{16,18},{18,... | collective-permute-start | bytes 786440 | tf_op jit(solution)/shard_map/ppermute | solution.py:55
  55.7 2.8 %collective-permute-start.11 = (bf16[128,1024]{1,0:T(8,128)(2,1)S(1)}, bf16[128,1024]{1,0:T(8,128)(2,1)S(1)}, u32[]{:S(2)}, u32[]{:S(2)}) collective-permute-start(bf16[128,1024]{1,0:T(8,128)(2,1)S(1)} %rest.3), channel_id=1, source_target_pairs={{0,2},{2,0},{4,6},{6,4},{8,10},{10,8},{12,14},{14,12},{16,18},{18,... | collective-permute-start | bytes 786440 | tf_op jit(solution)/shard_map/ppermute | solution.py:55
  56.3 8.3 %collective-permute-start.12 = (bf16[128,1024]{1,0:T(8,128)(2,1)S(1)}, bf16[128,1024]{1,0:T(8,128)(2,1)S(1)}, u32[]{:S(2)}, u32[]{:S(2)}) collective-permute-start(bf16[128,1024]{1,0:T(8,128)(2,1)S(1)} %add_convert_fusion.1.after_first), channel_id=1, source_target_pairs={{0,1},{1,0},{2,3},{3,2},{4,5},{5,4},{6,7},{7,6},{8,9},{9,8},{10,11... | collective-permute-start | bytes 786440 | tf_op jit(solution)/shard_map/ppermute | solution.py:55

commit v3 on v2

--- a/solution.py
+++ b/solution.py
@@ -83,6 +83,18 @@
     )
 
 
+def cut_kernel(hidden, own, rim, sems):
+    low = pl.multiple_of(spot()[1] * (own.shape[0] - EDGE), EDGE)
+    copies = [
+        pltpu.make_async_copy(hidden, own, sems.at[0]),
+        pltpu.make_async_copy(hidden.at[pl.ds(low, EDGE), :], rim, sems.at[1]),
+    ]
+    for copy in copies:
+        copy.start()
+    for copy in copies:
+        copy.wait()
+
+
 def between(chip, m):
     pair = chip >> 1
     other = pair ^ m
@@ -91,8 +103,8 @@
 
 
 def init_kernel(
-    bounds, tokens_all, w_in, conv_w, conv_b, proj, rate_all, skip, gain_all, embed_all, hidden,
-    signal_w, taps, offset, proj_half, rate, skip_half, norm_gain, embed, rim,
+    bounds, tokens_all, w_in, conv_w, conv_b, proj, rate_all, skip, gain_all, embed_all, after,
+    signal_w, taps, offset, proj_half, rate, skip_half, norm_gain, embed,
     bases, weigh, decay, keeps, tokens, sems,
 ):
     place, core, chip = spot()
@@ -113,10 +125,6 @@
                 (conv_b.at[:, mine], offset),
                 (proj.at[:, mine], proj_half),
                 (skip.at[:, mine], skip_half),
-                (
-                    hidden.at[pl.ds(pl.multiple_of(core * (rows - EDGE), EDGE), EDGE), :],
-                    rim,
-                ),
                 (w_in.at[0, :, mine], signal_w),
             )
         )
@@ -322,15 +330,12 @@
 
 def spread(bc, wide, stream):
     rows = bc.shape[1]
-    ones = jnp.ones((2 * rows, LANES), bf16)
-    lanes = lax.broadcasted_iota(jnp.int32, (STATE, 2 * rows), 1) & (rows - 1)
+    ones = jnp.ones((rows, LANES), bf16)
+    lanes = lax.broadcasted_iota(jnp.int32, (STATE, rows), 1)
     group = 8
     for half in range(HALVES):
         first = 2 * STATE * (2 * half + stream)
-        exact = bc[first : first + STATE, :]
-        high = exact.astype(bf16)
-        low = (exact - high.astype(f32)).astype(bf16)
-        entries = jnp.concatenate([high, low], axis=1).astype(f32)
+        entries = bc[first : first + STATE, :]
         for j in range(0, rows, group):
             alone = jnp.concatenate(
                 [jnp.where(lanes == j + i, entries, 0.0).astype(bf16) for i in range(group)], axis=0
@@ -341,7 +346,14 @@
             )
 
 
-def end_kernel(bc_own, bc_far, weigh, c, decay, end_gain, after_z, bc_out, end_out, wide):
+def end_kernel(
+    bc_own, bc_far, weigh, c, decay, drive, keeps, after_z, w,
+    bc_out, end_out, starts, w_out, wide, sem,
+):
+    inner = w_out.shape[0]
+    mine = pl.ds(pl.multiple_of(spot()[1] * inner, inner), inner)
+    fetch = pltpu.make_async_copy(w.at[mine, :], w_out, sem)
+    fetch.start()
     rows = bc_own.shape[1]
     length = 2 * rows
     count = c.shape[1]
@@ -350,86 +362,94 @@
         spread(bc_out, wide, s)
     a = tiles_of(decay, count)
 
-    def one(j, state):
-        after = []
+    def chunk(n, state):
         for s in range(STREAMS):
-            t0 = j if s == 0 else length - 1 - j
-            low = pl.multiple_of(t0 * STATE, STATE)
-            b = [wide[s, pl.ds(low + h * SUBS, SUBS), :] for h in range(2)]
             for t in range(count):
-                x = c[s, t, pl.ds(t0, 1), :]
                 for h in range(2):
-                    i = 2 * t + h
-                    after.append(a[i] * state[s * 2 * count + i] + b[h] * x)
-        return tuple(after)
+                    sub = slice(h * SUBS, (h + 1) * SUBS)
+                    starts[s, n, sub, tile(t)] = (
+                        state[s * 2 * count + 2 * t + h] * drive[sub, tile(t)]
+                    )
+        for j in range(CHUNK):
+            after = []
+            for s in range(STREAMS):
+                t0 = n * CHUNK + j if s == 0 else length - 1 - n * CHUNK - j
+                low = pl.multiple_of(t0 * STATE, STATE)
+                b = [wide[s, pl.ds(low + h * SUBS, SUBS), :] for h in range(2)]
+                for t in range(count):
+                    x = c[s, t, pl.ds(t0, 1), :]
+                    for h in range(2):
+                        i = 2 * t + h
+                        after.append(a[i] * state[s * 2 * count + i] + b[h] * x)
+            state = tuple(after)
+        return state
 
     zero = jnp.zeros((SUBS, LANES), f32)
-    state = lax.fori_loop(0, length, one, (zero,) * (STREAMS * 2 * count), unroll=8)
+    state = lax.fori_loop(0, length // CHUNK, chunk, (zero,) * (STREAMS * 2 * count))
     for s in range(STREAMS):
         for t in range(count):
             for h in range(2):
                 sub = slice(h * SUBS, (h + 1) * SUBS)
-                end_out[s, sub, tile(t)] = state[s * 2 * count + 2 * t + h] * end_gain[sub, tile(t)]
-
-
-def local_kernel(stream, bc, wide, c, decay, drive, skip, after_got, *rest):
-    if stream == 1:
-        w_out, y_out, readout, out_w, driven, sem = rest
-        inner = decay.shape[1]
-        mine = pl.ds(pl.multiple_of(spot()[1] * inner, inner), inner)
-        fetch = pltpu.make_async_copy(w_out.at[mine, :], out_w, sem)
-        fetch.start()
-    else:
-        y_out, readout, driven = rest
+                end_out[s, sub, tile(t)] = (
+                    state[s * 2 * count + 2 * t + h] * drive[sub, tile(t)] * keeps[0, 0:1, :]
+                )
+    fetch.wait()
+
+
+def local_kernel(
+    stream, bc, c, decay, drive, skip, after, y_out, readout, lined, c_lined, y_lined
+):
     rows = bc.shape[1]
     length = 2 * rows
     count = c.shape[1]
     span = CHUNK * STATE
-    turned = bc[...].T.astype(bf16)
+    places = length // CHUNK
+    turned = bc[...].T
+    r = lax.broadcasted_iota(jnp.int32, (rows, span), 0)
+    q = lax.broadcasted_iota(jnp.int32, (rows, span), 1)
+    step = r & (CHUNK - 1) if stream == 0 else CHUNK - 1 - (r & (CHUNK - 1))
     for half in range(HALVES):
-        r = lax.broadcasted_iota(jnp.int32, (rows, span), 0)
-        q = lax.broadcasted_iota(jnp.int32, (rows, span), 1)
-        first = 2 * STATE * (2 * half + stream) + STATE
-        pick = jnp.where(r == first + (q & (STATE - 1)), 1.0, 0.0).astype(bf16)
-        picked = jnp.dot(turned, pick, preferred_element_type=f32)
-        step = r & (CHUNK - 1) if stream == 0 else CHUNK - 1 - (r & (CHUNK - 1))
+        column = 2 * STATE * (2 * half + stream)
+        pick = jnp.where(r == column + STATE + (q & (STATE - 1)), 1.0, 0.0).astype(bf16)
+        picked = jnp.dot(turned.astype(bf16), pick, preferred_element_type=f32)
         readout[half * rows : (half + 1) * rows, :] = jnp.where(
             q // STATE == step, picked, 0.0
         ).astype(bf16)
-    a = tiles_of(decay, count)
-
-    def chunks(n, state):
-        state = list(state)
-        base = n * CHUNK if stream == 0 else length - (n + 1) * CHUNK
-        base = pl.multiple_of(base, CHUNK)
-        low = pl.multiple_of(base * STATE, span)
-        to = pl.multiple_of(n * span, span)
-        for j in range(CHUNK):
-            i = j if stream == 0 else CHUNK - 1 - j
-            b = [wide[stream, pl.ds(low + i * STATE + h * SUBS, SUBS), :] for h in range(2)]
-            for t in range(count):
-                x = c[stream, t, pl.ds(base + i, 1), :]
-                for h in range(2):
-                    m = 2 * t + h
-                    state[m] = a[m] * state[m] + b[h] * x
-                both = jnp.concatenate([state[2 * t], state[2 * t + 1]], axis=0)
-                driven[pl.ds(to + j * STATE, STATE), tile(t)] = (
-                    both.astype(bf16) * drive[:, tile(t)]
-                )
-        return tuple(state)
-
-    zero = jnp.zeros((SUBS, LANES), f32)
-    lax.fori_loop(0, length // CHUNK, chunks, (zero,) * (2 * count))
-    for n in range(length // CHUNK):
-        base = n * CHUNK if stream == 0 else length - (n + 1) * CHUNK
-        at = slice(base, base + CHUNK)
-        y = jnp.dot(
-            readout[at, :], driven[n * span : (n + 1) * span, :], preferred_element_type=f32
+        lined[0, half * rows : (half + 1) * rows, :] = (
+            turned if column == 0 else pltpu.roll(turned, LANES - column, 1)
         )
+    for j in range(CHUNK):
+        to = slice(j * places, (j + 1) * places)
+        lined[1, to, :] = lined[0, pl.ds(j, places, stride=CHUNK), :]
         for t in range(count):
-            y_out[at, tile(t)] = y[:, tile(t)] + skip[0:1, tile(t)] * c[stream, t, at, :]
-    if stream == 1:
-        fetch.wait()
+            c_lined[t, to, :] = c[stream, t, pl.ds(j, places, stride=CHUNK), :]
+    inputs = lined[1]
+    outputs = pltpu.roll(inputs, LANES - STATE, 1)
+    block = min(2, count)
+    for low in range(0, count, block):
+        wide = slice(low * LANES, (low + block) * LANES)
+        reach = drive[:, wide]
+        for lag in range(CHUNK):
+            shift = lag * places
+            near, far = slice(shift, length), slice(0, length - shift)
+            if stream == 1:
+                near, far = far, near
+            left = (outputs[near] * inputs[far])[:, :STATE].astype(bf16)
+            found = jnp.dot(left, reach.astype(bf16), preferred_element_type=f32)
+            for t in range(block):
+                part = found[:, tile(t)]
+                if lag == 0:
+                    part = part + skip[0:1, tile(low + t)]
+                part = part * c_lined[low + t, far, :]
+                if lag == 0:
+                    y_lined[low + t, near, :] = part
+                else:
+                    y_lined[low + t, near, :] += part
+            reach = reach * decay[:, wide]
+    for j in range(CHUNK):
+        at = slice(j * places, (j + 1) * places)
+        for t in range(count):
+            y_out[t, pl.ds(j, places, stride=CHUNK), :] = y_lined[t, at, :]
 
 
 def factor_kernel(rate, keeps, after_ends, strides, powers, first_step, leads):
@@ -495,9 +515,12 @@
 
 
 def finish_kernel(
-    same, powers, strides, got, leads, y_f, y_b, readout_f, readout_b, z, w, *rest
+    same, powers, strides, got, leads, starts, y_f, y_b, readout_f, readout_b, z, w, *rest
 ):
-    *arrived, out, gated = rest
+    if same:
+        *arrived, out, gated = rest
+    else:
+        *arrived, out, out_rest, gated = rest
     _, core, chip = spot()
     rows = out.shape[0]
     inner = w.shape[0]
@@ -510,20 +533,26 @@
         state = got[s].astype(f32) * jnp.where(chip & 1 == 1 - s, 1.0, 0.0)
         for m, part in enumerate(arrived):
             state = state + part[...].astype(f32) * leads[m, s]
-        state = state * jnp.where(half == 1 - s, strides[1], 1.0)
+        late = half == 1 - s
+        state = state * jnp.where(late, strides[1], 1.0)
+        first = jnp.where(late, rows // CHUNK, 0)
         for q in range(rows // CHUNK):
             row = q * CHUNK if s == 0 else rows - (q + 1) * CHUNK
             at = pl.ds(pl.multiple_of(base + row, CHUNK), CHUNK)
-            carried = powers[...].reshape(CHUNK, STATE, inner) * state.astype(bf16)[None]
+            begin = (state + starts[s, first + q]).astype(bf16)
+            carried = powers[...].reshape(CHUNK, STATE, inner) * begin[None]
             state = state * strides[0]
             y = jnp.dot(
                 readouts[s][at, :], carried.reshape(span, inner), preferred_element_type=f32
             )
-            y = y + local[s][at, :]
-            gated[s, row : row + CHUNK, :] = (
-                y * jax.nn.silu(z[s, at, :].astype(f32))
-            ).astype(bf16)
+            for t in range(inner // LANES):
+                gated[s, row : row + CHUNK, tile(t)] = (
+                    (y[:, tile(t)] + local[s][t, at, :])
+                    * jax.nn.silu(z[s, at, tile(t)].astype(f32))
+                ).astype(bf16)
     columns(gated, w, out, part_of(False))
+    if not same:
+        columns(gated, w, out_rest, part_of(True))
 
 
 def rest_kernel(gated, w, after_first, out):
@@ -556,11 +585,20 @@
     chips = seq_count // 2
     chip = spot()[2]
 
-    first, second = both_halves(hidden)
+    own, rim = call(
+        cut_kernel,
+        "cut",
+        [shaped(hidden.shape, bf16), shaped((EDGE, hidden.shape[1]), bf16)],
+        [ANYWHERE],
+        [pltpu.SemaphoreType.DMA((2,))],
+    )(in_hbm(hidden))
+    later = pl.BlockSpec(memory_space=pl.ANY)
+    rim_first, rim_second = rims(rim)
+    first, second = both_halves(own)
     channels = (STATE, inner)
     pairs = chips // 2
     (
-        signal_w, taps, offset, proj_half, rate, skip, gain, embed, rim,
+        signal_w, taps, offset, proj_half, rate, skip, gain, embed,
         bases, weigh, decay, keeps,
     ) = call(
         init_kernel,
@@ -574,14 +612,13 @@
             shaped((1, inner)),
             shaped((1, width)),
             shaped((4, width)),
-            shaped((EDGE, hidden.shape[1]), bf16),
             shaped((rows + EDGE, LANES)),
             shaped((4 * 2 * STATE, rows)),
             shaped(channels),
             shaped((max(pairs, 1) + 1, SUBS, LANES)),
         ],
-        [SCALARS] + [ANYWHERE] * 10,
-        [pltpu.VMEM((seq_count, rows), jnp.int32), pltpu.SemaphoreType.DMA((10,))],
+        [SCALARS] + [ANYWHERE] * 9 + [later],
+        [pltpu.VMEM((seq_count, rows), jnp.int32), pltpu.SemaphoreType.DMA((9,))],
     )(
         edit_bounds.T,
         *(
@@ -596,11 +633,10 @@
                 skip_gain[None, :],
                 norm_gain[None, :],
                 base_embed,
-                hidden,
             )
         ),
-    )
-    rim_first, rim_second = rims(rim)
+        rim,
+    )
     drive = jnp.sqrt(-jnp.expm1(-2.0 * rate))
     normed = call(norm_kernel, "norm", shaped((rows + EDGE, width), bf16), [WHOLE] * 7)(
         first, second, rim_first, rim_second, bases, gain, embed
@@ -632,29 +668,19 @@
     z = call(gate_kernel, "gate", shaped((STREAMS, length, inner), bf16), [WHOLE] * 2)(
         lined, gate_w
     )
-    later = pl.BlockSpec(memory_space=pl.ANY)
-    scaled, ends, wide = call(
+    scaled, ends, starts, out_w = call(
         end_kernel,
         "ends",
         [
             shaped((4 * 2 * STATE, rows)),
             shaped((STREAMS,) + channels),
-            shaped((STREAMS, length * STATE, LANES)),
+            shaped((STREAMS, length // CHUNK) + channels),
+            shaped((inner, width), bf16),
         ],
-        [WHOLE] * 6 + [later],
-    )(bc, bc_far, weigh, c, decay, drive * keeps[0, 0:1, 0:1], z)
-
-    def local(s, after):
-        fetched = s == 1
-        return call(
-            functools.partial(local_kernel, s),
-            "local",
-            [shaped((length, inner)), shaped((length, CHUNK * STATE), bf16)]
-            + [shaped((inner, width), bf16)] * fetched,
-            [WHOLE] * 6 + [later] + [ANYWHERE] * fetched,
-            [pltpu.VMEM((length * STATE, inner), bf16)] + [pltpu.SemaphoreType.DMA] * fetched,
-            megabytes=12,
-        )(scaled, wide, c, decay, drive.astype(bf16), skip, after, *[in_hbm(w_out)] * fetched)
+        [WHOLE] * 7 + [later, ANYWHERE],
+        [pltpu.VMEM((STREAMS, length * STATE, LANES), f32), pltpu.SemaphoreType.DMA],
+        megabytes=6,
+    )(bc, bc_far, weigh, c, decay, drive, keeps, z, in_hbm(w_out))
 
     got = swap(ends.astype(bf16), "seq", 2)
     strides, powers, first_step, leads = call(
@@ -668,7 +694,23 @@
         ],
         [WHOLE] * 2 + [later],
     )(rate, keeps, scaled)
-    y_f, readout_f = local(0, scaled)
+    by_tile = (tiles, length, LANES)
+
+    def local(s, after):
+        return call(
+            functools.partial(local_kernel, s),
+            "local",
+            [shaped(by_tile), shaped((length, CHUNK * STATE), bf16)],
+            [WHOLE] * 5 + [later],
+            [
+                pltpu.VMEM((2, length, LANES), f32),
+                pltpu.VMEM(by_tile, f32),
+                pltpu.VMEM(by_tile, f32),
+            ],
+            megabytes=6,
+        )(scaled, c, decay, drive, skip, after)
+
+    y_f, readout_f = local(0, ends)
     arrived = []
     if pairs > 1:
         sends = call(
@@ -678,30 +720,35 @@
             [WHOLE] * 3 + [later],
         )(ends, got, first_step, y_f)
         arrived = [swap(send, "seq", 4 * m) for m, send in enumerate(sends, 1)]
-    y_b, readout_b, out_w = local(1, sends[0] if pairs > 1 else got)
-
-    def finish(same, dtype):
-        return call(
-            functools.partial(finish_kernel, same),
-            "finish",
-            [shaped((rows, width // 2), dtype), shaped((STREAMS, rows, inner), bf16)],
-            [WHOLE] * (10 + len(arrived)),
-        )(powers, strides, got, leads, y_f, y_b, readout_f, readout_b, z, out_w, *arrived)
-
-    def rest(gated, dtype, after):
-        return call(
-            rest_kernel, "rest", shaped((rows, width // 2), dtype), [WHOLE] * 2 + [later]
-        )(gated, out_w, after)
-
-    send, gated_far = finish(False, bf16)
-    came = swap(send, "seq", 1)
-    keep, gated_own = finish(True, f32)
-    first = keep + came.astype(f32)
+    y_b, readout_b = local(1, sends[0] if pairs > 1 else got)
+
+    operands = (
+        powers, strides, got, leads, starts, y_f, y_b, readout_f, readout_b, z, out_w, *arrived
+    )
+    half_width = (rows, width // 2)
+    gated = (STREAMS, rows, inner)
+    both = call(
+        functools.partial(finish_kernel, False),
+        "finish",
+        [shaped(half_width, bf16)] * 2,
+        [WHOLE] * len(operands),
+        [pltpu.VMEM(gated, bf16)],
+    )(*operands)
+    first_far, second_far = [swap(send, "seq", 1) for send in both]
+    first, gated_own = call(
+        functools.partial(finish_kernel, True),
+        "finish",
+        [shaped(half_width), shaped(gated, bf16)],
+        [WHOLE] * len(operands),
+    )(*operands)
+    first = first + first_far.astype(f32)
     sent = first.astype(bf16)
     if ch_count == 2:
         came = swap(sent, "ch", 1)
-    second = swap(rest(gated_far, bf16, sent), "seq", 1)
-    second = rest(gated_own, f32, sent) + second.astype(f32)
+    second = call(rest_kernel, "rest", shaped(half_width), [WHOLE] * 2 + [later])(
+        gated_own, out_w, sent
+    )
+    second = second + second_far.astype(f32)
     if ch_count == 2:
         return (second + came.astype(f32)).astype(bf16)
     total = jnp.concatenate([first, second], axis=1)

time: 65.5 us -> 61.3 us (0.936)
  Pallas kernels: 32.1 us -> 26.4 us
  waiting for transfers between devices: 9.56 us -> 14.4 us
  starting transfers between devices: 20.7 us -> 18.5 us
    pallas_call x6, Pallas kernels: 16.4 us -> 10.8 us  [the longest x2 3.98 us: local(): call(functools.partial(local_kernel, s), 'local', [shaped(by_tile), shape...]
    ppermute x11, waiting for transfers between devices: 9.55 us -> 14.4 us  [swap(): return lax.ppermute(block, axis, [(i, i ^ apart) for i in range(count)])]
    ppermute x11, starting transfers between devices: 19.4 us -> 17.2 us  [swap(): return lax.ppermute(block, axis, [(i, i ^ apart) for i in range(count)])]
    convert_element_type x1 -> x0, other arithmetic: 0.69 us -> none  [local(): drive.astype(bf16)]
  transfers between devices with their start and end apart: 13 -> 13, of which waited for: 4 -> 8; matrix products, arithmetic and copies ran while one was open for 2% -> 0% of each run, Pallas kernels for 29% -> 21%
where the time goes in v3:
time: 61.3 us; the launch traced here: 61.1 us
  Pallas kernels  26.4 us (43%)
  starting transfers between devices  18.5 us (30%)
  waiting for transfers between devices  14.4 us (23%)
  other arithmetic  0.94 us (2%)
  local copies, waits for them, and re-layouts  0.67 us (1%)
    ppermute x11, starting transfers between devices, swap(): return lax.ppermute(block, axis, [(i, i ^ apart) for i in range(count)])  17.2 us
    ppermute x11, waiting for transfers between devices, swap(): return lax.ppermute(block, axis, [(i, i ^ apart) for i in range(count)])  14.4 us
    pallas_call x1, Pallas kernels, body(): call(end_kernel, 'ends', [shaped((4 * 2 * STATE, rows)), shaped((STREAMS,...  5.05 us
    pallas_call x1, Pallas kernels, body(): call(signal_kernel, 'signal', [shaped((2 * padded, width), bf16), shaped(...  4.42 us
    pallas_call x2, Pallas kernels, local(): call(functools.partial(local_kernel, s), 'local', [shaped(by_tile), shape...  3.98 us
    pallas_call x1, Pallas kernels, body(): call(init_kernel, 'init', [shaped((width, inner), bf16), shaped((CONV, in...  3 us
    pallas_call x1, Pallas kernels, body(): call(functools.partial(finish_kernel, False), 'finish', [shaped(half_widt...  2.8 us
    pallas_call x1, Pallas kernels, body(): call(gate_kernel, 'gate', shaped((STREAMS, length, inner), bf16), [WHOLE]...  2.33 us
  transfers between devices with their start and end apart: 13, of which 8 were waited for; matrix products, arithmetic and copies ran while one was open for 0% of the time, Pallas kernels for 21%

profile of v3, /device:TPU:0, one launch (start us, length us, event | category | flops | bytes accessed | tf_op | source)
XLA Modules:
  0.0 61.1 jit_solution(11329248283361080575)
XLA Ops:
  0.0 1.0 %cut.1 = (bf16[128,1024]{1,0:T(8,128)(2,1)S(1)}, bf16[16,1024]{1,0:T(8,128)(2,1)S(1)}) custom-call(bf16[128,1024]{1,0:T(8,128)(2,1)} %hidden.1), custom_call_target="tpu_custom_call" | custom-call | tf_op jit(solution)/shard_map/cut/pallas_call | solution.py:588
  1.0 3.0 %collective-permute-start = (bf16[128,1024]{1,0:T(8,128)(2,1)S(1)}, bf16[128,1024]{1,0:T(8,128)(2,1)S(1)}, u32[]{:S(2)}, u32[]{:S(2)}) collective-permute-start(bf16[128,1024]{1,0:T(8,128)(2,1)S(1)} %get-tuple-element.45.own), channel_id=1, source_target_pairs={{0,1},{1,0},{2,3},{3,2},{4,5},{5,4},{6,7},{7,6},{8,9},{9,8},{10,11... | collective-permute-start | bytes 786440 | tf_op jit(solution)/shard_map/ppermute | solution.py:55
  4.0 0.7 %collective-permute-start.1 = (bf16[16,1024]{1,0:T(8,128)(2,1)S(1)}, bf16[16,1024]{1,0:T(8,128)(2,1)S(1)}, u32[]{:S(2)}, u32[]{:S(2)}) collective-permute-start(bf16[16,1024]{1,0:T(8,128)(2,1)S(1)} %get-tuple-element.42.after), channel_id=1, source_target_pairs={{2,4},{3,5},{6,8},{7,9},{10,12},{11,13},{14,16},{15,17},{18,20},{1... | collective-permute-start | bytes 98312 | tf_op jit(solution)/shard_map/ppermute | solution.py:77
  4.7 0.7 %collective-permute-start.2 = (bf16[16,1024]{1,0:T(8,128)(2,1)S(1)}, bf16[16,1024]{1,0:T(8,128)(2,1)S(1)}, u32[]{:S(2)}, u32[]{:S(2)}) collective-permute-start(bf16[16,1024]{1,0:T(8,128)(2,1)S(1)} %get-tuple-element.42.after), channel_id=1, source_target_pairs={{3,4},{2,5},{7,8},{6,9},{11,12},{10,13},{15,16},{14,17},{19,20},{1... | collective-permute-start | bytes 98312 | tf_op jit(solution)/shard_map/ppermute | solution.py:77
  5.4 0.7 %copy-done = s32[8,2]{0,1:T(2,128)S(1)} copy-done((s32[8,2]{0,1:T(2,128)S(1)}, s32[8,2]{0,1:T(2,128)}, u32[]{:S(2)}) %copy-start) | copy-done | bytes 88
  6.0 3.0 %init.1 = (bf16[2048,1024]{1,0:T(8,128)(2,1)S(1)}, f32[4,1024]{1,0:T(4,128)S(1)}, f32[1,1024]{1,0:T(1,128)S(1)}, bf16[32,1024]{1,0:T(8,128)(2,1)S(1)}, f32[16,10...) custom-call(s32[2,8]{1,0:T(2,128)S(1)} %bitcast.5, ...), custom_call_target="tpu_custom_call" | custom-call | tf_op jit(solution)/shard_map/init/pallas_call | solution.py:603
  9.1 1.3 %collective-permute-done.far = bf16[128,1024]{1,0:T(8,128)(2,1)S(1)} collective-permute-done((bf16[128,1024]{1,0:T(8,128)(2,1)S(1)}, bf16[128,1024]{1,0:T(8,128)(2,1)S(1)}, u32[]{:S(2)}, u32[]{:S(2)}) %collective-permute-start) | collective-permute-done | bytes 262176 | tf_op jit(solution)/shard_map/ppermute | solution.py:55
  10.3 0.6 %norm.1.own = bf16[144,2048]{1,0:T(8,128)(2,1)S(1)} custom-call(bf16[128,1024]{1,0:T(8,128)(2,1)S(1)} %get-tuple-element.45.own, bf16[128,1024]{1,0:T(8,128)(2,1)S(1)} %collective-permute-done.far, bf16[16,1024]{1,0:T(8,128)(2,1)S(1)} %collective-permute-done.1.own_rim, bf16[16,1024]{1,0:T(8,128)(2,1)S(1)} %collective-permute-done.2.far_rim, ...), custom_call_target="tpu_custom_call" | custom-call | tf_op jit(solution)/shard_map/norm/pallas_call | solution.py:641
  10.9 3.4 %collective-permute-start.3 = (bf16[144,2048]{1,0:T(8,128)(2,1)S(1)}, bf16[144,2048]{1,0:T(8,128)(2,1)S(1)}, u32[]{:S(2)}, u32[]{:S(2)}) collective-permute-start(bf16[144,2048]{1,0:T(8,128)(2,1)S(1)} %norm.1.own), channel_id=1, source_target_pairs={{0,2},{2,0},{4,6},{6,4},{8,10},{10,8},{12,14},{14,12},{16,18},{18,... | collective-permute-start | bytes 1769480 | tf_op jit(solution)/shard_map/ppermute | solution.py:55
  14.4 1.6 %collective-permute-done.3.other = bf16[144,2048]{1,0:T(8,128)(2,1)S(1)} collective-permute-done((bf16[144,2048]{1,0:T(8,128)(2,1)S(1)}, bf16[144,2048]{1,0:T(8,128)(2,1)S(1)}, u32[]{:S(2)}, u32[]{:S(2)}) %collective-permute-start.3) | collective-permute-done | bytes 589856 | tf_op jit(solution)/shard_map/ppermute | solution.py:55
  16.0 4.4 %signal.1 = (bf16[544,2048]{1,0:T(8,128)(2,1)S(1)}, f32[2,8,256,128]{3,2,1,0:T(8,128)S(1)}, f32[128,128]{1,0:T(8,128)S(1)}, bf16[2048,1024]{1,0:T(8,128)(2,1)S(1)}) custom-call(bf16[144,2048]{1,0:T(8,128)(2,1)S(1)} %norm.1.own, bf16[144,2048]{1,0:T(8,128)(2,1)S(1)} %collective-permute-done.3.other, bf16[2048,1024]{1,0:T(8,128)(2,1)S(1)} %get-tuple-element.49.w, ...), custom_call_target="tpu_custom_call" | custom-call | tf_op jit(solution)/shard_map/signal/pallas_call | solution.py:646
  20.4 0.4 collective-permute-start.4
  20.9 0.9 %collective-permute-done.4 = f32[128,128]{1,0:T(8,128)S(1)} collective-permute-done((f32[128,128]{1,0:T(8,128)S(1)}, f32[128,128]{1,0:T(8,128)S(1)}, u32[]{:S(2)}, u32[]{:S(2)}) %collective-permute-start.4) | collective-permute-done | bytes 65568 | tf_op jit(solution)/shard_map/ppermute | solution.py:55
  21.8 1.1 %collective-permute-start.5 = (f32[128,128]{1,0:T(8,128)S(1)}, f32[128,128]{1,0:T(8,128)S(1)}, u32[]{:S(2)}, u32[]{:S(2)}) collective-permute-start(f32[128,128]{1,0:T(8,128)S(1)} %add.12.bc_own), channel_id=1, source_target_pairs={{0,1},{1,0},{2,3},{3,2},{4,5},{5,4},{6,7},{7,6},{8,9},{9,8},{10,11... | collective-permute-start | bytes 196616 | tf_op jit(solution)/shard_map/ppermute | solution.py:55
  22.9 2.3 %gate.1.after_z.z = bf16[2,256,1024]{2,1,0:T(8,128)(2,1)S(1)} custom-call(bf16[544,2048]{1,0:T(8,128)(2,1)S(1)} %get-tuple-element.57.lined, bf16[2048,1024]{1,0:T(8,128)(2,1)S(1)} %get-tuple-element.58.w), custom_call_target="tpu_custom_call" | custom-call | tf_op jit(solution)/shard_map/gate/pallas_call | solution.py:668
  25.2 1.0 %collective-permute-done.5.bc_far = f32[128,128]{1,0:T(8,128)S(1)} collective-permute-done((f32[128,128]{1,0:T(8,128)S(1)}, f32[128,128]{1,0:T(8,128)S(1)}, u32[]{:S(2)}, u32[]{:S(2)}) %collective-permute-start.5) | collective-permute-done | bytes 65568 | tf_op jit(solution)/shard_map/ppermute | solution.py:55
  26.2 5.1 %ends.1 = (f32[128,128]{1,0:T(8,128)S(1)}, f32[2,16,1024]{2,1,0:T(8,128)S(1)}, f32[2,16,16,1024]{3,2,1,0:T(8,128)S(1)}, bf16[1024,2048]{1,0:T(8,128)(2,1)S(1)}) custom-call(f32[128,128]{1,0:T(8,128)S(1)} %add.12.bc_own, f32[128,128]{1,0:T(8,128)S(1)} %collective-permute-done.5.bc_far, f32[128,128]{1,0:T(8,128)S(1)} %get-tuple-element.54.weigh, ...), custom_call_target="tpu_custom_call" | custom-call | tf_op jit(solution)/shard_map/ends/pallas_call | solution.py:671
  31.3 2.5 %collective-permute-start.6 = (bf16[2,16,1024]{2,1,0:T(8,128)(2,1)S(1)}, bf16[2,16,1024]{2,1,0:T(8,128)(2,1)S(1)}, u32[]{:S(2)}, u32[]{:S(2)}) collective-permute-start(bf16[2,16,1024]{2,1,0:T(8,128)(2,1)S(1)} %convert_element_type.18), channel_id=1, source_target_pairs={{0,4},{2,6},{4,0},{6,2},{8,12},{10,14},{12,8},{14,10},{16,20},{18,... | collective-permute-start | bytes 196616 | tf_op jit(solution)/shard_map/ppermute | solution.py:55
  33.8 0.2 factors.1
  34.0 2.0 %local.2 = (f32[8,256,128]{2,1,0:T(8,128)S(1)}, bf16[256,256]{1,0:T(8,128)(2,1)S(1)}) custom-call(f32[128,128]{1,0:T(8,128)S(1)} %get-tuple-element.59.after_ends.bc, f32[2,8,256,128]{3,2,1,0:T(8,128)S(1)} %get-tuple-element.55.c, f32[16,1024]{1,0:T(8,128)S(1)} %get-tuple-element.56.decay, f32[16,1024]{1,0:T(8,128)S(1)} %negate_sqrt_fusion.drive, ...), custom_call_target="tpu_custom_call" | custom-call | tf_op jit(solution)/shard_map/local/pallas_call | solution.py:700
  36.1 2.0 %collective-permute-start.7 = (bf16[16,1024]{1,0:T(8,128)(2,1)S(1)}, bf16[16,1024]{1,0:T(8,128)(2,1)S(1)}, u32[]{:S(2)}, u32[]{:S(2)}) collective-permute-start(bf16[16,1024]{1,0:T(8,128)(2,1)S(1)} %get-tuple-element.68.after), channel_id=1, source_target_pairs={{0,8},{2,10},{4,12},{6,14},{8,0},{10,2},{12,4},{14,6},{16,24},{18,... | collective-permute-start | bytes 98312 | tf_op jit(solution)/shard_map/ppermute | solution.py:55
  38.0 2.6 %collective-permute-start.8 = (bf16[16,1024]{1,0:T(8,128)(2,1)S(1)}, bf16[16,1024]{1,0:T(8,128)(2,1)S(1)}, u32[]{:S(2)}, u32[]{:S(2)}) collective-permute-start(bf16[16,1024]{1,0:T(8,128)(2,1)S(1)} %get-tuple-element.73), channel_id=1, source_target_pairs={{0,16},{2,18},{4,20},{6,22},{8,24},{10,26},{12,28},{14,30},{16,0},... | collective-permute-start | bytes 98312 | tf_op jit(solution)/shard_map/ppermute | solution.py:55
  40.6 2.0 %local.3 = (f32[8,256,128]{2,1,0:T(8,128)S(1)}, bf16[256,256]{1,0:T(8,128)(2,1)S(1)}) custom-call(f32[128,128]{1,0:T(8,128)S(1)} %get-tuple-element.59.after_ends.bc, f32[2,8,256,128]{3,2,1,0:T(8,128)S(1)} %get-tuple-element.55.c, f32[16,1024]{1,0:T(8,128)S(1)} %get-tuple-element.56.decay, f32[16,1024]{1,0:T(8,128)S(1)} %negate_sqrt_fusion.drive, ...), custom_call_target="tpu_custom_call" | custom-call | tf_op jit(solution)/shard_map/local/pallas_call | solution.py:700
  42.6 0.8 %collective-permute-done.8.rest_1_ = bf16[16,1024]{1,0:T(8,128)(2,1)S(1)} collective-permute-done((bf16[16,1024]{1,0:T(8,128)(2,1)S(1)}, bf16[16,1024]{1,0:T(8,128)(2,1)S(1)}, u32[]{:S(2)}, u32[]{:S(2)}) %collective-permute-start.8) | collective-permute-done | bytes 32800 | tf_op jit(solution)/shard_map/ppermute | solution.py:55
  43.5 2.9 %collective-permute-done.9.rest_2_ = bf16[16,1024]{1,0:T(8,128)(2,1)S(1)} collective-permute-done((bf16[16,1024]{1,0:T(8,128)(2,1)S(1)}, bf16[16,1024]{1,0:T(8,128)(2,1)S(1)}, u32[]{:S(2)}, u32[]{:S(2)}) %collective-permute-start.9) | collective-permute-done | bytes 32800 | tf_op jit(solution)/shard_map/ppermute | solution.py:55
  46.3 2.8 %finish.3 = (bf16[128,1024]{1,0:T(8,128)(2,1)S(1)}, bf16[128,1024]{1,0:T(8,128)(2,1)S(1)}) custom-call(bf16[256,1024]{1,0:T(8,128)(2,1)S(1)} %get-tuple-element.60.powers, f32[2,16,1024]{2,1,0:T(8,128)S(1)} %get-tuple-element.61.strides, bf16[2,16,1024]{2,1,0:T(8,128)(2,1)S(1)} %collective-permute-done.6.got, ...), custom_call_target="tpu_custom_call" | custom-call | tf_op jit(solution)/shard_map/finish/pallas_call | solution.py:730
  49.2 0.5 collective-permute-start.11
  49.7 2.2 %finish.2 = (f32[128,1024]{1,0:T(8,128)S(1)}, bf16[2,128,1024]{2,1,0:T(8,128)(2,1)S(1)}) custom-call(bf16[256,1024]{1,0:T(8,128)(2,1)S(1)} %get-tuple-element.60.powers, f32[2,16,1024]{2,1,0:T(8,128)S(1)} %get-tuple-element.61.strides, bf16[2,16,1024]{2,1,0:T(8,128)(2,1)S(1)} %collective-permute-done.6.got, f32[3,2,16,1024]{3,2,1,0:T(8,128)S(1)} %get-tuple-element.63.leads, ...), custom_call_target="tpu_custom_call" | custom-call | tf_op jit(solution)/shard_map/finish/pallas_call | solution.py:738
  52.0 1.6 %collective-permute-start.12 = (bf16[128,1024]{1,0:T(8,128)(2,1)S(1)}, bf16[128,1024]{1,0:T(8,128)(2,1)S(1)}, u32[]{:S(2)}, u32[]{:S(2)}) collective-permute-start(bf16[128,1024]{1,0:T(8,128)(2,1)S(1)} %add_convert_fusion.1.after_first), channel_id=1, source_target_pairs={{0,1},{1,0},{2,3},{3,2},{4,5},{5,4},{6,7},{7,6},{8,9},{9,8},{10,11... | collective-permute-start | bytes 786440 | tf_op jit(solution)/shard_map/ppermute | solution.py:55
  53.5 0.9 %rest.1 = f32[128,1024]{1,0:T(8,128)S(1)} custom-call(bf16[2,128,1024]{2,1,0:T(8,128)(2,1)S(1)} %get-tuple-element.75.gated, bf16[1024,2048]{1,0:T(8,128)(2,1)S(1)} %get-tuple-element.72.w, bf16[128,1024]{1,0:T(8,128)(2,1)S(1)} %add_convert_fusion.1.after_first), custom_call_target="tpu_custom_call" | custom-call | tf_op jit(solution)/shard_map/rest/pallas_call | solution.py:748
  54.5 5.9 %collective-permute-done.12 = bf16[128,1024]{1,0:T(8,128)(2,1)S(1)} collective-permute-done((bf16[128,1024]{1,0:T(8,128)(2,1)S(1)}, bf16[128,1024]{1,0:T(8,128)(2,1)S(1)}, u32[]{:S(2)}, u32[]{:S(2)}) %collective-permute-start.12) | collective-permute-done | bytes 262176 | tf_op jit(solution)/shard_map/ppermute | solution.py:55
  60.3 0.8 %add_convert_fusion = bf16[128,1024]{1,0:T(8,128)(2,1)} fusion(bf16[128,1024]{1,0:T(8,128)(2,1)S(1)} %collective-permute-done.12, f32[128,1024]{1,0:T(8,128)S(1)} %rest.1, bf16[128,1024]{1,0:T(8,128)(2,1)S(1)} %collective-permute-done.11), kind=kLoop, calls=%fused_computation | loop fusion | flops 655360 | bytes 1310720 | tf_op jit(solution)/shard_map/convert_element_type | solution.py:753
  (14 shorter events, 0.3 us)
Async XLA Ops:
  1.0 9.3 %collective-permute-start = (bf16[128,1024]{1,0:T(8,128)(2,1)S(1)}, bf16[128,1024]{1,0:T(8,128)(2,1)S(1)}, u32[]{:S(2)}, u32[]{:S(2)}) collective-permute-start(bf16[128,1024]{1,0:T(8,128)(2,1)S(1)} %get-tuple-element.45.own), channel_id=1, source_target_pairs={{0,1},{1,0},{2,3},{3,2},{4,5},{5,4},{6,7},{7,6},{8,9},{9,8},{10,11... | collective-permute-start | bytes 786440 | tf_op jit(solution)/shard_map/ppermute | solution.py:55
  4.0 5.0 %collective-permute-start.1 = (bf16[16,1024]{1,0:T(8,128)(2,1)S(1)}, bf16[16,1024]{1,0:T(8,128)(2,1)S(1)}, u32[]{:S(2)}, u32[]{:S(2)}) collective-permute-start(bf16[16,1024]{1,0:T(8,128)(2,1)S(1)} %get-tuple-element.42.after), channel_id=1, source_target_pairs={{2,4},{3,5},{6,8},{7,9},{10,12},{11,13},{14,16},{15,17},{18,20},{1... | collective-permute-start | bytes 98312 | tf_op jit(solution)/shard_map/ppermute | solution.py:77
  4.7 4.4 %collective-permute-start.2 = (bf16[16,1024]{1,0:T(8,128)(2,1)S(1)}, bf16[16,1024]{1,0:T(8,128)(2,1)S(1)}, u32[]{:S(2)}, u32[]{:S(2)}) collective-permute-start(bf16[16,1024]{1,0:T(8,128)(2,1)S(1)} %get-tuple-element.42.after), channel_id=1, source_target_pairs={{3,4},{2,5},{7,8},{6,9},{11,12},{10,13},{15,16},{14,17},{19,20},{1... | collective-permute-start | bytes 98312 | tf_op jit(solution)/shard_map/ppermute | solution.py:77
  5.3 0.7 %copy-start = (s32[8,2]{0,1:T(2,128)S(1)}, s32[8,2]{0,1:T(2,128)}, u32[]{:S(2)}) copy-start(s32[8,2]{0,1:T(2,128)} %param.14) | copy-start | bytes 196
  10.9 5.0 %collective-permute-start.3 = (bf16[144,2048]{1,0:T(8,128)(2,1)S(1)}, bf16[144,2048]{1,0:T(8,128)(2,1)S(1)}, u32[]{:S(2)}, u32[]{:S(2)}) collective-permute-start(bf16[144,2048]{1,0:T(8,128)(2,1)S(1)} %norm.1.own), channel_id=1, source_target_pairs={{0,2},{2,0},{4,6},{6,4},{8,10},{10,8},{12,14},{14,12},{16,18},{18,... | collective-permute-start | bytes 1769480 | tf_op jit(solution)/shard_map/ppermute | solution.py:55
  20.4 1.3 %collective-permute-start.4 = (f32[128,128]{1,0:T(8,128)S(1)}, f32[128,128]{1,0:T(8,128)S(1)}, u32[]{:S(2)}, u32[]{:S(2)}) collective-permute-start(f32[128,128]{1,0:T(8,128)S(1)} %get-tuple-element.53), channel_id=1, source_target_pairs={{0,2},{2,0},{4,6},{6,4},{8,10},{10,8},{12,14},{14,12},{16,18},{18,... | collective-permute-start | bytes 196616 | tf_op jit(solution)/shard_map/ppermute | solution.py:55
  21.8 4.4 %collective-permute-start.5 = (f32[128,128]{1,0:T(8,128)S(1)}, f32[128,128]{1,0:T(8,128)S(1)}, u32[]{:S(2)}, u32[]{:S(2)}) collective-permute-start(f32[128,128]{1,0:T(8,128)S(1)} %add.12.bc_own), channel_id=1, source_target_pairs={{0,1},{1,0},{2,3},{3,2},{4,5},{5,4},{6,7},{7,6},{8,9},{9,8},{10,11... | collective-permute-start | bytes 196616 | tf_op jit(solution)/shard_map/ppermute | solution.py:55
  31.3 4.7 %collective-permute-start.6 = (bf16[2,16,1024]{2,1,0:T(8,128)(2,1)S(1)}, bf16[2,16,1024]{2,1,0:T(8,128)(2,1)S(1)}, u32[]{:S(2)}, u32[]{:S(2)}) collective-permute-start(bf16[2,16,1024]{2,1,0:T(8,128)(2,1)S(1)} %convert_element_type.18), channel_id=1, source_target_pairs={{0,4},{2,6},{4,0},{6,2},{8,12},{10,14},{12,8},{14,10},{16,20},{18,... | collective-permute-start | bytes 196616 | tf_op jit(solution)/shard_map/ppermute | solution.py:55
  36.1 6.6 %collective-permute-start.7 = (bf16[16,1024]{1,0:T(8,128)(2,1)S(1)}, bf16[16,1024]{1,0:T(8,128)(2,1)S(1)}, u32[]{:S(2)}, u32[]{:S(2)}) collective-permute-start(bf16[16,1024]{1,0:T(8,128)(2,1)S(1)} %get-tuple-element.68.after), channel_id=1, source_target_pairs={{0,8},{2,10},{4,12},{6,14},{8,0},{10,2},{12,4},{14,6},{16,24},{18,... | collective-permute-start | bytes 98312 | tf_op jit(solution)/shard_map/ppermute | solution.py:55
  38.0 5.4 %collective-permute-start.8 = (bf16[16,1024]{1,0:T(8,128)(2,1)S(1)}, bf16[16,1024]{1,0:T(8,128)(2,1)S(1)}, u32[]{:S(2)}, u32[]{:S(2)}) collective-permute-start(bf16[16,1024]{1,0:T(8,128)(2,1)S(1)} %get-tuple-element.73), channel_id=1, source_target_pairs={{0,16},{2,18},{4,20},{6,22},{8,24},{10,26},{12,28},{14,30},{16,0},... | collective-permute-start | bytes 98312 | tf_op jit(solution)/shard_map/ppermute | solution.py:55
  40.6 5.7 %collective-permute-start.9 = (bf16[16,1024]{1,0:T(8,128)(2,1)S(1)}, bf16[16,1024]{1,0:T(8,128)(2,1)S(1)}, u32[]{:S(2)}, u32[]{:S(2)}) collective-permute-start(bf16[16,1024]{1,0:T(8,128)(2,1)S(1)} %get-tuple-element.74), channel_id=1, source_target_pairs={{0,24},{2,26},{4,28},{6,30},{8,16},{10,18},{12,20},{14,22},{16,8},... | collective-permute-start | bytes 98312 | tf_op jit(solution)/shard_map/ppermute | solution.py:55
  49.1 2.7 %collective-permute-start.10 = (bf16[128,1024]{1,0:T(8,128)(2,1)S(1)}, bf16[128,1024]{1,0:T(8,128)(2,1)S(1)}, u32[]{:S(2)}, u32[]{:S(2)}) collective-permute-start(bf16[128,1024]{1,0:T(8,128)(2,1)S(1)} %get-tuple-element.77), channel_id=1, source_target_pairs={{0,2},{2,0},{4,6},{6,4},{8,10},{10,8},{12,14},{14,12},{16,18},{18,... | collective-permute-start | bytes 786440 | tf_op jit(solution)/shard_map/ppermute | solution.py:55
  49.2 5.2 %collective-permute-start.11 = (bf16[128,1024]{1,0:T(8,128)(2,1)S(1)}, bf16[128,1024]{1,0:T(8,128)(2,1)S(1)}, u32[]{:S(2)}, u32[]{:S(2)}) collective-permute-start(bf16[128,1024]{1,0:T(8,128)(2,1)S(1)} %get-tuple-element.78), channel_id=1, source_target_pairs={{0,2},{2,0},{4,6},{6,4},{8,10},{10,8},{12,14},{14,12},{16,18},{18,... | collective-permute-start | bytes 786440 | tf_op jit(solution)/shard_map/ppermute | solution.py:55
  52.0 8.4 %collective-permute-start.12 = (bf16[128,1024]{1,0:T(8,128)(2,1)S(1)}, bf16[128,1024]{1,0:T(8,128)(2,1)S(1)}, u32[]{:S(2)}, u32[]{:S(2)}) collective-permute-start(bf16[128,1024]{1,0:T(8,128)(2,1)S(1)} %add_convert_fusion.1.after_first), channel_id=1, source_target_pairs={{0,1},{1,0},{2,3},{3,2},{4,5},{5,4},{6,7},{7,6},{8,9},{9,8},{10,11... | collective-permute-start | bytes 786440 | tf_op jit(solution)/shard_map/ppermute | solution.py:55

commit v4 on v3

--- a/solution.py
+++ b/solution.py
@@ -83,16 +83,11 @@
     )
 
 
-def cut_kernel(hidden, own, rim, sems):
-    low = pl.multiple_of(spot()[1] * (own.shape[0] - EDGE), EDGE)
-    copies = [
-        pltpu.make_async_copy(hidden, own, sems.at[0]),
-        pltpu.make_async_copy(hidden.at[pl.ds(low, EDGE), :], rim, sems.at[1]),
-    ]
-    for copy in copies:
-        copy.start()
-    for copy in copies:
-        copy.wait()
+def rim_kernel(hidden, rim, sem):
+    low = pl.multiple_of(spot()[1] * (hidden.shape[0] - EDGE), EDGE)
+    copy = pltpu.make_async_copy(hidden.at[pl.ds(low, EDGE), :], rim, sem)
+    copy.start()
+    copy.wait()
 
 
 def between(chip, m):
@@ -103,20 +98,21 @@
 
 
 def init_kernel(
-    bounds, tokens_all, w_in, conv_w, conv_b, proj, rate_all, skip, gain_all, embed_all, after,
-    signal_w, taps, offset, proj_half, rate, skip_half, norm_gain, embed,
-    bases, weigh, decay, keeps, tokens, sems,
+    bounds_all, tokens_all, w_in, conv_w, conv_b, proj, rate_all, skip, gain_all, embed_all, after,
+    signal_w, gate_w, taps, offset, proj_half, rate, skip_half, norm_gain, embed,
+    bases, weigh, decay, keeps, bounds, tokens, sems,
 ):
     place, core, chip = spot()
     count, rows = tokens.shape
     length = 2 * rows
-    inner = signal_w.shape[1]
+    inner = rate.shape[1]
     chips = count // 2
     mine = pl.ds(pl.multiple_of(core * inner, inner), inner)
     copies = [
         pltpu.make_async_copy(source, target, sems.at[i])
         for i, (source, target) in enumerate(
             (
+                (bounds_all, bounds),
                 (rate_all.at[:, mine], rate),
                 (tokens_all, tokens),
                 (gain_all, norm_gain),
@@ -126,12 +122,14 @@
                 (proj.at[:, mine], proj_half),
                 (skip.at[:, mine], skip_half),
                 (w_in.at[0, :, mine], signal_w),
+                (w_in.at[1, :, mine], gate_w),
             )
         )
     ]
     for copy in copies:
         copy.start()
 
+    copies[0].wait()
     marks = [bounds[k, i] for i in range(bounds.shape[1]) for k in range(2)]
     factors = []
     for i, mark in enumerate(marks):
@@ -172,11 +170,11 @@
     for m in range(1, chips // 2):
         low, high, _ = between(chip, m)
         keeps[1 + m] = kept(low, high)
-    copies[0].wait()
+    copies[1].wait()
     for t in range(inner // LANES):
         decay[:, tile(t)] = jnp.exp(-rate[:, tile(t)])
 
-    copies[1].wait()
+    copies[2].wait()
 
     def column(row):
         line = tokens[pl.ds(row, 1), :].astype(f32)
@@ -187,7 +185,7 @@
     beyond = jnp.where(core == 0, beyond[rows - EDGE :], beyond[:EDGE])
     inside = jnp.where(core == 0, place > 0, place < count - 1)
     bases[rows:, :] = jnp.where(inside, beyond, -1.0)
-    for copy in copies[2:]:
+    for copy in copies[3:]:
         copy.wait()
 
 
@@ -226,55 +224,62 @@
         one(far_rim, own_rim, rows, EDGE)
 
 
+def both_ways(normed, lined):
+    count, width = normed.shape
+    lined[:count, :] = normed[...]
+    r = lax.broadcasted_iota(jnp.int32, (LANES, LANES), 0)
+    q = lax.broadcasted_iota(jnp.int32, (LANES, LANES), 1)
+    turn = jnp.where(r + q == LANES - 1, 1.0, 0.0).astype(bf16)
+    for t in range(width // LANES):
+        piece = normed[:, tile(width // LANES - 1 - t)]
+        lined[count:, tile(t)] = jnp.dot(piece, turn, preferred_element_type=f32).astype(bf16)
+
+
+def own_signal_kernel(normed, w, lined, x_out):
+    inner = w.shape[1]
+    block = min(BLOCK, inner)
+    both_ways(normed, lined)
+    for b in range(inner // block):
+        cols = slice(b * block, (b + 1) * block)
+        x = jnp.dot(lined[...], w[:, cols], preferred_element_type=f32)
+        x_out[:, cols] = x.astype(bf16).astype(f32)
+
+
 def signal_kernel(
-    own, other, w, taps, offset, proj, w_in, lined, c_out, bc_out, gate_w, x_tiles, sem
+    normed, x_own, w, taps, offset, proj, lined, c_out, bc_out, x_tiles
 ):
     _, core, _ = spot()
-    rows = own.shape[0] - EDGE
+    count = normed.shape[0]
+    rows = count - EDGE
     length = 2 * rows
-    width = own.shape[1]
-    padded = length + EDGE
     inner = w.shape[1]
     block = min(BLOCK, inner)
     tiles = block // LANES
-    fetch = pltpu.make_async_copy(
-        w_in.at[1, :, pl.ds(pl.multiple_of(core * inner, inner), inner)], gate_w, sem
-    )
-    fetch.start()
-
-    def line_up(first, second):
-        lined[0:EDGE, :] = first[rows:, :]
-        lined[EDGE : EDGE + rows, :] = first[:rows, :]
-        lined[EDGE + rows : padded, :] = second[:rows, :]
-        r = lax.broadcasted_iota(jnp.int32, (LANES, LANES), 0)
-        q = lax.broadcasted_iota(jnp.int32, (LANES, LANES), 1)
-        turn = jnp.where(r + q == LANES - 1, 1.0, 0.0).astype(bf16)
-        for t in range(width // LANES):
-            at = tile(width // LANES - 1 - t)
-            for base, piece in ((0, first[:rows, at]), (rows, second[:, at])):
-                turned = jnp.dot(piece, turn, preferred_element_type=f32).astype(bf16)
-                lined[padded + base : padded + base + piece.shape[0], tile(t)] = turned
-
-    @pl.when(core == 0)
-    def _():
-        line_up(own, other)
-
-    @pl.when(core != 0)
-    def _():
-        line_up(other, own)
-
+    both_ways(normed, lined)
     inner_bc = 2 * STATE
     sums = [jnp.zeros((inner_bc, rows), f32) for _ in range(STREAMS * HALVES)]
 
-    def project(b, s):
-        x = jnp.dot(
-            lined[s * padded : (s + 1) * padded, :],
-            w[:, b * block : (b + 1) * block],
-            preferred_element_type=f32,
+    def project(b):
+        other = jnp.dot(
+            lined[...], w[:, b * block : (b + 1) * block], preferred_element_type=f32
         )
-        x = x.astype(bf16).astype(f32)
-        for t in range(tiles):
-            x_tiles[(b % 2 * STREAMS + s) * tiles + t] = x[:, tile(t)]
+        other = other.astype(bf16).astype(f32)
+        for s in range(STREAMS):
+            first = EDGE * (1 - s)
+            low = s * count
+            for t in range(tiles):
+                slot = (b % 2 * STREAMS + s) * tiles + t
+                mine = x_own[low : low + count, tile(b * tiles + t)]
+                far = other[low : low + count, tile(t)]
+                x_tiles[slot, first : first + rows, :] = jnp.where(
+                    core == 0, mine[:rows], far[:rows]
+                )
+                x_tiles[slot, first + rows : first + length, :] = jnp.where(
+                    core == 0, far[:rows], mine[:rows]
+                )
+                x_tiles[slot, s * length : s * length + EDGE, :] = jnp.where(
+                    core == s, mine[rows:], far[rows:]
+                )
 
     def convolve(b, s):
         mixed = []
@@ -297,27 +302,30 @@
                 preferred_element_type=f32,
             )
 
-    turns = [(b, s) for b in range(inner // block) for s in range(STREAMS)]
-    project(*turns[0])
-    for before, after in zip(turns, turns[1:] + [None]):
-        if after is not None:
-            project(*after)
-        convolve(*before)
+    blocks = inner // block
+    project(0)
+    for b in range(blocks):
+        if b + 1 < blocks:
+            project(b + 1)
+        for s in range(STREAMS):
+            convolve(b, s)
     for i, total in enumerate(sums):
         bc_out[i * inner_bc : (i + 1) * inner_bc, :] = total
-    fetch.wait()
-
-
-def gate_kernel(lined, w, z_out):
-    padded = lined.shape[0] // 2
-    length = padded - EDGE
+
+
+def gate_kernel(lined_own, lined_other, w, z_out):
+    _, core, _ = spot()
+    count = lined_own.shape[0] // 2
+    rows = count - EDGE
     inner = w.shape[1]
     block = min(BLOCK, inner)
     for b in range(inner // block):
         cols = slice(b * block, (b + 1) * block)
-        for s, first in ((0, EDGE), (1, padded)):
-            z = jnp.dot(lined[first : first + length, :], w[:, cols], preferred_element_type=f32)
-            z_out[s, :, cols] = z.astype(bf16)
+        for lined, half in ((lined_own, core), (lined_other, 1 - core)):
+            z = jnp.dot(lined[...], w[:, cols], preferred_element_type=f32).astype(bf16)
+            at = pl.ds(pl.multiple_of(half * rows, rows), rows)
+            for s in range(STREAMS):
+                z_out[s, at, cols] = z[s * count : s * count + rows]
 
 
 def lane_of(values, lane):
@@ -585,25 +593,26 @@
     chips = seq_count // 2
     chip = spot()[2]
 
-    own, rim = call(
-        cut_kernel,
-        "cut",
-        [shaped(hidden.shape, bf16), shaped((EDGE, hidden.shape[1]), bf16)],
+    first, second = both_halves(hidden)
+    rim = call(
+        rim_kernel,
+        "rim",
+        shaped((EDGE, hidden.shape[1]), bf16),
         [ANYWHERE],
-        [pltpu.SemaphoreType.DMA((2,))],
+        [pltpu.SemaphoreType.DMA],
     )(in_hbm(hidden))
     later = pl.BlockSpec(memory_space=pl.ANY)
     rim_first, rim_second = rims(rim)
-    first, second = both_halves(own)
     channels = (STATE, inner)
     pairs = chips // 2
     (
-        signal_w, taps, offset, proj_half, rate, skip, gain, embed,
+        signal_w, gate_w, taps, offset, proj_half, rate, skip, gain, embed,
         bases, weigh, decay, keeps,
     ) = call(
         init_kernel,
         "init",
         [
+            shaped((width, inner), bf16),
             shaped((width, inner), bf16),
             shaped((CONV, inner)),
             shaped((1, inner)),
@@ -617,13 +626,17 @@
             shaped(channels),
             shaped((max(pairs, 1) + 1, SUBS, LANES)),
         ],
-        [SCALARS] + [ANYWHERE] * 9 + [later],
-        [pltpu.VMEM((seq_count, rows), jnp.int32), pltpu.SemaphoreType.DMA((9,))],
+        [ANYWHERE] * 10 + [later],
+        [
+            pltpu.SMEM(edit_bounds.shape[::-1], jnp.int32),
+            pltpu.VMEM((seq_count, rows), jnp.int32),
+            pltpu.SemaphoreType.DMA((11,)),
+        ],
     )(
-        edit_bounds.T,
         *(
             in_hbm(array)
             for array in (
+                edit_bounds.T,
                 tokens.reshape(seq_count, rows),
                 w_in,
                 conv_w,
@@ -643,30 +656,33 @@
     )
     partner = swap(normed, "seq", 1)
 
-    lined, c, bc, gate_w = call(
+    lined = shaped((2 * (rows + EDGE), width), bf16)
+    lined_own, x_own = call(
+        own_signal_kernel,
+        "own_signal",
+        [lined, shaped((2 * (rows + EDGE), inner))],
+        [WHOLE] * 2,
+    )(normed, signal_w)
+    lined_other, c, bc = call(
         signal_kernel,
         "signal",
         [
-            shaped((2 * padded, width), bf16),
+            lined,
             shaped((STREAMS, tiles, length, LANES)),
             shaped((4 * 2 * STATE, rows)),
-            shaped((width, inner), bf16),
         ],
-        [WHOLE] * 6 + [ANYWHERE],
-        [
-            pltpu.VMEM((2 * STREAMS * block // LANES, padded, LANES), f32),
-            pltpu.SemaphoreType.DMA,
-        ],
+        [WHOLE] * 6,
+        [pltpu.VMEM((2 * STREAMS * block // LANES, padded, LANES), f32)],
         megabytes=6,
-    )(normed, partner, signal_w, taps, offset, proj_half, in_hbm(w_in))
+    )(partner, x_own, signal_w, taps, offset, proj_half)
     bc = bc + swap(bc, "seq", 1)
     if ch_count == 2:
         bc_far = swap(bc, "ch", 1)
     else:
         bc, bc_far = lax.psum(bc, "ch"), jnp.zeros_like(bc)
 
-    z = call(gate_kernel, "gate", shaped((STREAMS, length, inner), bf16), [WHOLE] * 2)(
-        lined, gate_w
+    z = call(gate_kernel, "gate", shaped((STREAMS, length, inner), bf16), [WHOLE] * 3)(
+        lined_own, lined_other, gate_w
     )
     scaled, ends, starts, out_w = call(
         end_kernel,

time: 61.3 us -> 59.3 us (0.967)
  waiting for transfers between devices: 14.4 us -> 11.6 us
  Pallas kernels: 26.4 us -> 27.2 us
  local copies, waits for them, and re-layouts: 0.67 us -> 0.01 us
    ppermute x11, waiting for transfers between devices: 14.4 us -> 11.6 us  [swap(): return lax.ppermute(block, axis, [(i, i ^ apart) for i in range(count)])]
    pallas_call x3 -> x4, Pallas kernels: 8.39 us -> 9.06 us  [the longest x1 3.78 us: body(): call(init_kernel, 'init', [shaped((width, inner), bf16), shaped((width, i...]
    unnamed x2, local copies, waits for them, and re-layouts: 0.67 us -> 0.01 us
    ppermute x11, starting transfers between devices: 17.2 us -> 17.8 us  [swap(): return lax.ppermute(block, axis, [(i, i ^ apart) for i in range(count)])]
  transfers between devices with their start and end apart: 13 -> 13, of which waited for: 8 -> 7; matrix products, arithmetic and copies ran while one was open for 0% -> 0% of each run, Pallas kernels for 21% -> 27%
where the time goes in v4:
time: 59.3 us; the launch traced here: 59.1 us
  Pallas kernels  27.2 us (46%)
  starting transfers between devices  19.1 us (32%)
  waiting for transfers between devices  11.6 us (20%)
  other arithmetic  0.93 us (2%)
    ppermute x11, starting transfers between devices, swap(): return lax.ppermute(block, axis, [(i, i ^ apart) for i in range(count)])  17.8 us
    ppermute x11, waiting for transfers between devices, swap(): return lax.ppermute(block, axis, [(i, i ^ apart) for i in range(count)])  11.6 us
    pallas_call x1, Pallas kernels, body(): call(end_kernel, 'ends', [shaped((4 * 2 * STATE, rows)), shaped((STREAMS,...  5.05 us
    pallas_call x2, Pallas kernels, local(): call(functools.partial(local_kernel, s), 'local', [shaped(by_tile), shape...  3.97 us
    pallas_call x1, Pallas kernels, body(): call(init_kernel, 'init', [shaped((width, inner), bf16), shaped((width, i...  3.78 us
    pallas_call x1, Pallas kernels, body(): call(signal_kernel, 'signal', [lined, shaped((STREAMS, tiles, length, LAN...  2.8 us
    pallas_call x1, Pallas kernels, body(): call(functools.partial(finish_kernel, False), 'finish', [shaped(half_widt...  2.7 us
    pallas_call x1, Pallas kernels, body(): call(gate_kernel, 'gate', shaped((STREAMS, length, inner), bf16), [WHOLE]...  2.65 us
  transfers between devices with their start and end apart: 13, of which 7 were waited for; matrix products, arithmetic and copies ran while one was open for 0% of the time, Pallas kernels for 27%

profile of v4, /device:TPU:0, one launch (start us, length us, event | category | flops | bytes accessed | tf_op | source)
XLA Modules:
  0.0 59.1 jit_solution(14302245921114377626)
XLA Ops:
  0.0 3.0 %collective-permute-start = (bf16[128,1024]{1,0:T(8,128)(2,1)}, bf16[128,1024]{1,0:T(8,128)(2,1)S(1)}, u32[]{:S(2)}, u32[]{:S(2)}) collective-permute-start(bf16[128,1024]{1,0:T(8,128)(2,1)} %own.1), channel_id=1, source_target_pairs={{0,1},{1,0},{2,3},{3,2},{4,5},{5,4},{6,7},{7,6},{8,9},{9,8},{10,11... | collective-permute-start | bytes 786440 | tf_op jit(solution)/shard_map/ppermute | solution.py:55
  3.0 0.8 %rim.1.after = bf16[16,1024]{1,0:T(8,128)(2,1)S(1)} custom-call(bf16[128,1024]{1,0:T(8,128)(2,1)} %own.1), custom_call_target="tpu_custom_call" | custom-call | tf_op jit(solution)/shard_map/rim/pallas_call | solution.py:597
  3.8 0.7 %collective-permute-start.1 = (bf16[16,1024]{1,0:T(8,128)(2,1)S(1)}, bf16[16,1024]{1,0:T(8,128)(2,1)S(1)}, u32[]{:S(2)}, u32[]{:S(2)}) collective-permute-start(bf16[16,1024]{1,0:T(8,128)(2,1)S(1)} %rim.1.after), channel_id=1, source_target_pairs={{2,4},{3,5},{6,8},{7,9},{10,12},{11,13},{14,16},{15,17},{18,20},{1... | collective-permute-start | bytes 98312 | tf_op jit(solution)/shard_map/ppermute | solution.py:77
  4.4 0.7 %collective-permute-start.2 = (bf16[16,1024]{1,0:T(8,128)(2,1)S(1)}, bf16[16,1024]{1,0:T(8,128)(2,1)S(1)}, u32[]{:S(2)}, u32[]{:S(2)}) collective-permute-start(bf16[16,1024]{1,0:T(8,128)(2,1)S(1)} %rim.1.after), channel_id=1, source_target_pairs={{3,4},{2,5},{7,8},{6,9},{11,12},{10,13},{15,16},{14,17},{19,20},{1... | collective-permute-start | bytes 98312 | tf_op jit(solution)/shard_map/ppermute | solution.py:77
  5.1 3.8 %init.1 = (bf16[2048,1024]{1,0:T(8,128)(2,1)S(1)}, bf16[2048,1024]{1,0:T(8,128)(2,1)S(1)}, f32[4,1024]{1,0:T(4,128)S(1)}, f32[1,1024]{1,0:T(1,128)S(1)}, bf16[32...) custom-call(s32[2,8]{1,0:T(2,128)} %bitcast.9, ...), custom_call_target="tpu_custom_call" | custom-call | tf_op jit(solution)/shard_map/init/pallas_call | solution.py:611
  8.9 0.5 collective-permute-done.far
  9.5 0.6 %norm.1.normed = bf16[144,2048]{1,0:T(8,128)(2,1)S(1)} custom-call(bf16[128,1024]{1,0:T(8,128)(2,1)S(1)} %copy-done, bf16[128,1024]{1,0:T(8,128)(2,1)S(1)} %collective-permute-done.far, bf16[16,1024]{1,0:T(8,128)(2,1)S(1)} %collective-permute-done.1.own_rim, bf16[16,1024]{1,0:T(8,128)(2,1)S(1)} %collective-permute-done.2.far_rim, ...), custom_call_target="tpu_custom_call" | custom-call | tf_op jit(solution)/shard_map/norm/pallas_call | solution.py:654
  10.1 4.0 %collective-permute-start.3 = (bf16[144,2048]{1,0:T(8,128)(2,1)S(1)}, bf16[144,2048]{1,0:T(8,128)(2,1)S(1)}, u32[]{:S(2)}, u32[]{:S(2)}) collective-permute-start(bf16[144,2048]{1,0:T(8,128)(2,1)S(1)} %norm.1.normed), channel_id=1, source_target_pairs={{0,2},{2,0},{4,6},{6,4},{8,10},{10,8},{12,14},{14,12},{16,18},{18,... | collective-permute-start | bytes 1769480 | tf_op jit(solution)/shard_map/ppermute | solution.py:55
  14.1 1.7 %own_signal.1 = (bf16[288,2048]{1,0:T(8,128)(2,1)S(1)}, f32[288,1024]{1,0:T(8,128)S(1)}) custom-call(bf16[144,2048]{1,0:T(8,128)(2,1)S(1)} %norm.1.normed, bf16[2048,1024]{1,0:T(8,128)(2,1)S(1)} %get-tuple-element.47.w), custom_call_target="tpu_custom_call" | custom-call | tf_op jit(solution)/shard_map/own_signal/pallas_call | solution.py:660
  15.8 2.8 %signal.1 = (bf16[288,2048]{1,0:T(8,128)(2,1)S(1)}, f32[2,8,256,128]{3,2,1,0:T(8,128)S(1)}, f32[128,128]{1,0:T(8,128)S(1)}) custom-call(bf16[144,2048]{1,0:T(8,128)(2,1)S(1)} %collective-permute-done.3.normed, f32[288,1024]{1,0:T(8,128)S(1)} %get-tuple-element.48.x_own, bf16[2048,1024]{1,0:T(8,128)(2,1)S(1)} %get-tuple-element.47.w, ...), custom_call_target="tpu_custom_call" | custom-call | tf_op jit(solution)/shard_map/signal/pallas_call | solution.py:666
  18.6 0.3 collective-permute-start.4
  19.0 1.0 %collective-permute-done.4 = f32[128,128]{1,0:T(8,128)S(1)} collective-permute-done((f32[128,128]{1,0:T(8,128)S(1)}, f32[128,128]{1,0:T(8,128)S(1)}, u32[]{:S(2)}, u32[]{:S(2)}) %collective-permute-start.4) | collective-permute-done | bytes 65568 | tf_op jit(solution)/shard_map/ppermute | solution.py:55
  19.9 1.2 %collective-permute-start.5 = (f32[128,128]{1,0:T(8,128)S(1)}, f32[128,128]{1,0:T(8,128)S(1)}, u32[]{:S(2)}, u32[]{:S(2)}) collective-permute-start(f32[128,128]{1,0:T(8,128)S(1)} %add.12.bc_own), channel_id=1, source_target_pairs={{0,1},{1,0},{2,3},{3,2},{4,5},{5,4},{6,7},{7,6},{8,9},{9,8},{10,11... | collective-permute-start | bytes 196616 | tf_op jit(solution)/shard_map/ppermute | solution.py:55
  21.1 2.7 %gate.1.after_z.z = bf16[2,256,1024]{2,1,0:T(8,128)(2,1)S(1)} custom-call(bf16[288,2048]{1,0:T(8,128)(2,1)S(1)} %get-tuple-element.56.lined_own, bf16[288,2048]{1,0:T(8,128)(2,1)S(1)} %get-tuple-element.57.lined_other, bf16[2048,1024]{1,0:T(8,128)(2,1)S(1)} %get-tuple-element.58.w), custom_call_target="tpu_custom_call" | custom-call | tf_op jit(solution)/shard_map/gate/pallas_call | solution.py:684
  23.8 0.5 collective-permute-done.5.bc_far
  24.3 5.0 %ends.1 = (f32[128,128]{1,0:T(8,128)S(1)}, f32[2,16,1024]{2,1,0:T(8,128)S(1)}, f32[2,16,16,1024]{3,2,1,0:T(8,128)S(1)}, bf16[1024,2048]{1,0:T(8,128)(2,1)S(1)}) custom-call(f32[128,128]{1,0:T(8,128)S(1)} %add.12.bc_own, f32[128,128]{1,0:T(8,128)S(1)} %collective-permute-done.5.bc_far, f32[128,128]{1,0:T(8,128)S(1)} %get-tuple-element.53.weigh, ...), custom_call_target="tpu_custom_call" | custom-call | tf_op jit(solution)/shard_map/ends/pallas_call | solution.py:687
  29.4 2.5 %collective-permute-start.6 = (bf16[2,16,1024]{2,1,0:T(8,128)(2,1)S(1)}, bf16[2,16,1024]{2,1,0:T(8,128)(2,1)S(1)}, u32[]{:S(2)}, u32[]{:S(2)}) collective-permute-start(bf16[2,16,1024]{2,1,0:T(8,128)(2,1)S(1)} %convert_element_type.18), channel_id=1, source_target_pairs={{0,4},{2,6},{4,0},{6,2},{8,12},{10,14},{12,8},{14,10},{16,20},{18,... | collective-permute-start | bytes 196616 | tf_op jit(solution)/shard_map/ppermute | solution.py:55
  31.9 0.2 factors.1
  32.1 2.0 %local.2 = (f32[8,256,128]{2,1,0:T(8,128)S(1)}, bf16[256,256]{1,0:T(8,128)(2,1)S(1)}) custom-call(f32[128,128]{1,0:T(8,128)S(1)} %get-tuple-element.59.after_ends.bc, f32[2,8,256,128]{3,2,1,0:T(8,128)S(1)} %get-tuple-element.54.c, f32[16,1024]{1,0:T(8,128)S(1)} %get-tuple-element.55.decay, f32[16,1024]{1,0:T(8,128)S(1)} %negate_sqrt_fusion.drive, ...), custom_call_target="tpu_custom_call" | custom-call | tf_op jit(solution)/shard_map/local/pallas_call | solution.py:716
  34.0 0.1 collective-permute-done.6.got
  34.2 2.1 %collective-permute-start.7 = (bf16[16,1024]{1,0:T(8,128)(2,1)S(1)}, bf16[16,1024]{1,0:T(8,128)(2,1)S(1)}, u32[]{:S(2)}, u32[]{:S(2)}) collective-permute-start(bf16[16,1024]{1,0:T(8,128)(2,1)S(1)} %get-tuple-element.68.after), channel_id=1, source_target_pairs={{0,8},{2,10},{4,12},{6,14},{8,0},{10,2},{12,4},{14,6},{16,24},{18,... | collective-permute-start | bytes 98312 | tf_op jit(solution)/shard_map/ppermute | solution.py:55
  36.2 2.6 %collective-permute-start.8 = (bf16[16,1024]{1,0:T(8,128)(2,1)S(1)}, bf16[16,1024]{1,0:T(8,128)(2,1)S(1)}, u32[]{:S(2)}, u32[]{:S(2)}) collective-permute-start(bf16[16,1024]{1,0:T(8,128)(2,1)S(1)} %get-tuple-element.73), channel_id=1, source_target_pairs={{0,16},{2,18},{4,20},{6,22},{8,24},{10,26},{12,28},{14,30},{16,0},... | collective-permute-start | bytes 98312 | tf_op jit(solution)/shard_map/ppermute | solution.py:55
  38.8 2.0 %local.3 = (f32[8,256,128]{2,1,0:T(8,128)S(1)}, bf16[256,256]{1,0:T(8,128)(2,1)S(1)}) custom-call(f32[128,128]{1,0:T(8,128)S(1)} %get-tuple-element.59.after_ends.bc, f32[2,8,256,128]{3,2,1,0:T(8,128)S(1)} %get-tuple-element.54.c, f32[16,1024]{1,0:T(8,128)S(1)} %get-tuple-element.55.decay, f32[16,1024]{1,0:T(8,128)S(1)} %negate_sqrt_fusion.drive, ...), custom_call_target="tpu_custom_call" | custom-call | tf_op jit(solution)/shard_map/local/pallas_call | solution.py:716
  40.9 0.4 collective-permute-done.8.rest_1_
  41.3 3.2 %collective-permute-done.9.rest_2_ = bf16[16,1024]{1,0:T(8,128)(2,1)S(1)} collective-permute-done((bf16[16,1024]{1,0:T(8,128)(2,1)S(1)}, bf16[16,1024]{1,0:T(8,128)(2,1)S(1)}, u32[]{:S(2)}, u32[]{:S(2)}) %collective-permute-start.9) | collective-permute-done | bytes 32800 | tf_op jit(solution)/shard_map/ppermute | solution.py:55
  44.5 2.7 %finish.3 = (bf16[128,1024]{1,0:T(8,128)(2,1)S(1)}, bf16[128,1024]{1,0:T(8,128)(2,1)S(1)}) custom-call(bf16[256,1024]{1,0:T(8,128)(2,1)S(1)} %get-tuple-element.60.powers, f32[2,16,1024]{2,1,0:T(8,128)S(1)} %get-tuple-element.61.strides, bf16[2,16,1024]{2,1,0:T(8,128)(2,1)S(1)} %collective-permute-done.6.got, ...), custom_call_target="tpu_custom_call" | custom-call | tf_op jit(solution)/shard_map/finish/pallas_call | solution.py:746
  47.3 0.5 collective-permute-start.11
  47.8 2.1 %finish.2 = (f32[128,1024]{1,0:T(8,128)S(1)}, bf16[2,128,1024]{2,1,0:T(8,128)(2,1)S(1)}) custom-call(bf16[256,1024]{1,0:T(8,128)(2,1)S(1)} %get-tuple-element.60.powers, f32[2,16,1024]{2,1,0:T(8,128)S(1)} %get-tuple-element.61.strides, bf16[2,16,1024]{2,1,0:T(8,128)(2,1)S(1)} %collective-permute-done.6.got, f32[3,2,16,1024]{3,2,1,0:T(8,128)S(1)} %get-tuple-element.63.leads, ...), custom_call_target="tpu_custom_call" | custom-call | tf_op jit(solution)/shard_map/finish/pallas_call | solution.py:754
  50.0 1.6 %collective-permute-start.12 = (bf16[128,1024]{1,0:T(8,128)(2,1)S(1)}, bf16[128,1024]{1,0:T(8,128)(2,1)S(1)}, u32[]{:S(2)}, u32[]{:S(2)}) collective-permute-start(bf16[128,1024]{1,0:T(8,128)(2,1)S(1)} %add_convert_fusion.1.after_first), channel_id=1, source_target_pairs={{0,1},{1,0},{2,3},{3,2},{4,5},{5,4},{6,7},{7,6},{8,9},{9,8},{10,11... | collective-permute-start | bytes 786440 | tf_op jit(solution)/shard_map/ppermute | solution.py:55
  51.6 0.9 %rest.1 = f32[128,1024]{1,0:T(8,128)S(1)} custom-call(bf16[2,128,1024]{2,1,0:T(8,128)(2,1)S(1)} %get-tuple-element.75.gated, bf16[1024,2048]{1,0:T(8,128)(2,1)S(1)} %get-tuple-element.72.w, bf16[128,1024]{1,0:T(8,128)(2,1)S(1)} %add_convert_fusion.1.after_first), custom_call_target="tpu_custom_call" | custom-call | tf_op jit(solution)/shard_map/rest/pallas_call | solution.py:764
  52.5 5.8 %collective-permute-done.12 = bf16[128,1024]{1,0:T(8,128)(2,1)S(1)} collective-permute-done((bf16[128,1024]{1,0:T(8,128)(2,1)S(1)}, bf16[128,1024]{1,0:T(8,128)(2,1)S(1)}, u32[]{:S(2)}, u32[]{:S(2)}) %collective-permute-start.12) | collective-permute-done | bytes 262176 | tf_op jit(solution)/shard_map/ppermute | solution.py:55
  58.3 0.8 %add_convert_fusion = bf16[128,1024]{1,0:T(8,128)(2,1)} fusion(bf16[128,1024]{1,0:T(8,128)(2,1)S(1)} %collective-permute-done.12, f32[128,1024]{1,0:T(8,128)S(1)} %rest.1, bf16[128,1024]{1,0:T(8,128)(2,1)S(1)} %collective-permute-done.11), kind=kLoop, calls=%fused_computation | loop fusion | flops 655360 | bytes 1310720 | tf_op jit(solution)/shard_map/convert_element_type | solution.py:769
  (15 shorter events, 0.3 us)
Async XLA Ops:
  0.0 9.5 %collective-permute-start = (bf16[128,1024]{1,0:T(8,128)(2,1)}, bf16[128,1024]{1,0:T(8,128)(2,1)S(1)}, u32[]{:S(2)}, u32[]{:S(2)}) collective-permute-start(bf16[128,1024]{1,0:T(8,128)(2,1)} %own.1), channel_id=1, source_target_pairs={{0,1},{1,0},{2,3},{3,2},{4,5},{5,4},{6,7},{7,6},{8,9},{9,8},{10,11... | collective-permute-start | bytes 786440 | tf_op jit(solution)/shard_map/ppermute | solution.py:55
  3.8 5.1 %collective-permute-start.1 = (bf16[16,1024]{1,0:T(8,128)(2,1)S(1)}, bf16[16,1024]{1,0:T(8,128)(2,1)S(1)}, u32[]{:S(2)}, u32[]{:S(2)}) collective-permute-start(bf16[16,1024]{1,0:T(8,128)(2,1)S(1)} %rim.1.after), channel_id=1, source_target_pairs={{2,4},{3,5},{6,8},{7,9},{10,12},{11,13},{14,16},{15,17},{18,20},{1... | collective-permute-start | bytes 98312 | tf_op jit(solution)/shard_map/ppermute | solution.py:77
  4.4 4.5 %collective-permute-start.2 = (bf16[16,1024]{1,0:T(8,128)(2,1)S(1)}, bf16[16,1024]{1,0:T(8,128)(2,1)S(1)}, u32[]{:S(2)}, u32[]{:S(2)}) collective-permute-start(bf16[16,1024]{1,0:T(8,128)(2,1)S(1)} %rim.1.after), channel_id=1, source_target_pairs={{3,4},{2,5},{7,8},{6,9},{11,12},{10,13},{15,16},{14,17},{19,20},{1... | collective-permute-start | bytes 98312 | tf_op jit(solution)/shard_map/ppermute | solution.py:77
  5.1 4.4 %copy-start = (bf16[128,1024]{1,0:T(8,128)(2,1)S(1)}, bf16[128,1024]{1,0:T(8,128)(2,1)}, u32[]{:S(2)}) copy-start(bf16[128,1024]{1,0:T(8,128)(2,1)} %own.1) | copy-start | bytes 786436
  10.1 5.7 %collective-permute-start.3 = (bf16[144,2048]{1,0:T(8,128)(2,1)S(1)}, bf16[144,2048]{1,0:T(8,128)(2,1)S(1)}, u32[]{:S(2)}, u32[]{:S(2)}) collective-permute-start(bf16[144,2048]{1,0:T(8,128)(2,1)S(1)} %norm.1.normed), channel_id=1, source_target_pairs={{0,2},{2,0},{4,6},{6,4},{8,10},{10,8},{12,14},{14,12},{16,18},{18,... | collective-permute-start | bytes 1769480 | tf_op jit(solution)/shard_map/ppermute | solution.py:55
  18.6 1.3 %collective-permute-start.4 = (f32[128,128]{1,0:T(8,128)S(1)}, f32[128,128]{1,0:T(8,128)S(1)}, u32[]{:S(2)}, u32[]{:S(2)}) collective-permute-start(f32[128,128]{1,0:T(8,128)S(1)} %get-tuple-element.52), channel_id=1, source_target_pairs={{0,2},{2,0},{4,6},{6,4},{8,10},{10,8},{12,14},{14,12},{16,18},{18,... | collective-permute-start | bytes 196616 | tf_op jit(solution)/shard_map/ppermute | solution.py:55
  19.9 4.4 %collective-permute-start.5 = (f32[128,128]{1,0:T(8,128)S(1)}, f32[128,128]{1,0:T(8,128)S(1)}, u32[]{:S(2)}, u32[]{:S(2)}) collective-permute-start(f32[128,128]{1,0:T(8,128)S(1)} %add.12.bc_own), channel_id=1, source_target_pairs={{0,1},{1,0},{2,3},{3,2},{4,5},{5,4},{6,7},{7,6},{8,9},{9,8},{10,11... | collective-permute-start | bytes 196616 | tf_op jit(solution)/shard_map/ppermute | solution.py:55
  29.4 4.8 %collective-permute-start.6 = (bf16[2,16,1024]{2,1,0:T(8,128)(2,1)S(1)}, bf16[2,16,1024]{2,1,0:T(8,128)(2,1)S(1)}, u32[]{:S(2)}, u32[]{:S(2)}) collective-permute-start(bf16[2,16,1024]{2,1,0:T(8,128)(2,1)S(1)} %convert_element_type.18), channel_id=1, source_target_pairs={{0,4},{2,6},{4,0},{6,2},{8,12},{10,14},{12,8},{14,10},{16,20},{18,... | collective-permute-start | bytes 196616 | tf_op jit(solution)/shard_map/ppermute | solution.py:55
  34.2 6.7 %collective-permute-start.7 = (bf16[16,1024]{1,0:T(8,128)(2,1)S(1)}, bf16[16,1024]{1,0:T(8,128)(2,1)S(1)}, u32[]{:S(2)}, u32[]{:S(2)}) collective-permute-start(bf16[16,1024]{1,0:T(8,128)(2,1)S(1)} %get-tuple-element.68.after), channel_id=1, source_target_pairs={{0,8},{2,10},{4,12},{6,14},{8,0},{10,2},{12,4},{14,6},{16,24},{18,... | collective-permute-start | bytes 98312 | tf_op jit(solution)/shard_map/ppermute | solution.py:55
  36.2 5.1 %collective-permute-start.8 = (bf16[16,1024]{1,0:T(8,128)(2,1)S(1)}, bf16[16,1024]{1,0:T(8,128)(2,1)S(1)}, u32[]{:S(2)}, u32[]{:S(2)}) collective-permute-start(bf16[16,1024]{1,0:T(8,128)(2,1)S(1)} %get-tuple-element.73), channel_id=1, source_target_pairs={{0,16},{2,18},{4,20},{6,22},{8,24},{10,26},{12,28},{14,30},{16,0},... | collective-permute-start | bytes 98312 | tf_op jit(solution)/shard_map/ppermute | solution.py:55
  38.8 5.7 %collective-permute-start.9 = (bf16[16,1024]{1,0:T(8,128)(2,1)S(1)}, bf16[16,1024]{1,0:T(8,128)(2,1)S(1)}, u32[]{:S(2)}, u32[]{:S(2)}) collective-permute-start(bf16[16,1024]{1,0:T(8,128)(2,1)S(1)} %get-tuple-element.74), channel_id=1, source_target_pairs={{0,24},{2,26},{4,28},{6,30},{8,16},{10,18},{12,20},{14,22},{16,8},... | collective-permute-start | bytes 98312 | tf_op jit(solution)/shard_map/ppermute | solution.py:55
  47.3 2.6 %collective-permute-start.10 = (bf16[128,1024]{1,0:T(8,128)(2,1)S(1)}, bf16[128,1024]{1,0:T(8,128)(2,1)S(1)}, u32[]{:S(2)}, u32[]{:S(2)}) collective-permute-start(bf16[128,1024]{1,0:T(8,128)(2,1)S(1)} %get-tuple-element.77), channel_id=1, source_target_pairs={{0,2},{2,0},{4,6},{6,4},{8,10},{10,8},{12,14},{14,12},{16,18},{18,... | collective-permute-start | bytes 786440 | tf_op jit(solution)/shard_map/ppermute | solution.py:55
  47.3 5.1 %collective-permute-start.11 = (bf16[128,1024]{1,0:T(8,128)(2,1)S(1)}, bf16[128,1024]{1,0:T(8,128)(2,1)S(1)}, u32[]{:S(2)}, u32[]{:S(2)}) collective-permute-start(bf16[128,1024]{1,0:T(8,128)(2,1)S(1)} %get-tuple-element.78), channel_id=1, source_target_pairs={{0,2},{2,0},{4,6},{6,4},{8,10},{10,8},{12,14},{14,12},{16,18},{18,... | collective-permute-start | bytes 786440 | tf_op jit(solution)/shard_map/ppermute | solution.py:55
  50.0 8.4 %collective-permute-start.12 = (bf16[128,1024]{1,0:T(8,128)(2,1)S(1)}, bf16[128,1024]{1,0:T(8,128)(2,1)S(1)}, u32[]{:S(2)}, u32[]{:S(2)}) collective-permute-start(bf16[128,1024]{1,0:T(8,128)(2,1)S(1)} %add_convert_fusion.1.after_first), channel_id=1, source_target_pairs={{0,1},{1,0},{2,3},{3,2},{4,5},{5,4},{6,7},{7,6},{8,9},{9,8},{10,11... | collective-permute-start | bytes 786440 | tf_op jit(solution)/shard_map/ppermute | solution.py:55

commit v5 on v4

--- a/solution.py
+++ b/solution.py
@@ -336,22 +336,25 @@
     return [ref[h * SUBS : (h + 1) * SUBS, tile(t)] for t in range(count) for h in range(2)]
 
 
-def spread(bc, wide, stream):
+def spread(bc, wide):
     rows = bc.shape[1]
-    ones = jnp.ones((rows, LANES), bf16)
-    lanes = lax.broadcasted_iota(jnp.int32, (STATE, rows), 1)
+    across = STREAMS * LANES
+    r = lax.broadcasted_iota(jnp.int32, (STREAMS * rows, across), 0)
+    q = lax.broadcasted_iota(jnp.int32, (STREAMS * rows, across), 1)
+    ones = jnp.where(r // rows == q // LANES, 1.0, 0.0).astype(bf16)
+    lanes = lax.broadcasted_iota(jnp.int32, (STATE, STREAMS * rows), 1) & (rows - 1)
     group = 8
     for half in range(HALVES):
-        first = 2 * STATE * (2 * half + stream)
-        entries = bc[first : first + STATE, :]
+        firsts = [2 * STATE * (2 * half + s) for s in range(STREAMS)]
+        entries = jnp.concatenate([bc[low : low + STATE, :] for low in firsts], axis=1)
         for j in range(0, rows, group):
             alone = jnp.concatenate(
                 [jnp.where(lanes == j + i, entries, 0.0).astype(bf16) for i in range(group)], axis=0
             )
             at = (half * rows + j) * STATE
-            wide[stream, at : at + group * STATE, :] = jnp.dot(
-                alone, ones, preferred_element_type=f32
-            )
+            found = jnp.dot(alone, ones, preferred_element_type=f32)
+            for s in range(STREAMS):
+                wide[s, at : at + group * STATE, :] = found[:, tile(s)]
 
 
 def end_kernel(
@@ -366,8 +369,7 @@
     length = 2 * rows
     count = c.shape[1]
     bc_out[...] = (bc_own[...] + bc_far[...]) * weigh[...]
-    for s in range(STREAMS):
-        spread(bc_out, wide, s)
+    spread(bc_out, wide)
     a = tiles_of(decay, count)
 
     def chunk(n, state):

time: 59.3 us -> 59.3 us (level)
  no operation moved by 1% of the time
where the time goes in v5:
time: 59.3 us; the launch traced here: 59.1 us
  Pallas kernels  27.2 us (46%)
  starting transfers between devices  19.1 us (32%)
  waiting for transfers between devices  11.6 us (20%)
  other arithmetic  0.93 us (2%)
    ppermute x11, starting transfers between devices, swap(): return lax.ppermute(block, axis, [(i, i ^ apart) for i in range(count)])  17.8 us
    ppermute x11, waiting for transfers between devices, swap(): return lax.ppermute(block, axis, [(i, i ^ apart) for i in range(count)])  11.6 us
    pallas_call x1, Pallas kernels, body(): call(end_kernel, 'ends', [shaped((4 * 2 * STATE, rows)), shaped((STREAMS,...  5.02 us
    pallas_call x2, Pallas kernels, local(): call(functools.partial(local_kernel, s), 'local', [shaped(by_tile), shape...  3.97 us
    pallas_call x1, Pallas kernels, body(): call(init_kernel, 'init', [shaped((width, inner), bf16), shaped((width, i...  3.78 us
    pallas_call x1, Pallas kernels, body(): call(signal_kernel, 'signal', [lined, shaped((STREAMS, tiles, length, LAN...  2.8 us
    pallas_call x1, Pallas kernels, body(): call(functools.partial(finish_kernel, False), 'finish', [shaped(half_widt...  2.7 us
    pallas_call x1, Pallas kernels, body(): call(gate_kernel, 'gate', shaped((STREAMS, length, inner), bf16), [WHOLE]...  2.65 us
  transfers between devices with their start and end apart: 13, of which 7 were waited for; matrix products, arithmetic and copies ran while one was open for 0% of the time, Pallas kernels for 27%

profile of v5, /device:TPU:0, one launch (start us, length us, event | category | flops | bytes accessed | tf_op | source)
XLA Modules:
  0.0 59.1 jit_solution(12526198652740278671)
XLA Ops:
  0.0 3.0 %collective-permute-start = (bf16[128,1024]{1,0:T(8,128)(2,1)}, bf16[128,1024]{1,0:T(8,128)(2,1)S(1)}, u32[]{:S(2)}, u32[]{:S(2)}) collective-permute-start(bf16[128,1024]{1,0:T(8,128)(2,1)} %own.1), channel_id=1, source_target_pairs={{0,1},{1,0},{2,3},{3,2},{4,5},{5,4},{6,7},{7,6},{8,9},{9,8},{10,11... | collective-permute-start | bytes 786440 | tf_op jit(solution)/shard_map/ppermute | solution.py:55
  3.0 0.8 %rim.1.after = bf16[16,1024]{1,0:T(8,128)(2,1)S(1)} custom-call(bf16[128,1024]{1,0:T(8,128)(2,1)} %own.1), custom_call_target="tpu_custom_call" | custom-call | tf_op jit(solution)/shard_map/rim/pallas_call | solution.py:599
  3.8 0.7 %collective-permute-start.1 = (bf16[16,1024]{1,0:T(8,128)(2,1)S(1)}, bf16[16,1024]{1,0:T(8,128)(2,1)S(1)}, u32[]{:S(2)}, u32[]{:S(2)}) collective-permute-start(bf16[16,1024]{1,0:T(8,128)(2,1)S(1)} %rim.1.after), channel_id=1, source_target_pairs={{2,4},{3,5},{6,8},{7,9},{10,12},{11,13},{14,16},{15,17},{18,20},{1... | collective-permute-start | bytes 98312 | tf_op jit(solution)/shard_map/ppermute | solution.py:77
  4.4 0.7 %collective-permute-start.2 = (bf16[16,1024]{1,0:T(8,128)(2,1)S(1)}, bf16[16,1024]{1,0:T(8,128)(2,1)S(1)}, u32[]{:S(2)}, u32[]{:S(2)}) collective-permute-start(bf16[16,1024]{1,0:T(8,128)(2,1)S(1)} %rim.1.after), channel_id=1, source_target_pairs={{3,4},{2,5},{7,8},{6,9},{11,12},{10,13},{15,16},{14,17},{19,20},{1... | collective-permute-start | bytes 98312 | tf_op jit(solution)/shard_map/ppermute | solution.py:77
  5.1 3.8 %init.1 = (bf16[2048,1024]{1,0:T(8,128)(2,1)S(1)}, bf16[2048,1024]{1,0:T(8,128)(2,1)S(1)}, f32[4,1024]{1,0:T(4,128)S(1)}, f32[1,1024]{1,0:T(1,128)S(1)}, bf16[32...) custom-call(s32[2,8]{1,0:T(2,128)} %bitcast.9, ...), custom_call_target="tpu_custom_call" | custom-call | tf_op jit(solution)/shard_map/init/pallas_call | solution.py:613
  8.9 0.5 collective-permute-done.far
  9.5 0.6 %norm.1.normed = bf16[144,2048]{1,0:T(8,128)(2,1)S(1)} custom-call(bf16[128,1024]{1,0:T(8,128)(2,1)S(1)} %copy-done, bf16[128,1024]{1,0:T(8,128)(2,1)S(1)} %collective-permute-done.far, bf16[16,1024]{1,0:T(8,128)(2,1)S(1)} %collective-permute-done.1.own_rim, bf16[16,1024]{1,0:T(8,128)(2,1)S(1)} %collective-permute-done.2.far_rim, ...), custom_call_target="tpu_custom_call" | custom-call | tf_op jit(solution)/shard_map/norm/pallas_call | solution.py:656
  10.1 4.0 %collective-permute-start.3 = (bf16[144,2048]{1,0:T(8,128)(2,1)S(1)}, bf16[144,2048]{1,0:T(8,128)(2,1)S(1)}, u32[]{:S(2)}, u32[]{:S(2)}) collective-permute-start(bf16[144,2048]{1,0:T(8,128)(2,1)S(1)} %norm.1.normed), channel_id=1, source_target_pairs={{0,2},{2,0},{4,6},{6,4},{8,10},{10,8},{12,14},{14,12},{16,18},{18,... | collective-permute-start | bytes 1769480 | tf_op jit(solution)/shard_map/ppermute | solution.py:55
  14.1 1.7 %own_signal.1 = (bf16[288,2048]{1,0:T(8,128)(2,1)S(1)}, f32[288,1024]{1,0:T(8,128)S(1)}) custom-call(bf16[144,2048]{1,0:T(8,128)(2,1)S(1)} %norm.1.normed, bf16[2048,1024]{1,0:T(8,128)(2,1)S(1)} %get-tuple-element.47.w), custom_call_target="tpu_custom_call" | custom-call | tf_op jit(solution)/shard_map/own_signal/pallas_call | solution.py:662
  15.8 2.8 %signal.1 = (bf16[288,2048]{1,0:T(8,128)(2,1)S(1)}, f32[2,8,256,128]{3,2,1,0:T(8,128)S(1)}, f32[128,128]{1,0:T(8,128)S(1)}) custom-call(bf16[144,2048]{1,0:T(8,128)(2,1)S(1)} %collective-permute-done.3.normed, f32[288,1024]{1,0:T(8,128)S(1)} %get-tuple-element.48.x_own, bf16[2048,1024]{1,0:T(8,128)(2,1)S(1)} %get-tuple-element.47.w, ...), custom_call_target="tpu_custom_call" | custom-call | tf_op jit(solution)/shard_map/signal/pallas_call | solution.py:668
  18.6 0.3 collective-permute-start.4
  19.0 1.0 %collective-permute-done.4 = f32[128,128]{1,0:T(8,128)S(1)} collective-permute-done((f32[128,128]{1,0:T(8,128)S(1)}, f32[128,128]{1,0:T(8,128)S(1)}, u32[]{:S(2)}, u32[]{:S(2)}) %collective-permute-start.4) | collective-permute-done | bytes 65568 | tf_op jit(solution)/shard_map/ppermute | solution.py:55
  19.9 1.2 %collective-permute-start.5 = (f32[128,128]{1,0:T(8,128)S(1)}, f32[128,128]{1,0:T(8,128)S(1)}, u32[]{:S(2)}, u32[]{:S(2)}) collective-permute-start(f32[128,128]{1,0:T(8,128)S(1)} %add.12.bc_own), channel_id=1, source_target_pairs={{0,1},{1,0},{2,3},{3,2},{4,5},{5,4},{6,7},{7,6},{8,9},{9,8},{10,11... | collective-permute-start | bytes 196616 | tf_op jit(solution)/shard_map/ppermute | solution.py:55
  21.1 2.7 %gate.1.after_z.z = bf16[2,256,1024]{2,1,0:T(8,128)(2,1)S(1)} custom-call(bf16[288,2048]{1,0:T(8,128)(2,1)S(1)} %get-tuple-element.56.lined_own, bf16[288,2048]{1,0:T(8,128)(2,1)S(1)} %get-tuple-element.57.lined_other, bf16[2048,1024]{1,0:T(8,128)(2,1)S(1)} %get-tuple-element.58.w), custom_call_target="tpu_custom_call" | custom-call | tf_op jit(solution)/shard_map/gate/pallas_call | solution.py:686
  23.8 0.5 collective-permute-done.5.bc_far
  24.3 5.0 %ends.1 = (f32[128,128]{1,0:T(8,128)S(1)}, f32[2,16,1024]{2,1,0:T(8,128)S(1)}, f32[2,16,16,1024]{3,2,1,0:T(8,128)S(1)}, bf16[1024,2048]{1,0:T(8,128)(2,1)S(1)}) custom-call(f32[128,128]{1,0:T(8,128)S(1)} %add.12.bc_own, f32[128,128]{1,0:T(8,128)S(1)} %collective-permute-done.5.bc_far, f32[128,128]{1,0:T(8,128)S(1)} %get-tuple-element.53.weigh, ...), custom_call_target="tpu_custom_call" | custom-call | tf_op jit(solution)/shard_map/ends/pallas_call | solution.py:689
  29.3 2.5 %collective-permute-start.6 = (bf16[2,16,1024]{2,1,0:T(8,128)(2,1)S(1)}, bf16[2,16,1024]{2,1,0:T(8,128)(2,1)S(1)}, u32[]{:S(2)}, u32[]{:S(2)}) collective-permute-start(bf16[2,16,1024]{2,1,0:T(8,128)(2,1)S(1)} %convert_element_type.18), channel_id=1, source_target_pairs={{0,4},{2,6},{4,0},{6,2},{8,12},{10,14},{12,8},{14,10},{16,20},{18,... | collective-permute-start | bytes 196616 | tf_op jit(solution)/shard_map/ppermute | solution.py:55
  31.8 0.2 factors.1
  32.0 2.0 %local.2 = (f32[8,256,128]{2,1,0:T(8,128)S(1)}, bf16[256,256]{1,0:T(8,128)(2,1)S(1)}) custom-call(f32[128,128]{1,0:T(8,128)S(1)} %get-tuple-element.59.after_ends.bc, f32[2,8,256,128]{3,2,1,0:T(8,128)S(1)} %get-tuple-element.54.c, f32[16,1024]{1,0:T(8,128)S(1)} %get-tuple-element.55.decay, f32[16,1024]{1,0:T(8,128)S(1)} %negate_sqrt_fusion.drive, ...), custom_call_target="tpu_custom_call" | custom-call | tf_op jit(solution)/shard_map/local/pallas_call | solution.py:718
  34.0 0.1 collective-permute-done.6.got
  34.1 2.1 %collective-permute-start.7 = (bf16[16,1024]{1,0:T(8,128)(2,1)S(1)}, bf16[16,1024]{1,0:T(8,128)(2,1)S(1)}, u32[]{:S(2)}, u32[]{:S(2)}) collective-permute-start(bf16[16,1024]{1,0:T(8,128)(2,1)S(1)} %get-tuple-element.68.after), channel_id=1, source_target_pairs={{0,8},{2,10},{4,12},{6,14},{8,0},{10,2},{12,4},{14,6},{16,24},{18,... | collective-permute-start | bytes 98312 | tf_op jit(solution)/shard_map/ppermute | solution.py:55
  36.2 2.6 %collective-permute-start.8 = (bf16[16,1024]{1,0:T(8,128)(2,1)S(1)}, bf16[16,1024]{1,0:T(8,128)(2,1)S(1)}, u32[]{:S(2)}, u32[]{:S(2)}) collective-permute-start(bf16[16,1024]{1,0:T(8,128)(2,1)S(1)} %get-tuple-element.73), channel_id=1, source_target_pairs={{0,16},{2,18},{4,20},{6,22},{8,24},{10,26},{12,28},{14,30},{16,0},... | collective-permute-start | bytes 98312 | tf_op jit(solution)/shard_map/ppermute | solution.py:55
  38.8 2.0 %local.3 = (f32[8,256,128]{2,1,0:T(8,128)S(1)}, bf16[256,256]{1,0:T(8,128)(2,1)S(1)}) custom-call(f32[128,128]{1,0:T(8,128)S(1)} %get-tuple-element.59.after_ends.bc, f32[2,8,256,128]{3,2,1,0:T(8,128)S(1)} %get-tuple-element.54.c, f32[16,1024]{1,0:T(8,128)S(1)} %get-tuple-element.55.decay, f32[16,1024]{1,0:T(8,128)S(1)} %negate_sqrt_fusion.drive, ...), custom_call_target="tpu_custom_call" | custom-call | tf_op jit(solution)/shard_map/local/pallas_call | solution.py:718
  40.8 0.4 collective-permute-done.8.rest_1_
  41.3 3.2 %collective-permute-done.9.rest_2_ = bf16[16,1024]{1,0:T(8,128)(2,1)S(1)} collective-permute-done((bf16[16,1024]{1,0:T(8,128)(2,1)S(1)}, bf16[16,1024]{1,0:T(8,128)(2,1)S(1)}, u32[]{:S(2)}, u32[]{:S(2)}) %collective-permute-start.9) | collective-permute-done | bytes 32800 | tf_op jit(solution)/shard_map/ppermute | solution.py:55
  44.5 2.7 %finish.3 = (bf16[128,1024]{1,0:T(8,128)(2,1)S(1)}, bf16[128,1024]{1,0:T(8,128)(2,1)S(1)}) custom-call(bf16[256,1024]{1,0:T(8,128)(2,1)S(1)} %get-tuple-element.60.powers, f32[2,16,1024]{2,1,0:T(8,128)S(1)} %get-tuple-element.61.strides, bf16[2,16,1024]{2,1,0:T(8,128)(2,1)S(1)} %collective-permute-done.6.got, ...), custom_call_target="tpu_custom_call" | custom-call | tf_op jit(solution)/shard_map/finish/pallas_call | solution.py:748
  47.3 0.5 collective-permute-start.11
  47.8 2.1 %finish.2 = (f32[128,1024]{1,0:T(8,128)S(1)}, bf16[2,128,1024]{2,1,0:T(8,128)(2,1)S(1)}) custom-call(bf16[256,1024]{1,0:T(8,128)(2,1)S(1)} %get-tuple-element.60.powers, f32[2,16,1024]{2,1,0:T(8,128)S(1)} %get-tuple-element.61.strides, bf16[2,16,1024]{2,1,0:T(8,128)(2,1)S(1)} %collective-permute-done.6.got, f32[3,2,16,1024]{3,2,1,0:T(8,128)S(1)} %get-tuple-element.63.leads, ...), custom_call_target="tpu_custom_call" | custom-call | tf_op jit(solution)/shard_map/finish/pallas_call | solution.py:756
  49.9 1.6 %collective-permute-start.12 = (bf16[128,1024]{1,0:T(8,128)(2,1)S(1)}, bf16[128,1024]{1,0:T(8,128)(2,1)S(1)}, u32[]{:S(2)}, u32[]{:S(2)}) collective-permute-start(bf16[128,1024]{1,0:T(8,128)(2,1)S(1)} %add_convert_fusion.1.after_first), channel_id=1, source_target_pairs={{0,1},{1,0},{2,3},{3,2},{4,5},{5,4},{6,7},{7,6},{8,9},{9,8},{10,11... | collective-permute-start | bytes 786440 | tf_op jit(solution)/shard_map/ppermute | solution.py:55
  51.5 0.9 %rest.1 = f32[128,1024]{1,0:T(8,128)S(1)} custom-call(bf16[2,128,1024]{2,1,0:T(8,128)(2,1)S(1)} %get-tuple-element.75.gated, bf16[1024,2048]{1,0:T(8,128)(2,1)S(1)} %get-tuple-element.72.w, bf16[128,1024]{1,0:T(8,128)(2,1)S(1)} %add_convert_fusion.1.after_first), custom_call_target="tpu_custom_call" | custom-call | tf_op jit(solution)/shard_map/rest/pallas_call | solution.py:766
  52.5 5.8 %collective-permute-done.12 = bf16[128,1024]{1,0:T(8,128)(2,1)S(1)} collective-permute-done((bf16[128,1024]{1,0:T(8,128)(2,1)S(1)}, bf16[128,1024]{1,0:T(8,128)(2,1)S(1)}, u32[]{:S(2)}, u32[]{:S(2)}) %collective-permute-start.12) | collective-permute-done | bytes 262176 | tf_op jit(solution)/shard_map/ppermute | solution.py:55
  58.3 0.8 %add_convert_fusion = bf16[128,1024]{1,0:T(8,128)(2,1)} fusion(bf16[128,1024]{1,0:T(8,128)(2,1)S(1)} %collective-permute-done.12, f32[128,1024]{1,0:T(8,128)S(1)} %rest.1, bf16[128,1024]{1,0:T(8,128)(2,1)S(1)} %collective-permute-done.11), kind=kLoop, calls=%fused_computation | loop fusion | flops 655360 | bytes 1310720 | tf_op jit(solution)/shard_map/convert_element_type | solution.py:771
  (15 shorter events, 0.3 us)
Async XLA Ops:
  0.0 9.5 %collective-permute-start = (bf16[128,1024]{1,0:T(8,128)(2,1)}, bf16[128,1024]{1,0:T(8,128)(2,1)S(1)}, u32[]{:S(2)}, u32[]{:S(2)}) collective-permute-start(bf16[128,1024]{1,0:T(8,128)(2,1)} %own.1), channel_id=1, source_target_pairs={{0,1},{1,0},{2,3},{3,2},{4,5},{5,4},{6,7},{7,6},{8,9},{9,8},{10,11... | collective-permute-start | bytes 786440 | tf_op jit(solution)/shard_map/ppermute | solution.py:55
  3.8 5.1 %collective-permute-start.1 = (bf16[16,1024]{1,0:T(8,128)(2,1)S(1)}, bf16[16,1024]{1,0:T(8,128)(2,1)S(1)}, u32[]{:S(2)}, u32[]{:S(2)}) collective-permute-start(bf16[16,1024]{1,0:T(8,128)(2,1)S(1)} %rim.1.after), channel_id=1, source_target_pairs={{2,4},{3,5},{6,8},{7,9},{10,12},{11,13},{14,16},{15,17},{18,20},{1... | collective-permute-start | bytes 98312 | tf_op jit(solution)/shard_map/ppermute | solution.py:77
  4.4 4.5 %collective-permute-start.2 = (bf16[16,1024]{1,0:T(8,128)(2,1)S(1)}, bf16[16,1024]{1,0:T(8,128)(2,1)S(1)}, u32[]{:S(2)}, u32[]{:S(2)}) collective-permute-start(bf16[16,1024]{1,0:T(8,128)(2,1)S(1)} %rim.1.after), channel_id=1, source_target_pairs={{3,4},{2,5},{7,8},{6,9},{11,12},{10,13},{15,16},{14,17},{19,20},{1... | collective-permute-start | bytes 98312 | tf_op jit(solution)/shard_map/ppermute | solution.py:77
  5.1 4.4 %copy-start = (bf16[128,1024]{1,0:T(8,128)(2,1)S(1)}, bf16[128,1024]{1,0:T(8,128)(2,1)}, u32[]{:S(2)}) copy-start(bf16[128,1024]{1,0:T(8,128)(2,1)} %own.1) | copy-start | bytes 786436
  10.1 5.7 %collective-permute-start.3 = (bf16[144,2048]{1,0:T(8,128)(2,1)S(1)}, bf16[144,2048]{1,0:T(8,128)(2,1)S(1)}, u32[]{:S(2)}, u32[]{:S(2)}) collective-permute-start(bf16[144,2048]{1,0:T(8,128)(2,1)S(1)} %norm.1.normed), channel_id=1, source_target_pairs={{0,2},{2,0},{4,6},{6,4},{8,10},{10,8},{12,14},{14,12},{16,18},{18,... | collective-permute-start | bytes 1769480 | tf_op jit(solution)/shard_map/ppermute | solution.py:55
  18.6 1.3 %collective-permute-start.4 = (f32[128,128]{1,0:T(8,128)S(1)}, f32[128,128]{1,0:T(8,128)S(1)}, u32[]{:S(2)}, u32[]{:S(2)}) collective-permute-start(f32[128,128]{1,0:T(8,128)S(1)} %get-tuple-element.52), channel_id=1, source_target_pairs={{0,2},{2,0},{4,6},{6,4},{8,10},{10,8},{12,14},{14,12},{16,18},{18,... | collective-permute-start | bytes 196616 | tf_op jit(solution)/shard_map/ppermute | solution.py:55
  19.9 4.4 %collective-permute-start.5 = (f32[128,128]{1,0:T(8,128)S(1)}, f32[128,128]{1,0:T(8,128)S(1)}, u32[]{:S(2)}, u32[]{:S(2)}) collective-permute-start(f32[128,128]{1,0:T(8,128)S(1)} %add.12.bc_own), channel_id=1, source_target_pairs={{0,1},{1,0},{2,3},{3,2},{4,5},{5,4},{6,7},{7,6},{8,9},{9,8},{10,11... | collective-permute-start | bytes 196616 | tf_op jit(solution)/shard_map/ppermute | solution.py:55
  29.3 4.8 %collective-permute-start.6 = (bf16[2,16,1024]{2,1,0:T(8,128)(2,1)S(1)}, bf16[2,16,1024]{2,1,0:T(8,128)(2,1)S(1)}, u32[]{:S(2)}, u32[]{:S(2)}) collective-permute-start(bf16[2,16,1024]{2,1,0:T(8,128)(2,1)S(1)} %convert_element_type.18), channel_id=1, source_target_pairs={{0,4},{2,6},{4,0},{6,2},{8,12},{10,14},{12,8},{14,10},{16,20},{18,... | collective-permute-start | bytes 196616 | tf_op jit(solution)/shard_map/ppermute | solution.py:55
  34.1 6.7 %collective-permute-start.7 = (bf16[16,1024]{1,0:T(8,128)(2,1)S(1)}, bf16[16,1024]{1,0:T(8,128)(2,1)S(1)}, u32[]{:S(2)}, u32[]{:S(2)}) collective-permute-start(bf16[16,1024]{1,0:T(8,128)(2,1)S(1)} %get-tuple-element.68.after), channel_id=1, source_target_pairs={{0,8},{2,10},{4,12},{6,14},{8,0},{10,2},{12,4},{14,6},{16,24},{18,... | collective-permute-start | bytes 98312 | tf_op jit(solution)/shard_map/ppermute | solution.py:55
  36.2 5.1 %collective-permute-start.8 = (bf16[16,1024]{1,0:T(8,128)(2,1)S(1)}, bf16[16,1024]{1,0:T(8,128)(2,1)S(1)}, u32[]{:S(2)}, u32[]{:S(2)}) collective-permute-start(bf16[16,1024]{1,0:T(8,128)(2,1)S(1)} %get-tuple-element.73), channel_id=1, source_target_pairs={{0,16},{2,18},{4,20},{6,22},{8,24},{10,26},{12,28},{14,30},{16,0},... | collective-permute-start | bytes 98312 | tf_op jit(solution)/shard_map/ppermute | solution.py:55
  38.8 5.7 %collective-permute-start.9 = (bf16[16,1024]{1,0:T(8,128)(2,1)S(1)}, bf16[16,1024]{1,0:T(8,128)(2,1)S(1)}, u32[]{:S(2)}, u32[]{:S(2)}) collective-permute-start(bf16[16,1024]{1,0:T(8,128)(2,1)S(1)} %get-tuple-element.74), channel_id=1, source_target_pairs={{0,24},{2,26},{4,28},{6,30},{8,16},{10,18},{12,20},{14,22},{16,8},... | collective-permute-start | bytes 98312 | tf_op jit(solution)/shard_map/ppermute | solution.py:55
  47.2 2.6 %collective-permute-start.10 = (bf16[128,1024]{1,0:T(8,128)(2,1)S(1)}, bf16[128,1024]{1,0:T(8,128)(2,1)S(1)}, u32[]{:S(2)}, u32[]{:S(2)}) collective-permute-start(bf16[128,1024]{1,0:T(8,128)(2,1)S(1)} %get-tuple-element.77), channel_id=1, source_target_pairs={{0,2},{2,0},{4,6},{6,4},{8,10},{10,8},{12,14},{14,12},{16,18},{18,... | collective-permute-start | bytes 786440 | tf_op jit(solution)/shard_map/ppermute | solution.py:55
  47.3 5.1 %collective-permute-start.11 = (bf16[128,1024]{1,0:T(8,128)(2,1)S(1)}, bf16[128,1024]{1,0:T(8,128)(2,1)S(1)}, u32[]{:S(2)}, u32[]{:S(2)}) collective-permute-start(bf16[128,1024]{1,0:T(8,128)(2,1)S(1)} %get-tuple-element.78), channel_id=1, source_target_pairs={{0,2},{2,0},{4,6},{6,4},{8,10},{10,8},{12,14},{14,12},{16,18},{18,... | collective-permute-start | bytes 786440 | tf_op jit(solution)/shard_map/ppermute | solution.py:55
  49.9 8.4 %collective-permute-start.12 = (bf16[128,1024]{1,0:T(8,128)(2,1)S(1)}, bf16[128,1024]{1,0:T(8,128)(2,1)S(1)}, u32[]{:S(2)}, u32[]{:S(2)}) collective-permute-start(bf16[128,1024]{1,0:T(8,128)(2,1)S(1)} %add_convert_fusion.1.after_first), channel_id=1, source_target_pairs={{0,1},{1,0},{2,3},{3,2},{4,5},{5,4},{6,7},{7,6},{8,9},{9,8},{10,11... | collective-permute-start | bytes 786440 | tf_op jit(solution)/shard_map/ppermute | solution.py:55

commit v6 on v4

--- a/solution.py
+++ b/solution.py
@@ -494,8 +494,8 @@
         (got[s].astype(f32) * first_step[0, s] + ends[s] * first_step[1, s]).astype(bf16)
         for s in range(STREAMS)
     ]
-    for m, send in enumerate(sends):
-        _, _, below = between(chip, m + 1)
+    for k, send in enumerate(sends):
+        _, _, below = between(chip, len(sends) - k)
         send[...] = jnp.where(below, group[1], group[0])
 
 
@@ -735,7 +735,7 @@
             [shaped(channels, bf16)] * (pairs - 1),
             [WHOLE] * 3 + [later],
         )(ends, got, first_step, y_f)
-        arrived = [swap(send, "seq", 4 * m) for m, send in enumerate(sends, 1)]
+        arrived = [swap(send, "seq", 4 * (pairs - 1 - k)) for k, send in enumerate(sends)][::-1]
     y_b, readout_b = local(1, sends[0] if pairs > 1 else got)
 
     operands = (

time: 59.3 us -> 59.3 us (level)
  no operation moved by 1% of the time
where the time goes in v6:
time: 59.3 us; the launch traced here: 59.1 us
  Pallas kernels  27.2 us (46%)
  starting transfers between devices  19.1 us (32%)
  waiting for transfers between devices  11.6 us (20%)
  other arithmetic  0.93 us (2%)
    ppermute x11, starting transfers between devices, swap(): return lax.ppermute(block, axis, [(i, i ^ apart) for i in range(count)])  17.8 us
    ppermute x11, waiting for transfers between devices, swap(): return lax.ppermute(block, axis, [(i, i ^ apart) for i in range(count)])  11.6 us
    pallas_call x1, Pallas kernels, body(): call(end_kernel, 'ends', [shaped((4 * 2 * STATE, rows)), shaped((STREAMS,...  5.05 us
    pallas_call x2, Pallas kernels, local(): call(functools.partial(local_kernel, s), 'local', [shaped(by_tile), shape...  3.97 us
    pallas_call x1, Pallas kernels, body(): call(init_kernel, 'init', [shaped((width, inner), bf16), shaped((width, i...  3.78 us
    pallas_call x1, Pallas kernels, body(): call(signal_kernel, 'signal', [lined, shaped((STREAMS, tiles, length, LAN...  2.8 us
    pallas_call x1, Pallas kernels, body(): call(functools.partial(finish_kernel, False), 'finish', [shaped(half_widt...  2.7 us
    pallas_call x1, Pallas kernels, body(): call(gate_kernel, 'gate', shaped((STREAMS, length, inner), bf16), [WHOLE]...  2.65 us
  transfers between devices with their start and end apart: 13, of which 7 were waited for; matrix products, arithmetic and copies ran while one was open for 0% of the time, Pallas kernels for 27%

profile of v6, /device:TPU:0, one launch (start us, length us, event | category | flops | bytes accessed | tf_op | source)
XLA Modules:
  0.0 59.1 jit_solution(16961986856316564344)
XLA Ops:
  0.0 3.0 %collective-permute-start = (bf16[128,1024]{1,0:T(8,128)(2,1)}, bf16[128,1024]{1,0:T(8,128)(2,1)S(1)}, u32[]{:S(2)}, u32[]{:S(2)}) collective-permute-start(bf16[128,1024]{1,0:T(8,128)(2,1)} %own.1), channel_id=1, source_target_pairs={{0,1},{1,0},{2,3},{3,2},{4,5},{5,4},{6,7},{7,6},{8,9},{9,8},{10,11... | collective-permute-start | bytes 786440 | tf_op jit(solution)/shard_map/ppermute | solution.py:55
  3.0 0.8 %rim.1.after = bf16[16,1024]{1,0:T(8,128)(2,1)S(1)} custom-call(bf16[128,1024]{1,0:T(8,128)(2,1)} %own.1), custom_call_target="tpu_custom_call" | custom-call | tf_op jit(solution)/shard_map/rim/pallas_call | solution.py:597
  3.8 0.7 %collective-permute-start.1 = (bf16[16,1024]{1,0:T(8,128)(2,1)S(1)}, bf16[16,1024]{1,0:T(8,128)(2,1)S(1)}, u32[]{:S(2)}, u32[]{:S(2)}) collective-permute-start(bf16[16,1024]{1,0:T(8,128)(2,1)S(1)} %rim.1.after), channel_id=1, source_target_pairs={{2,4},{3,5},{6,8},{7,9},{10,12},{11,13},{14,16},{15,17},{18,20},{1... | collective-permute-start | bytes 98312 | tf_op jit(solution)/shard_map/ppermute | solution.py:77
  4.4 0.7 %collective-permute-start.2 = (bf16[16,1024]{1,0:T(8,128)(2,1)S(1)}, bf16[16,1024]{1,0:T(8,128)(2,1)S(1)}, u32[]{:S(2)}, u32[]{:S(2)}) collective-permute-start(bf16[16,1024]{1,0:T(8,128)(2,1)S(1)} %rim.1.after), channel_id=1, source_target_pairs={{3,4},{2,5},{7,8},{6,9},{11,12},{10,13},{15,16},{14,17},{19,20},{1... | collective-permute-start | bytes 98312 | tf_op jit(solution)/shard_map/ppermute | solution.py:77
  5.1 3.8 %init.1 = (bf16[2048,1024]{1,0:T(8,128)(2,1)S(1)}, bf16[2048,1024]{1,0:T(8,128)(2,1)S(1)}, f32[4,1024]{1,0:T(4,128)S(1)}, f32[1,1024]{1,0:T(1,128)S(1)}, bf16[32...) custom-call(s32[2,8]{1,0:T(2,128)} %bitcast.9, ...), custom_call_target="tpu_custom_call" | custom-call | tf_op jit(solution)/shard_map/init/pallas_call | solution.py:611
  8.9 0.5 collective-permute-done.far
  9.5 0.6 %norm.1.normed = bf16[144,2048]{1,0:T(8,128)(2,1)S(1)} custom-call(bf16[128,1024]{1,0:T(8,128)(2,1)S(1)} %copy-done, bf16[128,1024]{1,0:T(8,128)(2,1)S(1)} %collective-permute-done.far, bf16[16,1024]{1,0:T(8,128)(2,1)S(1)} %collective-permute-done.1.own_rim, bf16[16,1024]{1,0:T(8,128)(2,1)S(1)} %collective-permute-done.2.far_rim, ...), custom_call_target="tpu_custom_call" | custom-call | tf_op jit(solution)/shard_map/norm/pallas_call | solution.py:654
  10.1 4.0 %collective-permute-start.3 = (bf16[144,2048]{1,0:T(8,128)(2,1)S(1)}, bf16[144,2048]{1,0:T(8,128)(2,1)S(1)}, u32[]{:S(2)}, u32[]{:S(2)}) collective-permute-start(bf16[144,2048]{1,0:T(8,128)(2,1)S(1)} %norm.1.normed), channel_id=1, source_target_pairs={{0,2},{2,0},{4,6},{6,4},{8,10},{10,8},{12,14},{14,12},{16,18},{18,... | collective-permute-start | bytes 1769480 | tf_op jit(solution)/shard_map/ppermute | solution.py:55
  14.1 1.7 %own_signal.1 = (bf16[288,2048]{1,0:T(8,128)(2,1)S(1)}, f32[288,1024]{1,0:T(8,128)S(1)}) custom-call(bf16[144,2048]{1,0:T(8,128)(2,1)S(1)} %norm.1.normed, bf16[2048,1024]{1,0:T(8,128)(2,1)S(1)} %get-tuple-element.47.w), custom_call_target="tpu_custom_call" | custom-call | tf_op jit(solution)/shard_map/own_signal/pallas_call | solution.py:660
  15.8 2.8 %signal.1 = (bf16[288,2048]{1,0:T(8,128)(2,1)S(1)}, f32[2,8,256,128]{3,2,1,0:T(8,128)S(1)}, f32[128,128]{1,0:T(8,128)S(1)}) custom-call(bf16[144,2048]{1,0:T(8,128)(2,1)S(1)} %collective-permute-done.3.normed, f32[288,1024]{1,0:T(8,128)S(1)} %get-tuple-element.48.x_own, bf16[2048,1024]{1,0:T(8,128)(2,1)S(1)} %get-tuple-element.47.w, ...), custom_call_target="tpu_custom_call" | custom-call | tf_op jit(solution)/shard_map/signal/pallas_call | solution.py:666
  18.6 0.3 collective-permute-start.4
  19.0 1.0 %collective-permute-done.4 = f32[128,128]{1,0:T(8,128)S(1)} collective-permute-done((f32[128,128]{1,0:T(8,128)S(1)}, f32[128,128]{1,0:T(8,128)S(1)}, u32[]{:S(2)}, u32[]{:S(2)}) %collective-permute-start.4) | collective-permute-done | bytes 65568 | tf_op jit(solution)/shard_map/ppermute | solution.py:55
  19.9 1.2 %collective-permute-start.5 = (f32[128,128]{1,0:T(8,128)S(1)}, f32[128,128]{1,0:T(8,128)S(1)}, u32[]{:S(2)}, u32[]{:S(2)}) collective-permute-start(f32[128,128]{1,0:T(8,128)S(1)} %add.12.bc_own), channel_id=1, source_target_pairs={{0,1},{1,0},{2,3},{3,2},{4,5},{5,4},{6,7},{7,6},{8,9},{9,8},{10,11... | collective-permute-start | bytes 196616 | tf_op jit(solution)/shard_map/ppermute | solution.py:55
  21.1 2.7 %gate.1.after_z.z = bf16[2,256,1024]{2,1,0:T(8,128)(2,1)S(1)} custom-call(bf16[288,2048]{1,0:T(8,128)(2,1)S(1)} %get-tuple-element.56.lined_own, bf16[288,2048]{1,0:T(8,128)(2,1)S(1)} %get-tuple-element.57.lined_other, bf16[2048,1024]{1,0:T(8,128)(2,1)S(1)} %get-tuple-element.58.w), custom_call_target="tpu_custom_call" | custom-call | tf_op jit(solution)/shard_map/gate/pallas_call | solution.py:684
  23.8 0.5 collective-permute-done.5.bc_far
  24.3 5.0 %ends.1 = (f32[128,128]{1,0:T(8,128)S(1)}, f32[2,16,1024]{2,1,0:T(8,128)S(1)}, f32[2,16,16,1024]{3,2,1,0:T(8,128)S(1)}, bf16[1024,2048]{1,0:T(8,128)(2,1)S(1)}) custom-call(f32[128,128]{1,0:T(8,128)S(1)} %add.12.bc_own, f32[128,128]{1,0:T(8,128)S(1)} %collective-permute-done.5.bc_far, f32[128,128]{1,0:T(8,128)S(1)} %get-tuple-element.53.weigh, ...), custom_call_target="tpu_custom_call" | custom-call | tf_op jit(solution)/shard_map/ends/pallas_call | solution.py:687
  29.4 2.5 %collective-permute-start.6 = (bf16[2,16,1024]{2,1,0:T(8,128)(2,1)S(1)}, bf16[2,16,1024]{2,1,0:T(8,128)(2,1)S(1)}, u32[]{:S(2)}, u32[]{:S(2)}) collective-permute-start(bf16[2,16,1024]{2,1,0:T(8,128)(2,1)S(1)} %convert_element_type.18), channel_id=1, source_target_pairs={{0,4},{2,6},{4,0},{6,2},{8,12},{10,14},{12,8},{14,10},{16,20},{18,... | collective-permute-start | bytes 196616 | tf_op jit(solution)/shard_map/ppermute | solution.py:55
  31.9 0.2 factors.1
  32.1 2.0 %local.2 = (f32[8,256,128]{2,1,0:T(8,128)S(1)}, bf16[256,256]{1,0:T(8,128)(2,1)S(1)}) custom-call(f32[128,128]{1,0:T(8,128)S(1)} %get-tuple-element.59.after_ends.bc, f32[2,8,256,128]{3,2,1,0:T(8,128)S(1)} %get-tuple-element.54.c, f32[16,1024]{1,0:T(8,128)S(1)} %get-tuple-element.55.decay, f32[16,1024]{1,0:T(8,128)S(1)} %negate_sqrt_fusion.drive, ...), custom_call_target="tpu_custom_call" | custom-call | tf_op jit(solution)/shard_map/local/pallas_call | solution.py:716
  34.0 0.1 collective-permute-done.6.got
  34.2 2.1 %collective-permute-start.7 = (bf16[16,1024]{1,0:T(8,128)(2,1)S(1)}, bf16[16,1024]{1,0:T(8,128)(2,1)S(1)}, u32[]{:S(2)}, u32[]{:S(2)}) collective-permute-start(bf16[16,1024]{1,0:T(8,128)(2,1)S(1)} %get-tuple-element.73), channel_id=1, source_target_pairs={{0,8},{2,10},{4,12},{6,14},{8,0},{10,2},{12,4},{14,6},{16,24},{18,... | collective-permute-start | bytes 98312 | tf_op jit(solution)/shard_map/ppermute | solution.py:55
  36.2 2.6 %collective-permute-start.8 = (bf16[16,1024]{1,0:T(8,128)(2,1)S(1)}, bf16[16,1024]{1,0:T(8,128)(2,1)S(1)}, u32[]{:S(2)}, u32[]{:S(2)}) collective-permute-start(bf16[16,1024]{1,0:T(8,128)(2,1)S(1)} %get-tuple-element.74), channel_id=1, source_target_pairs={{0,16},{2,18},{4,20},{6,22},{8,24},{10,26},{12,28},{14,30},{16,0},... | collective-permute-start | bytes 98312 | tf_op jit(solution)/shard_map/ppermute | solution.py:55
  38.8 2.0 %local.3 = (f32[8,256,128]{2,1,0:T(8,128)S(1)}, bf16[256,256]{1,0:T(8,128)(2,1)S(1)}) custom-call(f32[128,128]{1,0:T(8,128)S(1)} %get-tuple-element.59.after_ends.bc, f32[2,8,256,128]{3,2,1,0:T(8,128)S(1)} %get-tuple-element.54.c, f32[16,1024]{1,0:T(8,128)S(1)} %get-tuple-element.55.decay, f32[16,1024]{1,0:T(8,128)S(1)} %negate_sqrt_fusion.drive, ...), custom_call_target="tpu_custom_call" | custom-call | tf_op jit(solution)/shard_map/local/pallas_call | solution.py:716
  40.9 0.4 collective-permute-done.8.rest_1_
  41.3 3.2 %collective-permute-done.9.rest_2_ = bf16[16,1024]{1,0:T(8,128)(2,1)S(1)} collective-permute-done((bf16[16,1024]{1,0:T(8,128)(2,1)S(1)}, bf16[16,1024]{1,0:T(8,128)(2,1)S(1)}, u32[]{:S(2)}, u32[]{:S(2)}) %collective-permute-start.9) | collective-permute-done | bytes 32800 | tf_op jit(solution)/shard_map/ppermute | solution.py:55
  44.5 2.7 %finish.3 = (bf16[128,1024]{1,0:T(8,128)(2,1)S(1)}, bf16[128,1024]{1,0:T(8,128)(2,1)S(1)}) custom-call(bf16[256,1024]{1,0:T(8,128)(2,1)S(1)} %get-tuple-element.60.powers, f32[2,16,1024]{2,1,0:T(8,128)S(1)} %get-tuple-element.61.strides, bf16[2,16,1024]{2,1,0:T(8,128)(2,1)S(1)} %collective-permute-done.6.got, ...), custom_call_target="tpu_custom_call" | custom-call | tf_op jit(solution)/shard_map/finish/pallas_call | solution.py:746
  47.3 0.5 collective-permute-start.11
  47.8 2.1 %finish.2 = (f32[128,1024]{1,0:T(8,128)S(1)}, bf16[2,128,1024]{2,1,0:T(8,128)(2,1)S(1)}) custom-call(bf16[256,1024]{1,0:T(8,128)(2,1)S(1)} %get-tuple-element.60.powers, f32[2,16,1024]{2,1,0:T(8,128)S(1)} %get-tuple-element.61.strides, bf16[2,16,1024]{2,1,0:T(8,128)(2,1)S(1)} %collective-permute-done.6.got, f32[3,2,16,1024]{3,2,1,0:T(8,128)S(1)} %get-tuple-element.63.leads, ...), custom_call_target="tpu_custom_call" | custom-call | tf_op jit(solution)/shard_map/finish/pallas_call | solution.py:754
  50.0 1.6 %collective-permute-start.12 = (bf16[128,1024]{1,0:T(8,128)(2,1)S(1)}, bf16[128,1024]{1,0:T(8,128)(2,1)S(1)}, u32[]{:S(2)}, u32[]{:S(2)}) collective-permute-start(bf16[128,1024]{1,0:T(8,128)(2,1)S(1)} %add_convert_fusion.1.after_first), channel_id=1, source_target_pairs={{0,1},{1,0},{2,3},{3,2},{4,5},{5,4},{6,7},{7,6},{8,9},{9,8},{10,11... | collective-permute-start | bytes 786440 | tf_op jit(solution)/shard_map/ppermute | solution.py:55
  51.6 0.9 %rest.1 = f32[128,1024]{1,0:T(8,128)S(1)} custom-call(bf16[2,128,1024]{2,1,0:T(8,128)(2,1)S(1)} %get-tuple-element.75.gated, bf16[1024,2048]{1,0:T(8,128)(2,1)S(1)} %get-tuple-element.72.w, bf16[128,1024]{1,0:T(8,128)(2,1)S(1)} %add_convert_fusion.1.after_first), custom_call_target="tpu_custom_call" | custom-call | tf_op jit(solution)/shard_map/rest/pallas_call | solution.py:764
  52.5 5.8 %collective-permute-done.12 = bf16[128,1024]{1,0:T(8,128)(2,1)S(1)} collective-permute-done((bf16[128,1024]{1,0:T(8,128)(2,1)S(1)}, bf16[128,1024]{1,0:T(8,128)(2,1)S(1)}, u32[]{:S(2)}, u32[]{:S(2)}) %collective-permute-start.12) | collective-permute-done | bytes 262176 | tf_op jit(solution)/shard_map/ppermute | solution.py:55
  58.3 0.8 %add_convert_fusion = bf16[128,1024]{1,0:T(8,128)(2,1)} fusion(bf16[128,1024]{1,0:T(8,128)(2,1)S(1)} %collective-permute-done.12, f32[128,1024]{1,0:T(8,128)S(1)} %rest.1, bf16[128,1024]{1,0:T(8,128)(2,1)S(1)} %collective-permute-done.11), kind=kLoop, calls=%fused_computation | loop fusion | flops 655360 | bytes 1310720 | tf_op jit(solution)/shard_map/convert_element_type | solution.py:769
  (15 shorter events, 0.3 us)
Async XLA Ops:
  0.0 9.5 %collective-permute-start = (bf16[128,1024]{1,0:T(8,128)(2,1)}, bf16[128,1024]{1,0:T(8,128)(2,1)S(1)}, u32[]{:S(2)}, u32[]{:S(2)}) collective-permute-start(bf16[128,1024]{1,0:T(8,128)(2,1)} %own.1), channel_id=1, source_target_pairs={{0,1},{1,0},{2,3},{3,2},{4,5},{5,4},{6,7},{7,6},{8,9},{9,8},{10,11... | collective-permute-start | bytes 786440 | tf_op jit(solution)/shard_map/ppermute | solution.py:55
  3.8 5.1 %collective-permute-start.1 = (bf16[16,1024]{1,0:T(8,128)(2,1)S(1)}, bf16[16,1024]{1,0:T(8,128)(2,1)S(1)}, u32[]{:S(2)}, u32[]{:S(2)}) collective-permute-start(bf16[16,1024]{1,0:T(8,128)(2,1)S(1)} %rim.1.after), channel_id=1, source_target_pairs={{2,4},{3,5},{6,8},{7,9},{10,12},{11,13},{14,16},{15,17},{18,20},{1... | collective-permute-start | bytes 98312 | tf_op jit(solution)/shard_map/ppermute | solution.py:77
  4.4 4.5 %collective-permute-start.2 = (bf16[16,1024]{1,0:T(8,128)(2,1)S(1)}, bf16[16,1024]{1,0:T(8,128)(2,1)S(1)}, u32[]{:S(2)}, u32[]{:S(2)}) collective-permute-start(bf16[16,1024]{1,0:T(8,128)(2,1)S(1)} %rim.1.after), channel_id=1, source_target_pairs={{3,4},{2,5},{7,8},{6,9},{11,12},{10,13},{15,16},{14,17},{19,20},{1... | collective-permute-start | bytes 98312 | tf_op jit(solution)/shard_map/ppermute | solution.py:77
  5.1 4.4 %copy-start = (bf16[128,1024]{1,0:T(8,128)(2,1)S(1)}, bf16[128,1024]{1,0:T(8,128)(2,1)}, u32[]{:S(2)}) copy-start(bf16[128,1024]{1,0:T(8,128)(2,1)} %own.1) | copy-start | bytes 786436
  10.1 5.7 %collective-permute-start.3 = (bf16[144,2048]{1,0:T(8,128)(2,1)S(1)}, bf16[144,2048]{1,0:T(8,128)(2,1)S(1)}, u32[]{:S(2)}, u32[]{:S(2)}) collective-permute-start(bf16[144,2048]{1,0:T(8,128)(2,1)S(1)} %norm.1.normed), channel_id=1, source_target_pairs={{0,2},{2,0},{4,6},{6,4},{8,10},{10,8},{12,14},{14,12},{16,18},{18,... | collective-permute-start | bytes 1769480 | tf_op jit(solution)/shard_map/ppermute | solution.py:55
  18.6 1.3 %collective-permute-start.4 = (f32[128,128]{1,0:T(8,128)S(1)}, f32[128,128]{1,0:T(8,128)S(1)}, u32[]{:S(2)}, u32[]{:S(2)}) collective-permute-start(f32[128,128]{1,0:T(8,128)S(1)} %get-tuple-element.52), channel_id=1, source_target_pairs={{0,2},{2,0},{4,6},{6,4},{8,10},{10,8},{12,14},{14,12},{16,18},{18,... | collective-permute-start | bytes 196616 | tf_op jit(solution)/shard_map/ppermute | solution.py:55
  19.9 4.4 %collective-permute-start.5 = (f32[128,128]{1,0:T(8,128)S(1)}, f32[128,128]{1,0:T(8,128)S(1)}, u32[]{:S(2)}, u32[]{:S(2)}) collective-permute-start(f32[128,128]{1,0:T(8,128)S(1)} %add.12.bc_own), channel_id=1, source_target_pairs={{0,1},{1,0},{2,3},{3,2},{4,5},{5,4},{6,7},{7,6},{8,9},{9,8},{10,11... | collective-permute-start | bytes 196616 | tf_op jit(solution)/shard_map/ppermute | solution.py:55
  29.4 4.8 %collective-permute-start.6 = (bf16[2,16,1024]{2,1,0:T(8,128)(2,1)S(1)}, bf16[2,16,1024]{2,1,0:T(8,128)(2,1)S(1)}, u32[]{:S(2)}, u32[]{:S(2)}) collective-permute-start(bf16[2,16,1024]{2,1,0:T(8,128)(2,1)S(1)} %convert_element_type.18), channel_id=1, source_target_pairs={{0,4},{2,6},{4,0},{6,2},{8,12},{10,14},{12,8},{14,10},{16,20},{18,... | collective-permute-start | bytes 196616 | tf_op jit(solution)/shard_map/ppermute | solution.py:55
  34.2 6.7 %collective-permute-start.7 = (bf16[16,1024]{1,0:T(8,128)(2,1)S(1)}, bf16[16,1024]{1,0:T(8,128)(2,1)S(1)}, u32[]{:S(2)}, u32[]{:S(2)}) collective-permute-start(bf16[16,1024]{1,0:T(8,128)(2,1)S(1)} %get-tuple-element.73), channel_id=1, source_target_pairs={{0,8},{2,10},{4,12},{6,14},{8,0},{10,2},{12,4},{14,6},{16,24},{18,... | collective-permute-start | bytes 98312 | tf_op jit(solution)/shard_map/ppermute | solution.py:55
  36.2 5.1 %collective-permute-start.8 = (bf16[16,1024]{1,0:T(8,128)(2,1)S(1)}, bf16[16,1024]{1,0:T(8,128)(2,1)S(1)}, u32[]{:S(2)}, u32[]{:S(2)}) collective-permute-start(bf16[16,1024]{1,0:T(8,128)(2,1)S(1)} %get-tuple-element.74), channel_id=1, source_target_pairs={{0,16},{2,18},{4,20},{6,22},{8,24},{10,26},{12,28},{14,30},{16,0},... | collective-permute-start | bytes 98312 | tf_op jit(solution)/shard_map/ppermute | solution.py:55
  38.8 5.7 %collective-permute-start.9 = (bf16[16,1024]{1,0:T(8,128)(2,1)S(1)}, bf16[16,1024]{1,0:T(8,128)(2,1)S(1)}, u32[]{:S(2)}, u32[]{:S(2)}) collective-permute-start(bf16[16,1024]{1,0:T(8,128)(2,1)S(1)} %get-tuple-element.68.after), channel_id=1, source_target_pairs={{0,24},{2,26},{4,28},{6,30},{8,16},{10,18},{12,20},{14,22},{16,8},... | collective-permute-start | bytes 98312 | tf_op jit(solution)/shard_map/ppermute | solution.py:55
  47.3 2.6 %collective-permute-start.10 = (bf16[128,1024]{1,0:T(8,128)(2,1)S(1)}, bf16[128,1024]{1,0:T(8,128)(2,1)S(1)}, u32[]{:S(2)}, u32[]{:S(2)}) collective-permute-start(bf16[128,1024]{1,0:T(8,128)(2,1)S(1)} %get-tuple-element.77), channel_id=1, source_target_pairs={{0,2},{2,0},{4,6},{6,4},{8,10},{10,8},{12,14},{14,12},{16,18},{18,... | collective-permute-start | bytes 786440 | tf_op jit(solution)/shard_map/ppermute | solution.py:55
  47.3 5.1 %collective-permute-start.11 = (bf16[128,1024]{1,0:T(8,128)(2,1)S(1)}, bf16[128,1024]{1,0:T(8,128)(2,1)S(1)}, u32[]{:S(2)}, u32[]{:S(2)}) collective-permute-start(bf16[128,1024]{1,0:T(8,128)(2,1)S(1)} %get-tuple-element.78), channel_id=1, source_target_pairs={{0,2},{2,0},{4,6},{6,4},{8,10},{10,8},{12,14},{14,12},{16,18},{18,... | collective-permute-start | bytes 786440 | tf_op jit(solution)/shard_map/ppermute | solution.py:55
  50.0 8.4 %collective-permute-start.12 = (bf16[128,1024]{1,0:T(8,128)(2,1)S(1)}, bf16[128,1024]{1,0:T(8,128)(2,1)S(1)}, u32[]{:S(2)}, u32[]{:S(2)}) collective-permute-start(bf16[128,1024]{1,0:T(8,128)(2,1)S(1)} %add_convert_fusion.1.after_first), channel_id=1, source_target_pairs={{0,1},{1,0},{2,3},{3,2},{4,5},{5,4},{6,7},{7,6},{8,9},{9,8},{10,11... | collective-permute-start | bytes 786440 | tf_op jit(solution)/shard_map/ppermute | solution.py:55
